TPU v7x, 512 devices: a whole 4x4x16 slice. The times are simulated.
512 devices in a mesh: rep: 32 (over z_hi, x, core), exp: 16 (over z_lo, y).
Axes of the slice: x: 4, y: 4, z: 16 (z_hi: 4, z_lo: 4; z = z_hi * 4 + z_lo), core: 2. Of those that a mesh axis runs over, the one named last changes fastest.
Arguments:
- query: bfloat16 [512, 8192], P('rep', 'exp'), may hold values from -150 to 150
- new_key: bfloat16 [512, 2048], P('rep', 'exp'), may hold values from -5 to 5
- new_value: bfloat16 [512, 2048], P('rep', 'exp'), may hold values from -6 to 6
- page_pool: bfloat16 [1536, 16, 2, 16, 128], P('rep', 'exp'), may hold values from -6 to 6
- block_table: int32 [512, 8], P('rep'), may hold values from 0 to 47, as said below
- lengths: int32 [512], replicated, may hold values from 1 to 128
- anchor: int32 [512], replicated, may hold values from 0 to 511, as said below
- conv_input: bfloat16 [512, 8192], P('rep', 'exp'), may hold values from -6 to 6
- gate_input: bfloat16 [512, 8192], P('rep', 'exp'), may hold values from -6 to 6
- window_state: bfloat16 [512, 3, 8192], P('rep', None, 'exp'), may hold values from -6 to 6
- scan_state: float32 [512, 16, 8192], P('rep', None, 'exp'), may hold values from -6 to 6
- filter_taps: float32 [4, 8192], P(None, 'exp'), may hold values from -3 to 3
- filter_bias: float32 [8192], P('exp'), may hold values from -3 to 3
- mix_weight: bfloat16 [8192, 288], P('exp'), may hold values from -0.0625 to 0.0625
- step_weight: bfloat16 [256, 8192], P(None, 'exp'), may hold values from -0.375 to 0.375
- step_bias: float32 [8192], P('exp'), may hold values from -1 to 1
- log_decay: float32 [16, 8192], P(None, 'exp'), may hold values from -2 to 1.5
- skip_gain: float32 [8192], P('exp'), may hold values from 0.5 to 1.5
- routes: int32 [512, 2], P('rep'), may hold values from 0 to 15, all different within a row; in each aligned block of 16 rows (0 to 15, 16 to 31, ...) at most 4 rows name the same one
- route_weight: float32 [512, 2], P('rep'), may hold values from 0.2 to 1
- expert_hidden: bfloat16 [16, 128, 12288], P('exp', None, 'rep'), may hold values from -6 to 6
- down_weight: bfloat16 [16, 12288, 4096], P('exp', 'rep'), may hold values from -0.0546875 to 0.0546875
Outputs:
- attention_out: bfloat16 [512, 8192], P('rep', 'exp')
- moved_pages: bfloat16 [64, 16, 2, 128, 128], P('rep', 'exp')
- mamba_out: bfloat16 [512, 8192], P('rep', 'exp')
- expert_mix: bfloat16 [512, 4096], P('rep', 'exp')
Inputs may be any that keep to these rules, and one draw needn't show every extreme that they name: anchor is a permutation. Exactly 2 new slots of each replica take requests from other replicas, each from a different replica, and exactly 2 requests of each replica leave it, each to a different replica. `block_table`: each replica has at least one request of length 128. The first ceil(lengths / 16) entries of a row are distinct pages of its replica's pool, used by no other request of that replica; later entries are arbitrary. `routes`: in the 16 rows of one replica no expert is named more than 4 times.
All inputs are finite; a program needn't handle non-finite values.
Results may differ from a plain program's by a relative error of at most 0.0065.
Values may be sent and summed in bfloat16 or wider, within the bound.
No kernel may reach another device: no remote copies, remote signals or barrier semaphores. Data moves between devices by JAX's collectives and lax.ppermute only.
A program may use at most 64 MiB of HBM per device.

v0:
```python
import math

import jax
import jax.numpy as jnp
from jax import lax
from jax.sharding import PartitionSpec as P

MIG = 2


def per_device(
    query,
    new_key,
    new_value,
    page_pool,
    block_table,
    lengths,
    anchor,
    conv_input,
    gate_input,
    window_state,
    scan_state,
    filter_taps,
    filter_bias,
    mix_weight,
    step_weight,
    step_bias,
    log_decay,
    skip_gain,
    routes,
    route_weight,
    expert_hidden,
    down_weight,
):
    requests = query.shape[0]
    replicas = lax.axis_size("rep")
    replica = lax.axis_index("rep")
    all_slots = anchor.shape[0]
    everyone = jnp.arange(all_slots, dtype=jnp.int32)
    target = jnp.zeros((all_slots,), jnp.int32).at[anchor].set(everyone)
    leaves = target // requests != everyone // requests
    leave_grid = leaves.reshape(replicas, requests).astype(jnp.int32)
    leave_rank = (jnp.cumsum(leave_grid, axis=1) - leave_grid).reshape(all_slots)
    outgoing = jnp.nonzero(
        lax.dynamic_slice_in_dim(leaves, replica * requests, requests), size=MIG
    )[0].astype(jnp.int32)
    anchors = lax.dynamic_slice_in_dim(anchor, replica * requests, requests)
    source_rep = anchors // requests
    arrived = source_rep != replica
    pages_out = page_pool[block_table[outgoing]]
    window_out = window_state[outgoing]
    scan_out = scan_state[outgoing]
    incoming_pages, incoming_window = (
        lax.all_gather(pages_out, "rep", axis=0, tiled=True),
        lax.all_gather(window_out, "rep", axis=0, tiled=True),
    )
    incoming_scan = lax.all_gather(scan_out, "rep", axis=0, tiled=True)
    chosen = source_rep * MIG + leave_rank[anchors]
    chosen = jnp.where(arrived, chosen, 0)
    local_index = jnp.clip(anchors - replica * requests, 0, requests - 1)
    blocks = jnp.where(
        arrived[:, None, None, None, None, None],
        incoming_pages[chosen],
        page_pool[block_table[local_index]],
    )
    window_old = jnp.where(
        arrived[:, None, None], incoming_window[chosen], window_state[local_index]
    )
    scan_old = jnp.where(arrived[:, None, None], incoming_scan[chosen], scan_state[local_index])
    head_size = new_key.shape[1]
    head_count = query.shape[1] // head_size
    scale = 1.0 / math.sqrt(head_size)
    cached_keys = blocks[:, :, 0, 0].reshape(requests, -1, head_size)
    cached_values = blocks[:, :, 0, 1].reshape(requests, -1, head_size)
    span = cached_keys.shape[1]
    queries = query.reshape(requests, head_count, head_size)
    scores = (
        jnp.einsum("rhd,rtd->rht", queries, cached_keys, preferred_element_type=jnp.float32) * scale
    )
    own_score = (
        jnp.einsum("rhd,rd->rh", queries, new_key, preferred_element_type=jnp.float32) * scale
    )
    live_len = lengths[anchors]
    visible = jnp.arange(span, dtype=jnp.int32)[None, None, :] < live_len[:, None, None]
    scores = jnp.where(visible, scores, -jnp.inf)
    highest = jnp.maximum(jnp.max(scores, axis=-1), own_score)
    expweights = jnp.exp(scores - highest[..., None])
    own_exp = jnp.exp(own_score - highest)
    denominator = jnp.sum(expweights, axis=-1) + own_exp
    weights = (expweights / denominator[..., None]).astype(jnp.bfloat16)
    own_weight = (own_exp / denominator).astype(jnp.bfloat16)
    context = jnp.einsum("rht,rtd->rhd", weights, cached_values, preferred_element_type=jnp.float32)
    context = context + own_weight[..., None].astype(jnp.float32) * new_value[:, None, :].astype(
        jnp.float32
    )
    attended = context.reshape(requests, head_count * head_size).astype(jnp.bfloat16)
    arrivals = jnp.nonzero(arrived, size=MIG)[0].astype(jnp.int32)
    arrival_blocks = jnp.transpose(blocks[arrivals], (0, 2, 3, 1, 4, 5)).reshape(
        MIG, 1, 2, span, head_size
    )
    keep = (
        jnp.arange(span, dtype=jnp.int32)[None, None, None, :, None]
        < live_len[arrivals][:, None, None, None, None]
    )
    moved = jnp.where(keep, arrival_blocks, jnp.zeros((), arrival_blocks.dtype))
    window = jnp.concatenate(
        [window_old.astype(jnp.float32), conv_input[:, None, :].astype(jnp.float32)], axis=1
    )
    mixed = jnp.sum(window * filter_taps[None], axis=1) + filter_bias
    activated = jax.nn.silu(mixed)
    partial_sum = jnp.dot(
        activated.astype(jnp.bfloat16), mix_weight, preferred_element_type=jnp.float32
    )
    projected = lax.psum(partial_sum, "exp")
    rank_width = step_weight.shape[0]
    state_width = log_decay.shape[0]
    step_size = jax.nn.softplus(
        jnp.dot(
            projected[:, :rank_width].astype(jnp.bfloat16),
            step_weight,
            preferred_element_type=jnp.float32,
        )
        + step_bias
    )
    inflow = projected[:, rank_width : rank_width + state_width]
    readout = projected[:, rank_width + state_width :]
    decay = jnp.exp(step_size[:, None, :] * (-jnp.exp(log_decay))[None])
    state = decay * scan_old + step_size[:, None, :] * inflow[:, :, None] * activated[:, None, :]
    output = jnp.sum(readout[:, :, None] * state, axis=1) + skip_gain * activated
    gated = (output * jax.nn.silu(gate_input.astype(jnp.float32))).astype(jnp.bfloat16)
    capacity = expert_hidden.shape[1] // replicas
    hidden = expert_hidden[0]
    weight = down_weight[0]
    full_terms = jnp.dot(hidden, weight, preferred_element_type=jnp.float32)
    totals = lax.psum(full_terms, "rep")
    slot_sums = lax.dynamic_slice_in_dim(totals, replica * capacity, capacity, 0).astype(
        jnp.bfloat16
    )
    spread = lax.all_to_all(slot_sums, "exp", split_axis=1, concat_axis=0, tiled=True)
    expert_count = lax.axis_size("exp")
    flat_routes = routes.reshape(-1)
    matches = (flat_routes[:, None] == jnp.arange(expert_count, dtype=jnp.int32)[None, :]).astype(
        jnp.int32
    )
    earlier = jnp.cumsum(matches, axis=0) - matches
    position = jnp.sum(earlier * matches, axis=1)
    gathered = (
        spread[flat_routes * capacity + position]
        .astype(jnp.float32)
        .reshape(requests, routes.shape[1], -1)
    )
    combined = jnp.sum(gathered * route_weight[:, :, None], axis=1).astype(jnp.bfloat16)
    return (attended, moved, gated, combined)


def solution(mesh):
    placed = (
        P("rep", "exp"),
        P("rep", "exp"),
        P("rep", "exp"),
        P("rep", "exp", None, None, None),
        P("rep", None),
        P(),
        P(),
        P("rep", "exp"),
        P("rep", "exp"),
        P("rep", None, "exp"),
        P("rep", None, "exp"),
        P(None, "exp"),
        P("exp"),
        P("exp", None),
        P(None, "exp"),
        P("exp"),
        P(None, "exp"),
        P("exp"),
        P("rep", None),
        P("rep", None),
        P("exp", None, "rep"),
        P("exp", "rep", None),
    )
    return jax.shard_map(
        per_device,
        mesh=mesh,
        in_specs=placed,
        out_specs=(
            P("rep", "exp"),
            P("rep", "exp", None, None, None),
            P("rep", "exp"),
            P("rep", "exp"),
        ),
        check_vma=False,
    )
```

profile of v0, /device:TPU:2, one launch (start us, length us, event | category | flops | bytes accessed | tf_op | source)
XLA Modules:
  0.0 510.7 jit_solution(17887741041562579106)
XLA Ops:
  7.2 0.8 compare_select_fusion.4
  8.1 2.4 scatter_custom_fusion
  11.6 0.7 fusion.41
  14.1 2.2 gather_fusion.12
  16.4 0.8 copy.65
  17.8 2.2 gather_fusion.2
  20.1 3.0 fusion
  23.0 254.9 %all-reduce.1 = bf16[128,4096]{1,0:T(8,128)(2,1)} all-reduce(f32[128,4096]{1,0:T(8,128)} %fusion), channel_id=1, replica_groups=mesh['rep'=32,'exp'=16] {'rep'}, use_global_device_ids=true, to_apply=%region_15.16 | all-reduce | flops 524288 | bytes 3145728 | tf_op jit(solution)/shard_map/psum | solution.py:135
  278.0 1.5 dynamic-slice_convert_fusion
  279.4 4.1 all-to-all-start
  283.6 1.2 gather_fusion.9
  284.8 2.0 compare_select_fusion.20
  287.4 1.3 gather_fusion.11
  288.7 1.4 gather_fusion.5
  290.8 1.5 reduce_window_sum.42
  292.3 1.4 reduce_window_sum.43
  293.7 0.7 copy.71
  294.4 1.4 copy.73
  295.7 0.8 copy.67
  297.1 1.4 copy.68
  298.4 1.3 reshape.433
  299.7 1.3 pad_clamp_fusion.7
  301.0 0.7 convert_subtract_fusion
  301.7 1.4 gather_fusion.3
  303.0 0.8 gather_fusion
  303.8 1.3 reshape.371
  306.4 1.3 reduce-window.13
  307.8 0.8 fusion.18
  308.6 1.3 scatter_custom_fusion.2
  309.9 1.4 select_n.237
  311.3 1.4 copy.76
  312.6 0.8 eq.18
  314.1 1.4 reduce_window_sum.44
  315.4 1.2 broadcast_multiply_fusion
  316.7 1.4 copy.75
  318.0 1.3 mul.166
  319.3 58.3 %all-gather.1 = bf16[64,3,512]{2,1,0:T(4,128)(2,1)} all-gather(bf16[2,3,512]{2,1,0:T(4,128)(2,1)S(1)} %copy.71), channel_id=3, replica_groups=mesh['rep'=32,'exp'=16] {'rep'}, dimensions={0}, use_global_device_ids=true | all-gather | bytes 202752 | tf_op jit(solution)/shard_map/all_gather | solution.py:55
  378.3 2.2 gather_fusion.10
  380.5 1.3 fusion.34
  382.4 1.0 copy_select_fusion
  383.4 0.9 multiply_reduce_fusion.1
  384.9 0.7 divide_multiply_fusion
  386.2 1.8 fusion.13
  388.0 80.0 %psum.14 = f32[16,288]{1,0:T(8,128)} all-reduce(f32[16,288]{1,0:T(8,128)} %fusion.13), channel_id=1, replica_groups=mesh['rep'=32,'exp'=16] {'exp'}, use_global_device_ids=true, to_apply=%region_13.14 | all-reduce | flops 4608 | bytes 36864 | tf_op jit(solution)/shard_map/psum | solution.py:114
  468.0 0.9 select_reduce_fusion
  469.6 1.2 fusion.35
  471.4 1.4 fusion.45
  472.8 1.5 fusion.19
  474.2 1.4 exponential_negate_fusion
  475.6 1.7 compare_select_fusion
  477.9 2.5 gather_fusion.14
  480.4 1.7 gather_fusion.6
  482.1 0.7 convert_element_type.76
  482.8 0.8 copy.77
  484.2 0.8 all_to_all.17
  485.7 0.7 multiply_reduce_fusion.2
  486.4 3.1 gather_fusion.13
  489.5 1.5 multiply_reduce_fusion
  491.0 1.4 fusion.10
  492.5 4.0 gather_fusion.4
  496.5 1.7 bitcast_select_fusion
  498.2 1.0 copy-done.3
  501.1 1.9 gather_fusion.8
  503.1 0.8 bitcast_select_fusion.1
  (83 shorter events, 15.1 us)
Async XLA Ops:
  7.2 12.9 %copy-start = (bf16[1,384,4096]{2,1,0:T(8,128)(2,1)S(1)}, bf16[1,384,4096]{2,1,0:T(8,128)(2,1)}, u32[]{:S(2)}) copy-start(bf16[1,384,4096]{2,1,0:T(8,128)(2,1)} %param.43) | copy-start | bytes 9437188
  7.2 479.2 %all-gather.8.cloned.1.call-start = ((), (), s32[]{:S(2)}) async-start(), calls=%async_computation.2 | async-start | bytes 2162688 | tf_op jit(solution)/shard_map/all_gather | solution.py:57
  11.1 0.5 copy-start.16
  12.6 5.1 %copy-start.18 = (s32[16]{0:T(128)}, s32[16]{0:T(128)S(1)}, u32[]{:S(2)}) copy-start(s32[16]{0:T(128)S(1)} %ne.101) | copy-start | bytes 196
  16.3 476.2 %all-gather.6.cloned.1.call-start = ((), (), s32[]{:S(2)}) async-start(), calls=%async_computation.1 | async-start | bytes 4325376 | tf_op jit(solution)/shard_map/all_gather | solution.py:54
  20.0 263.5 %copy-start.2 = (bf16[16,3,512]{2,0,1:T(8,128)(2,1)S(1)}, bf16[16,3,512]{2,0,1:T(8,128)(2,1)}, u32[]{:S(2)}) copy-start(bf16[16,3,512]{2,0,1:T(8,128)(2,1)} %param.31) | copy-start | bytes 147460
  23.0 267.1 %copy-start.11 = (s32[512]{0:T(512)S(1)}, s32[512]{0:T(512)}, u32[]{:S(2)}) copy-start(s32[512]{0:T(512)} %get-tuple-element.15) | copy-start | bytes 6148
  23.0 280.0 %copy-start.1 = (s32[512]{0:T(512)S(1)}, s32[512]{0:T(512)}, u32[]{:S(2)}) copy-start(s32[512]{0:T(512)} %param.27) | copy-start | bytes 6148
  279.4 204.8 %all-to-all-start = ((bf16[4,16,256]{2,0,1:T(4,128)(2,1)}), bf16[4,16,256]{2,0,1:T(4,128)(2,1)}, u32[]{:S(2)}, u32[]{:S(2)}) async-start(bf16[4,16,256]{2,0,1:T(4,128)(2,1)} %bitcast.26), calls=%async_computation | async-start | bytes 65536 | tf_op jit(solution)/shard_map/all_to_all | solution.py:139
  286.8 0.6 copy-start.13
  288.7 191.8 %copy-start.4 = (bf16[48,1,2,16,128]{4,3,2,1,0:T(8,128)(2,1)S(1)}, bf16[48,1,2,16,128]{4,3,2,1,0:T(8,128)(2,1)}, u32[]{:S(2)}) copy-start(bf16[48,1,2,16,128]{4,3,2,1,0:T(8,128)(2,1)} %param.25) | copy-start | bytes 1179652
  313.4 64.2 %copy-start.15 = (s32[32]{0:T(128)}, s32[32]{0:T(128)S(1)}, u32[]{:S(2)}) copy-start(s32[32]{0:T(128)S(1)} %eq.18) | copy-start | bytes 388
  378.3 106.0 %copy-start.12 = (s32[1024]{0:T(1024)}, s32[1024]{0:T(1024)S(1)}, u32[]{:S(2)}) copy-start(s32[1024]{0:T(1024)S(1)} %pad_clamp_fusion.4) | copy-start | bytes 12292
  381.8 89.0 %copy-start.14 = (s32[1024]{0:T(1024)}, s32[1024]{0:T(1024)S(1)}, u32[]{:S(2)}) copy-start(s32[1024]{0:T(1024)S(1)} %pad_clamp_fusion.1) | copy-start | bytes 12292
  384.3 0.6 copy-start.5
  385.6 0.6 copy-start.6
  482.1 14.3 %copy-start.9 = (pred[16]{0:T(512)(128)(4,1)S(1)}, pred[16]{0:T(512)(128)(4,1)}, u32[]{:S(2)}) copy-start(pred[16]{0:T(512)(128)(4,1)} %get-tuple-element.26) | copy-start | bytes 52
  496.4 3.0 copy-start.7
  496.4 3.0 copy-start.10
  496.5 3.5 copy-start.8
  496.5 6.6 %copy-start.17 = (pred[2,128]{1,0:T(4,128)(4,1)S(1)}, pred[2,128]{1,0:T(4,128)(4,1)}, u32[]{:S(2)}) copy-start(pred[2,128]{1,0:T(4,128)(4,1)} %iota_compare_fusion.2) | copy-start | bytes 772
  498.2 1.0 copy-start.3
Sparse Core Ops, SparseCore 0:
  16.4 86.3 all-gather.7
  106.5 101.1 all-gather.5
where the time goes:
time: 513 us; the launch traced here: 511 us
  blocking collectives  393 us (77%)
  local copies, waits for them, and re-layouts  53.9 us (11%)
  other arithmetic  36.3 us (7%)
  between operations  14.3 us (3%)
  matrix products  8.66 us (2%)
    psum x1, blocking collectives, per_device(): totals = lax.psum(full_terms, 'rep')  255 us
    psum x1, blocking collectives, per_device(): projected = lax.psum(partial_sum, 'exp')  80 us
    all_gather x1, blocking collectives, per_device(): lax.all_gather(window_out, 'rep', axis=0, tiled=True)  58.3 us
  transfers between devices with their start and end apart: 3, of which 0 were waited for; matrix products, arithmetic and copies ran while one was open for 15% of the time, Pallas kernels for 0%

commit v1 on v0

v1 whole, which is shorter than its diff:
```python
import math

import jax
import jax.numpy as jnp
from jax import lax
from jax.experimental import pallas as pl
from jax.experimental.pallas import tpu as pltpu
from jax.sharding import PartitionSpec as P

MIG = 2
LANES = 128
SUB = 8
F32 = jnp.float32
BF16 = jnp.bfloat16


def _smem():
    return pl.BlockSpec(memory_space=pltpu.SMEM)


def _vmem():
    return pl.BlockSpec(memory_space=pltpu.VMEM)


def _call(body, name, out_shape, ins, outs, args, scratch=(), flops=0, nbytes=0):
    return pl.pallas_call(
        body,
        name=name,
        out_shape=out_shape,
        in_specs=ins,
        out_specs=outs,
        scratch_shapes=list(scratch),
        compiler_params=pltpu.CompilerParams(vmem_limit_bytes=32 * 1024 * 1024),
        cost_estimate=pl.CostEstimate(flops=flops, bytes_accessed=nbytes, transcendentals=0),
    )(*args)


def _present(anchor_ref, base, requests):
    mask = jnp.int32(0)
    for g in range(requests):
        a = anchor_ref[base + g] - base
        inside = (a >= 0) & (a < requests)
        mask = mask | jnp.where(inside, jnp.int32(1) << jnp.clip(a, 0, requests - 1), 0)
    return mask


def _slots(rep_ref, anchor_ref, requests):
    base = rep_ref[0] * requests
    count = jnp.int32(0)
    found = []
    for g in range(requests):
        a = anchor_ref[base + g]
        local = a - base
        arrived = (local < 0) | (local >= requests)
        found.append((a, jnp.clip(local, 0, requests - 1), arrived, jnp.minimum(count, MIG - 1)))
        count = count + jnp.where(arrived, 1, 0)
    return found


def _pack_body(requests, rep_ref, anchor_ref, table_ref, pool_ref, window_ref, scan_ref, out_ref, win_ref):
    base = rep_ref[0] * requests
    mask = _present(anchor_ref, base, requests)
    first, second = jnp.int32(0), jnp.int32(0)
    for o in reversed(range(requests)):
        leaves = ((mask >> o) & 1) == 0
        second = jnp.where(leaves, first, second)
        first = jnp.where(leaves, o, first)
    pages = table_ref.shape[1]
    blocks = scan_ref.shape[2] // LANES
    taps = window_ref.shape[1]
    win_ref[...] = jnp.zeros_like(win_ref)
    for j, o in enumerate((first, second)):
        scan = scan_ref[o]
        high = scan.astype(BF16).astype(F32)
        rest = scan - high
        middle = rest.astype(BF16).astype(F32)
        low = rest - middle
        win_ref[0:taps, :] = window_ref[o].astype(F32)
        win = win_ref[...]
        tails = []
        for part in (high, middle, low):
            for b in range(blocks):
                for h in range(scan.shape[0] // SUB):
                    tails.append(part[h * SUB : (h + 1) * SUB, b * LANES : (b + 1) * LANES])
        for b in range(blocks):
            tails.append(win[:, b * LANES : (b + 1) * LANES])
        for m in range(pages):
            page = pool_ref[table_ref[o, m], 0].astype(F32)
            for c in range(2):
                for h in range(2):
                    i = 4 * m + 2 * c + h
                    tail = tails[i] if i < len(tails) else jnp.zeros((SUB, LANES), F32)
                    head = page[c, h * SUB : (h + 1) * SUB, :]
                    out_ref[i, j] = jnp.concatenate([head, tail], axis=0).astype(BF16)


def _route_body(replicas, requests, anchor_ref, dep_ref, out_ref, bit_ref):
    def note(s, carry):
        mask = _present(anchor_ref, s * requests, requests)
        bit_ref[s] = (~mask) & (mask + 1)
        return carry

    lax.fori_loop(0, replicas, note, 0)

    def place(d, carry):
        count = jnp.int32(0)
        for g in range(requests):
            a = anchor_ref[d * requests + g]
            s = a // requests
            bit = jnp.int32(1) << (a - s * requests)
            out_ref[d * MIG + count] = s * MIG + jnp.where(bit_ref[s] != bit, 1, 0)
            count = count + jnp.where(s != d, 1, 0)
        return carry

    lax.fori_loop(0, replicas, place, 0)


def _select_body(count, index_ref, in_ref, out_ref):
    for k in range(count):
        i = index_ref[k]
        out_ref[k // MIG, k % MIG] = in_ref[i // MIG, i % MIG]


def _expert_body(rep_ref, hidden_ref, weight_ref, keep_ref, send_ref, rows_ref):
    slots = hidden_ref.shape[1]
    cap = slots // 32
    r = rep_ref[0]

    @pl.when(pl.program_id(0) == 0)
    def _():
        row = lax.broadcasted_iota(jnp.int32, (slots, slots), 0)
        col = lax.broadcasted_iota(jnp.int32, (slots, slots), 1)
        zh, x, c = r // 8, (r // 2) % 4, r % 2
        to_c = (c + row // (slots // 2)) % 2
        to_x = (x + (row // (slots // 8)) % 4) % 4
        to_z = (zh + (row // cap) % 4) % 4
        want = ((to_z * 4 + to_x) * 2 + to_c) * cap + row % cap
        pick = jnp.where(want == col, 1.0, 0.0).astype(BF16)
        rows_ref[...] = jnp.dot(pick, hidden_ref[0], preferred_element_type=F32).astype(BF16)

    total = jnp.dot(rows_ref[...], weight_ref[0], preferred_element_type=F32)
    half = slots // 2
    keep_ref[...] = total[:half].astype(BF16)
    send_ref[...] = total[half:].astype(BF16)


def _fold2_body(keep_ref, got_ref, o0, o1, o2, o3):
    total = keep_ref[...].astype(F32) + got_ref[...].astype(F32)
    n = total.shape[0] // 4
    for k, o in enumerate((o0, o1, o2, o3)):
        o[...] = total[k * n : (k + 1) * n].astype(BF16)


def _fold4_body(a, b, c, d, o0, o1, o2, o3):
    total = (a[...].astype(F32) + b[...].astype(F32)) + (c[...].astype(F32) + d[...].astype(F32))
    n = total.shape[0] // 4
    for k, o in enumerate((o0, o1, o2, o3)):
        o[...] = total[k * n : (k + 1) * n].astype(BF16)


def _act_body(
    requests, rep_ref, anchor_ref, moved_ref, window_ref, conv_ref, taps_ref, bias_ref, mix_ref,
    e0, e1, e2, e3, out_ref, act_ref, win_ref, mixed_ref,
):
    blocks = conv_ref.shape[1] // LANES
    taps = window_ref.shape[1]
    first = 3 * blocks * 2
    for j in range(MIG):
        for b in range(blocks):
            win_ref[j, :, b * LANES : (b + 1) * LANES] = moved_ref[first + b, j].astype(F32)[SUB : 2 * SUB]
    weights = taps_ref[...]
    for g, (_, local, arrived, order) in enumerate(_slots(rep_ref, anchor_ref, requests)):
        mine = window_ref[local].astype(F32)
        other = win_ref[order][0:taps]
        window = jnp.where(arrived, other, mine)
        mixed_ref[g : g + 1, :] = jnp.sum(window * weights[0:taps], axis=0, keepdims=True)
    mixed = mixed_ref[...] + conv_ref[...].astype(F32) * weights[taps : taps + 1] + bias_ref[...]
    act = mixed * (1.0 / (1.0 + jnp.exp(-mixed)))
    act_ref[...] = act
    partial = jnp.dot(act.astype(BF16), mix_ref[...], preferred_element_type=F32)
    rank = 2 * LANES
    high = partial.astype(BF16).astype(F32)
    low = (partial - high)[:, rank:]
    fill = jnp.zeros((requests, LANES - 2 * low.shape[1]), F32)
    tail = jnp.concatenate([high[:, rank:], low, fill], axis=1)
    packed = jnp.concatenate([high[:, :rank], tail], axis=1)
    total = (e0[...].astype(F32) + e1[...].astype(F32)) + (e2[...].astype(F32) + e3[...].astype(F32))
    experts = out_ref.shape[0]
    width = total.shape[1] // experts
    empty = jnp.zeros((requests - 2 * total.shape[0], LANES), F32)
    for e in range(experts):
        left = total[:, e * width : e * width + LANES]
        right = total[:, e * width + LANES : (e + 1) * width]
        block = jnp.concatenate([left, right, empty], axis=0)
        out_ref[e] = jnp.concatenate([packed, block], axis=1).astype(BF16)


def _final_body(
    requests, states, rep_ref, anchor_ref, routes_ref, share_ref, sums_ref, moved_ref, act_ref, gate_ref, scan_ref,
    step_ref, bias_ref, decay_ref, skip_ref, gated_ref, mix_ref, arr_ref, count_ref, y_ref,
):
    experts = sums_ref.shape[0]
    blocks = act_ref.shape[1] // LANES
    rank = 2 * LANES
    for e in range(experts):
        count_ref[e] = 0
    row = lax.broadcasted_iota(jnp.int32, (requests, LANES), 0)
    col = lax.broadcasted_iota(jnp.int32, (requests, LANES), 1)
    share = jnp.zeros((requests, LANES), F32)
    cap = SUB // 2
    for t in range(requests):
        for k in range(routes_ref.shape[1]):
            e = routes_ref[t, k]
            place = count_ref[e]
            count_ref[e] = place + 1
            share = share + jnp.where((row == t) & (col == e * SUB + place), share_ref[t, k], 0.0)
    parts = []
    rest = share
    for _ in range(3):
        part = rest.astype(BF16)
        parts.append(part)
        rest = rest - part.astype(F32)
    outs = sums_ref[:, :, rank + LANES :].astype(F32)[:, 0:SUB].reshape(experts * SUB, LANES).astype(BF16)
    left = sum(jnp.dot(p, outs, preferred_element_type=F32) for p in reversed(parts))
    shifted = [pltpu.roll(p.astype(F32), cap, 1).astype(BF16) for p in parts]
    right = sum(jnp.dot(p, outs, preferred_element_type=F32) for p in reversed(shifted))
    mix_ref[...] = jnp.concatenate([left, right], axis=1).astype(BF16)
    projected = sums_ref[0, :, 0 : rank + LANES].astype(F32)
    for e in range(1, experts):
        projected = projected + sums_ref[e, :, 0 : rank + LANES].astype(F32)
    step = jnp.dot(projected[:, :rank].astype(BF16), step_ref[...], preferred_element_type=F32) + bias_ref[...]
    step = jnp.maximum(step, 0.0) + jnp.log1p(jnp.exp(-jnp.abs(step)))
    tail = projected[:, rank:]
    both = tail + pltpu.roll(tail, LANES - 2 * states, 1)
    columns = jnp.transpose(both)
    for j in range(MIG):
        for b in range(blocks):
            for h in range(states // SUB):
                i = b * (states // SUB) + h
                n = blocks * (states // SUB)
                high = moved_ref[i, j].astype(F32)[SUB : 2 * SUB]
                middle = moved_ref[n + i, j].astype(F32)[SUB : 2 * SUB]
                lowest = moved_ref[2 * n + i, j].astype(F32)[SUB : 2 * SUB]
                arr_ref[j, h * SUB : (h + 1) * SUB, b * LANES : (b + 1) * LANES] = high + (middle + lowest)
    rate = -jnp.exp(decay_ref[...])
    act = act_ref[...]
    flow = step * act
    for g, (_, local, arrived, order) in enumerate(_slots(rep_ref, anchor_ref, requests)):
        old = jnp.where(arrived, arr_ref[order], scan_ref[local])
        inflow = columns[0:states, g : g + 1]
        readout = columns[states : 2 * states, g : g + 1]
        state = jnp.exp(step[g : g + 1] * rate) * old + inflow * flow[g : g + 1]
        y_ref[g : g + 1, :] = jnp.sum(readout * state, axis=0, keepdims=True)
    gate = gate_ref[...].astype(F32)
    output = y_ref[...] + skip_ref[...] * act
    gated_ref[...] = (output * (gate * (1.0 / (1.0 + jnp.exp(-gate))))).astype(BF16)


def _attend_body(
    requests, rep_ref, anchor_ref, len_ref, table_ref, query_ref, key_ref, value_ref, pool_ref, moved_ref, dep_ref,
    out_ref, pages_ref, keys_ref, values_ref,
):
    head = key_ref.shape[1]
    heads = query_ref.shape[1] // head
    pool, _, _, page, _ = pool_ref.shape
    table = table_ref[...].astype(F32).astype(BF16)
    pages = table.shape[1]
    span = pages * page
    slots = _slots(rep_ref, anchor_ref, requests)
    row1 = lax.broadcasted_iota(jnp.int32, (requests, 1), 0)
    row = lax.broadcasted_iota(jnp.int32, (requests, requests), 0)
    col = lax.broadcasted_iota(jnp.int32, (requests, requests), 1)
    live = jnp.zeros((requests, 1), jnp.int32)
    order = jnp.full((requests, 1), -1, jnp.int32)
    pick = jnp.zeros((requests, requests), F32)
    live_of = [jnp.int32(0)] * MIG
    for g, (a, local, arrived, place) in enumerate(slots):
        length = len_ref[a]
        live = jnp.where(row1 == g, length, live)
        order = jnp.where((row1 == g) & arrived, place, order)
        pick = jnp.where((row == g) & (col == local), 1.0, pick)
        live_of = [jnp.where(arrived & (place == j), length, live_of[j]) for j in range(MIG)]
    mine = jnp.dot(pick.astype(BF16), table, preferred_element_type=F32).astype(jnp.int32)
    here = jnp.where(order < 0, live, 0)
    at = lax.broadcasted_iota(jnp.int32, (requests, pool * page), 1)
    which, token = at // page, at % page
    seen = jnp.zeros((requests, pool * page), jnp.bool_)
    for m in range(pages):
        seen = seen | ((mine[:, m : m + 1] == which) & (token + m * page < here))
    at = lax.broadcasted_iota(jnp.int32, (requests, MIG * span), 1)
    seen_moved = (at // span == order) & (at % span < live)
    down = lax.broadcasted_iota(jnp.int32, (span, head), 0)
    for j in range(MIG):
        for m in range(pages):
            for h in range(2):
                for c, ref in ((0, keys_ref), (1, values_ref)):
                    start = j * span + m * page + h * SUB
                    ref[start : start + SUB, :] = moved_ref[4 * m + 2 * c + h, j].astype(F32)[0:SUB]
        for c, ref in ((0, keys_ref), (1, values_ref)):
            block = ref[j * span : (j + 1) * span, :]
            pages_ref[j, 0, c] = jnp.where(down < live_of[j], block, 0.0).astype(BF16)
    moved_keys = keys_ref[...].astype(BF16)
    moved_values = values_ref[...].astype(BF16)
    pool_keys = pool_ref[:, 0, 0].reshape(pool * page, head)
    pool_values = pool_ref[:, 0, 1].reshape(pool * page, head)
    query = query_ref[...]
    queries = jnp.concatenate([query[:, h * head : (h + 1) * head] for h in range(heads)], axis=0)
    scale = 1.0 / math.sqrt(head)
    turn = (((1,), (1,)), ((), ()))
    scores = lax.dot_general(queries, pool_keys, turn, preferred_element_type=F32) * scale
    scores_moved = lax.dot_general(queries, moved_keys, turn, preferred_element_type=F32) * scale
    new_key = jnp.concatenate([key_ref[...].astype(F32)] * heads, axis=0)
    new_value = jnp.concatenate([value_ref[...].astype(F32)] * heads, axis=0)
    own = jnp.sum(queries.astype(F32) * new_key, axis=1, keepdims=True) * scale
    far = F32(-1e30)
    seen = jnp.concatenate([jnp.where(seen, 1.0, 0.0)] * heads, axis=0) > 0.5
    seen_moved = jnp.concatenate([jnp.where(seen_moved, 1.0, 0.0)] * heads, axis=0) > 0.5
    scores = jnp.where(seen, scores, far)
    scores_moved = jnp.where(seen_moved, scores_moved, far)
    highest = jnp.maximum(
        jnp.maximum(jnp.max(scores, axis=1, keepdims=True), jnp.max(scores_moved, axis=1, keepdims=True)), own
    )
    e_pool = jnp.exp(scores - highest)
    e_moved = jnp.exp(scores_moved - highest)
    e_own = jnp.exp(own - highest)
    total = jnp.sum(e_pool, axis=1, keepdims=True) + jnp.sum(e_moved, axis=1, keepdims=True) + e_own
    w_pool = (e_pool / total).astype(BF16)
    w_moved = (e_moved / total).astype(BF16)
    w_own = (e_own / total).astype(BF16).astype(F32)
    context = jnp.dot(w_pool, pool_values, preferred_element_type=F32)
    context = context + jnp.dot(w_moved, moved_values, preferred_element_type=F32) + w_own * new_value
    for h in range(heads):
        out_ref[:, h * head : (h + 1) * head] = context[h * requests : (h + 1) * requests].astype(BF16)


def per_device(
    query,
    new_key,
    new_value,
    page_pool,
    block_table,
    lengths,
    anchor,
    conv_input,
    gate_input,
    window_state,
    scan_state,
    filter_taps,
    filter_bias,
    mix_weight,
    step_weight,
    step_bias,
    log_decay,
    skip_gain,
    routes,
    route_weight,
    expert_hidden,
    down_weight,
):
    requests, channels = query.shape
    replicas = lax.axis_size("rep")
    experts = lax.axis_size("exp")
    rep = lax.axis_index("rep").astype(jnp.int32).reshape(1)
    states = log_decay.shape[0]
    head = new_key.shape[1]
    pages, page = block_table.shape[1], page_pool.shape[3]
    slots = expert_hidden.shape[1]
    features = down_weight.shape[2]
    piece = jax.ShapeDtypeStruct((replicas, MIG, 2 * SUB, LANES), BF16)

    packed = _call(
        lambda *refs: _pack_body(requests, *refs),
        "pack_leaving",
        piece,
        [_smem()] * 3 + [_vmem()] * 3,
        _vmem(),
        (rep, anchor, block_table, page_pool, window_state, scan_state),
        scratch=[pltpu.VMEM((SUB, channels), F32)],
        nbytes=1 << 20,
    )
    spread = lax.all_to_all(packed, "rep", split_axis=0, concat_axis=0, tiled=True)

    index = _call(
        lambda *refs: _route_body(replicas, requests, *refs),
        "route_pieces",
        jax.ShapeDtypeStruct((replicas * MIG + SUB,), jnp.int32),
        [_smem(), pl.BlockSpec(memory_space=pl.ANY)],
        _smem(),
        (anchor, packed),
        scratch=[pltpu.SMEM((replicas,), jnp.int32)],
        nbytes=8 << 20,
    )

    tile = features // 4
    keep, send = pl.pallas_call(
        _expert_body,
        name="expert_terms",
        grid=(features // tile,),
        out_shape=[jax.ShapeDtypeStruct((slots // 2, features), BF16)] * 2,
        in_specs=[
            _smem(),
            pl.BlockSpec((1, slots, expert_hidden.shape[2]), lambda i: (0, 0, 0)),
            pl.BlockSpec((1, down_weight.shape[1], tile), lambda i: (0, 0, i)),
        ],
        out_specs=[pl.BlockSpec((slots // 2, tile), lambda i: (0, i))] * 2,
        scratch_shapes=[pltpu.VMEM((slots, expert_hidden.shape[2]), BF16)],
        compiler_params=pltpu.CompilerParams(vmem_limit_bytes=32 * 1024 * 1024),
        cost_estimate=pl.CostEstimate(flops=2 * slots * 384 * features, bytes_accessed=5 << 20, transcendentals=0),
    )(rep, expert_hidden, down_weight)

    def at(z, x, c):
        return (z * 4 + x) * 2 + c

    every = [(z, x, c) for z in range(4) for x in range(4) for c in range(2)]
    got = lax.ppermute(send, "rep", [(at(z, x, c), at(z, x, 1 - c)) for z, x, c in every])
    part = jax.ShapeDtypeStruct((slots // 8, features), BF16)
    by_x = _call(_fold2_body, "fold_cores", [part] * 4, [_vmem()] * 2, [_vmem()] * 4, (keep, got), nbytes=2 << 20)
    came = [by_x[0]] + [
        lax.ppermute(by_x[k], "rep", [(at(z, x, c), at(z, (x + k) % 4, c)) for z, x, c in every]) for k in (2, 1, 3)
    ]
    part = jax.ShapeDtypeStruct((slots // 32, features), BF16)
    by_z = _call(_fold4_body, "fold_x", [part] * 4, [_vmem()] * 4, [_vmem()] * 4, came, nbytes=1 << 20)
    own = [by_z[0]] + [
        lax.ppermute(by_z[k], "rep", [(at(z, x, c), at((z + k) % 4, x, c)) for z, x, c in every]) for k in (2, 1, 3)
    ]

    onward = _call(
        lambda *refs: _select_body(replicas * MIG, *refs),
        "select_pieces",
        piece,
        [_smem(), _vmem()],
        _vmem(),
        (index, spread),
        nbytes=1 << 19,
    )
    moved = lax.all_to_all(onward, "rep", split_axis=0, concat_axis=0, tiled=True)

    sums, act = _call(
        lambda *refs: _act_body(requests, *refs),
        "filter_and_project",
        [
            jax.ShapeDtypeStruct((experts, requests, 4 * LANES), BF16),
            jax.ShapeDtypeStruct((requests, channels), F32),
        ],
        [_smem()] * 2 + [_vmem()] * 10,
        [_vmem()] * 2,
        (rep, anchor, moved, window_state, conv_input, filter_taps, filter_bias.reshape(1, channels), mix_weight, *own),
        scratch=[pltpu.VMEM((MIG, SUB, channels), F32), pltpu.VMEM((requests, channels), F32)],
        nbytes=1 << 20,
    )
    sums_all = lax.all_to_all(sums, "exp", split_axis=0, concat_axis=0, tiled=True)

    attended, pages_out = _call(
        lambda *refs: _attend_body(requests, *refs),
        "attend",
        [
            jax.ShapeDtypeStruct((requests, channels), BF16),
            jax.ShapeDtypeStruct((MIG, 1, 2, pages * page, head), BF16),
        ],
        [_smem()] * 3 + [_vmem()] * 6 + [pl.BlockSpec(memory_space=pl.ANY)],
        [_vmem()] * 2,
        (rep, anchor, lengths, block_table, query, new_key, new_value, page_pool, moved, act),
        scratch=[pltpu.VMEM((MIG * pages * page, head), F32)] * 2,
        nbytes=4 << 20,
    )

    gated, mixed = _call(
        lambda *refs: _final_body(requests, states, *refs),
        "update_state",
        [
            jax.ShapeDtypeStruct((requests, channels), BF16),
            jax.ShapeDtypeStruct((requests, features // experts), BF16),
        ],
        [_smem()] * 4 + [_vmem()] * 9,
        [_vmem()] * 2,
        (
            rep, anchor, routes, route_weight, sums_all, moved, act, gate_input, scan_state, step_weight,
            step_bias.reshape(1, channels), log_decay, skip_gain.reshape(1, channels),
        ),
        scratch=[
            pltpu.VMEM((MIG, states, channels), F32),
            pltpu.SMEM((experts,), jnp.int32),
            pltpu.VMEM((requests, channels), F32),
        ],
        nbytes=1 << 20,
    )
    return (attended, pages_out, gated, mixed)


def solution(mesh):
    placed = (
        P("rep", "exp"),
        P("rep", "exp"),
        P("rep", "exp"),
        P("rep", "exp", None, None, None),
        P("rep", None),
        P(),
        P(),
        P("rep", "exp"),
        P("rep", "exp"),
        P("rep", None, "exp"),
        P("rep", None, "exp"),
        P(None, "exp"),
        P("exp"),
        P("exp", None),
        P(None, "exp"),
        P("exp"),
        P(None, "exp"),
        P("exp"),
        P("rep", None),
        P("rep", None),
        P("exp", None, "rep"),
        P("exp", "rep", None),
    )
    return jax.shard_map(
        per_device,
        mesh=mesh,
        in_specs=placed,
        out_specs=(
            P("rep", "exp"),
            P("rep", "exp", None, None, None),
            P("rep", "exp"),
            P("rep", "exp"),
        ),
        check_vma=False,
    )
```

time: 513 us -> 123 us (0.24)
  the two profiles are of different devices: /device:TPU:2 before, /device:TPU:6 now
where the time goes in v1:
time: 123 us; the launch traced here: 122 us
  starting transfers between devices  65.5 us (53%)
  waiting for transfers between devices  27.7 us (23%)
  Pallas kernels  17.9 us (15%)
  local copies, waits for them, and re-layouts  9.52 us (8%)
    ppermute x3, starting transfers between devices, per_device(): lax.ppermute(by_z[k], 'rep', [(at(z, x, c), at((z + k) % 4, x, c)) for z,...  21.9 us
    all_to_all x1, starting transfers between devices, per_device(): lax.all_to_all(packed, 'rep', split_axis=0, concat_axis=0, tiled=True)  18.2 us
    pallas_call x8, Pallas kernels, _call(): pl.pallas_call(body, name=name, out_shape=out_shape, in_specs=ins, out_sp...  16.1 us
    all_to_all x1, waiting for transfers between devices, per_device(): lax.all_to_all(packed, 'rep', split_axis=0, concat_axis=0, tiled=True)  10.8 us
    unnamed x53, local copies, waits for them, and re-layouts  9.52 us
    ppermute x3, starting transfers between devices, per_device(): lax.ppermute(by_x[k], 'rep', [(at(z, x, c), at(z, (x + k) % 4, c)) for z,...  9.29 us
    all_to_all x1, starting transfers between devices, per_device(): lax.all_to_all(onward, 'rep', split_axis=0, concat_axis=0, tiled=True)  7.87 us
    all_to_all x1, waiting for transfers between devices, per_device(): lax.all_to_all(sums, 'exp', split_axis=0, concat_axis=0, tiled=True)  7.83 us
  transfers between devices with their start and end apart: 10, of which 7 were waited for; matrix products, arithmetic and copies ran while one was open for 1% of the time, Pallas kernels for 10%

profile of v1, /device:TPU:6, one launch (start us, length us, event | category | flops | bytes accessed | tf_op | source)
XLA Modules:
  0.0 121.7 jit_solution(10828866830430792169)
XLA Ops:
  0.6 0.0 copy-start
  0.6 1.0 copy.27.refs_4_.refs_3_
  1.6 0.8 copy.30.refs_2_.refs_3_
  2.4 1.0 copy-done.1
  3.4 1.0 copy-done.3
  4.4 0.7 copy-done.8
  5.1 1.5 %pack_leaving.1.refs_1_ = bf16[32,2,16,128]{3,2,1,0:T(8,128)(2,1)} custom-call(s32[1]{0:T(128)} %bitcast.refs_0_.rep_ref, s32[512]{0:T(512)S(1)} %copy-done.8, s32[16,8]{1,0:T(8,128)S(1)} %copy.30.refs_2_.refs_3_, bf16[48,1,2,16,128]{4,3,2,1,0:T(8,128)(2,1)S(1)} %copy-done.3, bf16[16,3,512]{2,1,0:T(4,128)(2,1)S(1)} %copy.27.refs_4_.refs_3_, ...), custom_call_target="tpu_custom_call" | custom-call | bytes 1048576 | tf_op jit(solution)/shard_map/pack_leaving/pallas_call | solution.py:26
  6.6 18.2 %all-to-all-start = ((bf16[32,2,16,128]{3,2,1,0:T(8,128)(2,1)}), bf16[32,2,16,128]{3,2,1,0:T(8,128)(2,1)S(1)}, u32[]{:S(2)}, u32[]{:S(2)}) async-start(bf16[32,2,16,128]{3,2,1,0:T(8,128)(2,1)} %pack_leaving.1.refs_1_), calls=%async_computation | async-start | bytes 524288 | tf_op jit(solution)/shard_map/all_to_all | solution.py:381
  24.8 0.0 copy-start.9
  24.8 0.7 copy-done.9
  25.5 7.8 %route_pieces.1.refs_0_ = s32[72]{0:T(128)S(1)} custom-call(s32[512]{0:T(512)S(1)} %copy-done.9, bf16[32,2,16,128]{3,2,1,0:T(8,128)(2,1)} %pack_leaving.1.refs_1_), custom_call_target="tpu_custom_call" | custom-call | bytes 8388608 | tf_op jit(solution)/shard_map/route_pieces/pallas_call | solution.py:26
  33.3 10.8 %all-to-all-done.refs_1_ = bf16[32,2,16,128]{3,2,1,0:T(8,128)(2,1)S(1)} async-done(((bf16[32,2,16,128]{3,2,1,0:T(8,128)(2,1)}), bf16[32,2,16,128]{3,2,1,0:T(8,128)(2,1)S(1)}, u32[]{:S(2)}, u32[]{:S(2)}) %all-to-all-start) | async-done | bytes 262176 | tf_op jit(solution)/shard_map/all_to_all | solution.py:381
  44.1 1.0 select_pieces.1
  45.0 0.0 copy-start.5
  45.0 0.7 copy-done.5
  45.7 7.9 %all-to-all-start.1 = ((bf16[32,2,16,128]{3,2,1,0:T(8,128)(2,1)}), bf16[32,2,16,128]{3,2,1,0:T(8,128)(2,1)S(1)}, u32[]{:S(2)}, u32[]{:S(2)}) async-start(bf16[32,2,16,128]{3,2,1,0:T(8,128)(2,1)} %copy-done.5), calls=%async_computation.1 | async-start | bytes 524288 | tf_op jit(solution)/shard_map/all_to_all | solution.py:436
  53.6 0.0 copy-done
  53.6 0.0 copy-start.7
  53.6 0.9 copy-done.7
  54.5 1.8 %expert_terms.1 = (bf16[64,4096]{1,0:T(8,128)(2,1)S(1)}, bf16[64,4096]{1,0:T(8,128)(2,1)S(1)}) custom-call(s32[1]{0:T(128)} %bitcast.refs_0_.rep_ref, bf16[1,128,384]{2,1,0:T(8,128)(2,1)S(1)} %copy-done.7, bf16[1,384,4096]{2,1,0:T(8,128)(2,1)S(1)} %copy-done), custom_call_target="tpu_custom_call" | custom-call | flops 402653184 | bytes 5242880 | tf_op jit(solution)/shard_map/expert_terms/pallas_call | solution.py:395
  56.3 0.0 copy-start.22
  56.3 0.0 copy-start.23
  56.4 0.0 copy-start.4
  56.4 0.0 copy-start.14
  56.4 0.0 copy-start.17
  56.4 0.0 copy-start.19
  56.4 0.0 copy-start.2
  56.4 0.0 copy-start.6
  56.4 0.0 copy-start.20
  56.4 0.0 copy-start.21
  56.5 2.2 %collective-permute-start = (bf16[64,4096]{1,0:T(8,128)(2,1)S(1)}, bf16[64,4096]{1,0:T(8,128)(2,1)S(1)}, u32[]{:S(2)}, u32[]{:S(2)}) collective-permute-start(bf16[64,4096]{1,0:T(8,128)(2,1)S(1)} %get-tuple-element.21), channel_id=1, source_target_pairs={{0,16},{16,0},{32,48},{48,32},{64,80},{80,64},{96,112},{112,96},{1... | collective-permute-start | bytes 1572872 | tf_op jit(solution)/shard_map/ppermute | solution.py:415
  58.7 1.7 %collective-permute-done.got_ref = bf16[64,4096]{1,0:T(8,128)(2,1)S(1)} collective-permute-done((bf16[64,4096]{1,0:T(8,128)(2,1)S(1)}, bf16[64,4096]{1,0:T(8,128)(2,1)S(1)}, u32[]{:S(2)}, u32[]{:S(2)}) %collective-permute-start) | collective-permute-done | bytes 524320 | tf_op jit(solution)/shard_map/ppermute | solution.py:415
  60.4 0.1 fold_cores.1
  60.5 3.4 %collective-permute-start.1 = (bf16[16,4096]{1,0:T(8,128)(2,1)S(1)}, bf16[16,4096]{1,0:T(8,128)(2,1)S(1)}, u32[]{:S(2)}, u32[]{:S(2)}) collective-permute-start(bf16[16,4096]{1,0:T(8,128)(2,1)S(1)} %get-tuple-element.23), channel_id=1, source_target_pairs={{0,64},{16,80},{32,96},{48,112},{64,0},{80,16},{96,32},{112,48},{1... | collective-permute-start | bytes 393224 | tf_op jit(solution)/shard_map/ppermute | solution.py:419
  63.9 4.0 %collective-permute-start.2 = (bf16[16,4096]{1,0:T(8,128)(2,1)S(1)}, bf16[16,4096]{1,0:T(8,128)(2,1)S(1)}, u32[]{:S(2)}, u32[]{:S(2)}) collective-permute-start(bf16[16,4096]{1,0:T(8,128)(2,1)S(1)} %get-tuple-element.24), channel_id=1, source_target_pairs={{0,32},{16,48},{32,64},{48,80},{64,96},{80,112},{96,0},{112,16},{1... | collective-permute-start | bytes 393224 | tf_op jit(solution)/shard_map/ppermute | solution.py:419
  67.9 1.9 %collective-permute-start.3 = (bf16[16,4096]{1,0:T(8,128)(2,1)S(1)}, bf16[16,4096]{1,0:T(8,128)(2,1)S(1)}, u32[]{:S(2)}, u32[]{:S(2)}) collective-permute-start(bf16[16,4096]{1,0:T(8,128)(2,1)S(1)} %get-tuple-element.25), channel_id=1, source_target_pairs={{0,96},{16,112},{32,0},{48,16},{64,32},{80,48},{96,64},{112,80},{1... | collective-permute-start | bytes 393224 | tf_op jit(solution)/shard_map/ppermute | solution.py:419
  69.8 0.1 collective-permute-done.1.b
  70.0 1.2 %collective-permute-done.2.c = bf16[16,4096]{1,0:T(8,128)(2,1)S(1)} collective-permute-done((bf16[16,4096]{1,0:T(8,128)(2,1)S(1)}, bf16[16,4096]{1,0:T(8,128)(2,1)S(1)}, u32[]{:S(2)}, u32[]{:S(2)}) %collective-permute-start.2) | collective-permute-done | bytes 131104 | tf_op jit(solution)/shard_map/ppermute | solution.py:419
  71.2 4.8 %collective-permute-done.3.d = bf16[16,4096]{1,0:T(8,128)(2,1)S(1)} collective-permute-done((bf16[16,4096]{1,0:T(8,128)(2,1)S(1)}, bf16[16,4096]{1,0:T(8,128)(2,1)S(1)}, u32[]{:S(2)}, u32[]{:S(2)}) %collective-permute-start.3) | collective-permute-done | bytes 131104 | tf_op jit(solution)/shard_map/ppermute | solution.py:419
  76.0 0.1 fold_x.1
  76.1 12.1 %collective-permute-start.4 = (bf16[4,4096]{1,0:T(4,128)(2,1)S(1)}, bf16[4,4096]{1,0:T(4,128)(2,1)S(1)}, u32[]{:S(2)}, u32[]{:S(2)}) collective-permute-start(bf16[4,4096]{1,0:T(4,128)(2,1)S(1)} %get-tuple-element.27), channel_id=1, source_target_pairs={{0,256},{16,272},{32,288},{48,304},{64,320},{80,336},{96,352},{112... | collective-permute-start | bytes 98312 | tf_op jit(solution)/shard_map/ppermute | solution.py:424
  88.2 2.5 %collective-permute-start.5 = (bf16[4,4096]{1,0:T(4,128)(2,1)S(1)}, bf16[4,4096]{1,0:T(4,128)(2,1)S(1)}, u32[]{:S(2)}, u32[]{:S(2)}) collective-permute-start(bf16[4,4096]{1,0:T(4,128)(2,1)S(1)} %get-tuple-element.28), channel_id=1, source_target_pairs={{0,128},{16,144},{32,160},{48,176},{64,192},{80,208},{96,224},{112... | collective-permute-start | bytes 98312 | tf_op jit(solution)/shard_map/ppermute | solution.py:424
  90.7 7.2 %collective-permute-start.6 = (bf16[4,4096]{1,0:T(4,128)(2,1)S(1)}, bf16[4,4096]{1,0:T(4,128)(2,1)S(1)}, u32[]{:S(2)}, u32[]{:S(2)}) collective-permute-start(bf16[4,4096]{1,0:T(4,128)(2,1)S(1)} %get-tuple-element.29), channel_id=1, source_target_pairs={{0,384},{16,400},{32,416},{48,432},{64,448},{80,464},{96,480},{112... | collective-permute-start | bytes 98312 | tf_op jit(solution)/shard_map/ppermute | solution.py:424
  97.9 1.2 copy.29.refs_7_
  99.1 0.0 collective-permute-done.4.refs_9_
  99.1 0.0 collective-permute-done.5.refs_10_
  99.1 1.3 %collective-permute-done.6.refs_11_ = bf16[4,4096]{1,0:T(4,128)(2,1)S(1)} collective-permute-done((bf16[4,4096]{1,0:T(4,128)(2,1)S(1)}, bf16[4,4096]{1,0:T(4,128)(2,1)S(1)}, u32[]{:S(2)}, u32[]{:S(2)}) %collective-permute-start.6) | collective-permute-done | bytes 32800 | tf_op jit(solution)/shard_map/ppermute | solution.py:424
  100.4 0.0 all-to-all-done.1.refs_2_.refs_8_.refs_5_
  100.4 0.0 copy-done.10
  100.4 0.0 copy-done.13
  100.4 0.0 copy-start.15
  100.5 0.7 copy-done.15
  101.1 0.7 copy-done.18
  101.8 1.6 %filter_and_project.1 = (bf16[16,16,512]{2,1,0:T(8,128)(2,1)}, f32[16,512]{1,0:T(8,128)S(1)}) custom-call(s32[1]{0:T(128)} %bitcast.refs_0_.rep_ref, s32[512]{0:T(512)S(1)} %copy-done.10, bf16[32,2,16,128]{3,2,1,0:T(8,128)(2,1)S(1)} %all-to-all-done.1.refs_2_.refs_8_.refs_5_, bf16[16,3,512]{2,1,0:T(4,128)(2,1)S(1)} %copy.27.refs_4_.refs_3_, ...), custom_call_target="tpu_custom_call" | custom-call | bytes 1048576 | tf_op jit(solution)/shard_map/filter_and_project/pallas_call | solution.py:26
  103.5 6.1 %all-to-all-start.2 = ((bf16[16,16,512]{2,1,0:T(8,128)(2,1)}), bf16[16,16,512]{2,1,0:T(8,128)(2,1)S(1)}, u32[]{:S(2)}, u32[]{:S(2)}) async-start(bf16[16,16,512]{2,1,0:T(8,128)(2,1)} %get-tuple-element.33), calls=%async_computation.2 | async-start | bytes 524288 | tf_op jit(solution)/shard_map/all_to_all | solution.py:451
  109.6 0.0 copy-done.22
  109.6 0.1 copy.31.refs_2_
  109.7 0.0 copy-done.23
  109.7 0.1 copy.32.refs_3_
  109.8 0.0 copy-done.16
  109.8 1.9 %attend.1 = (bf16[16,512]{1,0:T(8,128)(2,1)}, bf16[2,1,2,128,128]{4,3,2,1,0:T(8,128)(2,1)}) custom-call(s32[1]{0:T(128)} %bitcast.refs_0_.rep_ref, s32[512]{0:T(512)S(1)} %copy-done.10, s32[512]{0:T(512)S(1)} %copy-done.19, s32[16,8]{1,0:T(8,128)S(1)} %copy.30.refs_2_.refs_3_, bf16[16,512]{1,0:T(8,128)(2,1)S(1)} %copy-done.14, ...), custom_call_target="tpu_custom_call" | custom-call | bytes 4194304 | tf_op jit(solution)/shard_map/attend/pallas_call | solution.py:26
  111.7 7.8 %all-to-all-done.2.refs_4_ = bf16[16,16,512]{2,1,0:T(8,128)(2,1)S(1)} async-done(((bf16[16,16,512]{2,1,0:T(8,128)(2,1)}), bf16[16,16,512]{2,1,0:T(8,128)(2,1)S(1)}, u32[]{:S(2)}, u32[]{:S(2)}) %all-to-all-start.2) | async-done | bytes 262176 | tf_op jit(solution)/shard_map/all_to_all | solution.py:451
  119.6 0.0 copy-done.2
  119.6 2.1 %update_state.1 = (bf16[16,512]{1,0:T(8,128)(2,1)}, bf16[16,256]{1,0:T(8,128)(2,1)}) custom-call(s32[1]{0:T(128)} %bitcast.refs_0_.rep_ref, s32[512]{0:T(512)S(1)} %copy-done.10, s32[16,2]{1,0:T(8,128)S(1)} %copy.31.refs_2_, f32[16,2]{1,0:T(8,128)S(1)} %copy.32.refs_3_, bf16[16,16,512]{2,1,0:T(8,128)(2,1)S(1)} %all-to-all-done.2.refs_4_, ...), custom_call_target="tpu_custom_call" | custom-call | bytes 1048576 | tf_op jit(solution)/shard_map/update_state/pallas_call | solution.py:26
  (18 shorter events, 0.0 us)
Async XLA Ops:
  0.6 53.0 %copy-start = (bf16[1,384,4096]{2,1,0:T(8,128)(2,1)S(1)}, bf16[1,384,4096]{2,1,0:T(8,128)(2,1)}, u32[]{:S(2)}) copy-start(bf16[1,384,4096]{2,1,0:T(8,128)(2,1)} %weight_ref.1) | copy-start | bytes 9437188
  2.4 1.0 copy-start.1
  3.4 1.0 copy-start.3
  4.4 0.7 copy-start.8
  6.6 37.4 %all-to-all-start = ((bf16[32,2,16,128]{3,2,1,0:T(8,128)(2,1)}), bf16[32,2,16,128]{3,2,1,0:T(8,128)(2,1)S(1)}, u32[]{:S(2)}, u32[]{:S(2)}) async-start(bf16[32,2,16,128]{3,2,1,0:T(8,128)(2,1)} %pack_leaving.1.refs_1_), calls=%async_computation | async-start | bytes 524288 | tf_op jit(solution)/shard_map/all_to_all | solution.py:381
  24.8 0.7 copy-start.9
  45.0 0.7 copy-start.5
  45.7 54.7 %copy-start.10 = (s32[512]{0:T(512)S(1)}, s32[512]{0:T(512)}, u32[]{:S(2)}) copy-start(s32[512]{0:T(512)} %refs_1_.7) | copy-start | bytes 6148
  45.7 54.7 %copy-start.13 = (bf16[16,512]{1,0:T(8,128)(2,1)S(1)}, bf16[16,512]{1,0:T(8,128)(2,1)}, u32[]{:S(2)}) copy-start(bf16[16,512]{1,0:T(8,128)(2,1)} %refs_4_.3) | copy-start | bytes 49156
  45.7 54.7 %all-to-all-start.1 = ((bf16[32,2,16,128]{3,2,1,0:T(8,128)(2,1)}), bf16[32,2,16,128]{3,2,1,0:T(8,128)(2,1)S(1)}, u32[]{:S(2)}, u32[]{:S(2)}) async-start(bf16[32,2,16,128]{3,2,1,0:T(8,128)(2,1)} %copy-done.5), calls=%async_computation.1 | async-start | bytes 524288 | tf_op jit(solution)/shard_map/all_to_all | solution.py:436
  53.6 0.9 copy-start.7
  54.5 55.3 %copy-start.16 = (bf16[16,128]{1,0:T(8,128)(2,1)S(1)}, bf16[16,128]{1,0:T(8,128)(2,1)}, u32[]{:S(2)}) copy-start(bf16[16,128]{1,0:T(8,128)(2,1)} %refs_5_.5) | copy-start | bytes 12292
  54.5 65.1 %copy-start.11 = (f32[16,512]{1,0:T(8,128)S(1)}, f32[16,512]{1,0:T(8,128)}, u32[]{:S(2)}) copy-start(f32[16,512]{1,0:T(8,128)} %refs_11_.1) | copy-start | bytes 98308
  54.5 65.1 %copy-start.12 = (bf16[16,512]{1,0:T(8,128)(2,1)S(1)}, bf16[16,512]{1,0:T(8,128)(2,1)}, u32[]{:S(2)}) copy-start(bf16[16,512]{1,0:T(8,128)(2,1)} %refs_7_.4) | copy-start | bytes 49156
  56.3 53.3 %copy-start.22 = (s32[16,2]{0,1:T(2,128)S(1)}, s32[16,2]{0,1:T(2,128)}, u32[]{:S(2)}) copy-start(s32[16,2]{0,1:T(2,128)} %param.40) | copy-start | bytes 388
  56.3 53.3 %copy-start.23 = (f32[16,2]{0,1:T(2,128)S(1)}, f32[16,2]{0,1:T(2,128)}, u32[]{:S(2)}) copy-start(f32[16,2]{0,1:T(2,128)} %param.41) | copy-start | bytes 388
  56.4 53.4 %copy-start.4 = (bf16[48,1,2,16,128]{4,3,2,1,0:T(8,128)(2,1)S(1)}, bf16[48,1,2,16,128]{4,3,2,1,0:T(8,128)(2,1)}, u32[]{:S(2)}) copy-start(bf16[48,1,2,16,128]{4,3,2,1,0:T(8,128)(2,1)} %refs_7_.3) | copy-start | bytes 1179652
  56.4 53.4 %copy-start.14 = (bf16[16,512]{1,0:T(8,128)(2,1)S(1)}, bf16[16,512]{1,0:T(8,128)(2,1)}, u32[]{:S(2)}) copy-start(bf16[16,512]{1,0:T(8,128)(2,1)} %refs_4_.4) | copy-start | bytes 49156
  56.4 53.4 %copy-start.17 = (bf16[16,128]{1,0:T(8,128)(2,1)S(1)}, bf16[16,128]{1,0:T(8,128)(2,1)}, u32[]{:S(2)}) copy-start(bf16[16,128]{1,0:T(8,128)(2,1)} %refs_6_.1) | copy-start | bytes 12292
  56.4 53.4 %copy-start.19 = (s32[512]{0:T(512)S(1)}, s32[512]{0:T(512)}, u32[]{:S(2)}) copy-start(s32[512]{0:T(512)} %refs_2_.3) | copy-start | bytes 6148
  56.4 63.2 %copy-start.2 = (f32[16,16,512]{2,1,0:T(8,128)S(1)}, f32[16,16,512]{2,1,0:T(8,128)}, u32[]{:S(2)}) copy-start(f32[16,16,512]{2,1,0:T(8,128)} %refs_8_.1) | copy-start | bytes 1572868
  56.4 63.2 %copy-start.6 = (bf16[256,512]{1,0:T(8,128)(2,1)S(1)}, bf16[256,512]{1,0:T(8,128)(2,1)}, u32[]{:S(2)}) copy-start(bf16[256,512]{1,0:T(8,128)(2,1)} %refs_9_.1) | copy-start | bytes 786436
  56.4 63.2 %copy-start.20 = (f32[512]{0:T(512)S(1)}, f32[512]{0:T(512)}, u32[]{:S(2)}) copy-start(f32[512]{0:T(512)} %param.37) | copy-start | bytes 6148
  56.4 63.2 %copy-start.21 = (f32[512]{0:T(512)S(1)}, f32[512]{0:T(512)}, u32[]{:S(2)}) copy-start(f32[512]{0:T(512)} %param.39) | copy-start | bytes 6148
  56.5 3.9 %collective-permute-start = (bf16[64,4096]{1,0:T(8,128)(2,1)S(1)}, bf16[64,4096]{1,0:T(8,128)(2,1)S(1)}, u32[]{:S(2)}, u32[]{:S(2)}) collective-permute-start(bf16[64,4096]{1,0:T(8,128)(2,1)S(1)} %get-tuple-element.21), channel_id=1, source_target_pairs={{0,16},{16,0},{32,48},{48,32},{64,80},{80,64},{96,112},{112,96},{1... | collective-permute-start | bytes 1572872 | tf_op jit(solution)/shard_map/ppermute | solution.py:415
  60.5 9.5 %collective-permute-start.1 = (bf16[16,4096]{1,0:T(8,128)(2,1)S(1)}, bf16[16,4096]{1,0:T(8,128)(2,1)S(1)}, u32[]{:S(2)}, u32[]{:S(2)}) collective-permute-start(bf16[16,4096]{1,0:T(8,128)(2,1)S(1)} %get-tuple-element.23), channel_id=1, source_target_pairs={{0,64},{16,80},{32,96},{48,112},{64,0},{80,16},{96,32},{112,48},{1... | collective-permute-start | bytes 393224 | tf_op jit(solution)/shard_map/ppermute | solution.py:419
  63.9 7.3 %collective-permute-start.2 = (bf16[16,4096]{1,0:T(8,128)(2,1)S(1)}, bf16[16,4096]{1,0:T(8,128)(2,1)S(1)}, u32[]{:S(2)}, u32[]{:S(2)}) collective-permute-start(bf16[16,4096]{1,0:T(8,128)(2,1)S(1)} %get-tuple-element.24), channel_id=1, source_target_pairs={{0,32},{16,48},{32,64},{48,80},{64,96},{80,112},{96,0},{112,16},{1... | collective-permute-start | bytes 393224 | tf_op jit(solution)/shard_map/ppermute | solution.py:419
  67.9 8.1 %collective-permute-start.3 = (bf16[16,4096]{1,0:T(8,128)(2,1)S(1)}, bf16[16,4096]{1,0:T(8,128)(2,1)S(1)}, u32[]{:S(2)}, u32[]{:S(2)}) collective-permute-start(bf16[16,4096]{1,0:T(8,128)(2,1)S(1)} %get-tuple-element.25), channel_id=1, source_target_pairs={{0,96},{16,112},{32,0},{48,16},{64,32},{80,48},{96,64},{112,80},{1... | collective-permute-start | bytes 393224 | tf_op jit(solution)/shard_map/ppermute | solution.py:419
  76.1 23.1 %collective-permute-start.4 = (bf16[4,4096]{1,0:T(4,128)(2,1)S(1)}, bf16[4,4096]{1,0:T(4,128)(2,1)S(1)}, u32[]{:S(2)}, u32[]{:S(2)}) collective-permute-start(bf16[4,4096]{1,0:T(4,128)(2,1)S(1)} %get-tuple-element.27), channel_id=1, source_target_pairs={{0,256},{16,272},{32,288},{48,304},{64,320},{80,336},{96,352},{112... | collective-permute-start | bytes 98312 | tf_op jit(solution)/shard_map/ppermute | solution.py:424
  88.2 11.0 %collective-permute-start.5 = (bf16[4,4096]{1,0:T(4,128)(2,1)S(1)}, bf16[4,4096]{1,0:T(4,128)(2,1)S(1)}, u32[]{:S(2)}, u32[]{:S(2)}) collective-permute-start(bf16[4,4096]{1,0:T(4,128)(2,1)S(1)} %get-tuple-element.28), channel_id=1, source_target_pairs={{0,128},{16,144},{32,160},{48,176},{64,192},{80,208},{96,224},{112... | collective-permute-start | bytes 98312 | tf_op jit(solution)/shard_map/ppermute | solution.py:424
  90.7 9.7 %collective-permute-start.6 = (bf16[4,4096]{1,0:T(4,128)(2,1)S(1)}, bf16[4,4096]{1,0:T(4,128)(2,1)S(1)}, u32[]{:S(2)}, u32[]{:S(2)}) collective-permute-start(bf16[4,4096]{1,0:T(4,128)(2,1)S(1)} %get-tuple-element.29), channel_id=1, source_target_pairs={{0,384},{16,400},{32,416},{48,432},{64,448},{80,464},{96,480},{112... | collective-permute-start | bytes 98312 | tf_op jit(solution)/shard_map/ppermute | solution.py:424
  100.4 0.7 copy-start.15
  101.1 0.7 copy-start.18
  103.5 16.1 %all-to-all-start.2 = ((bf16[16,16,512]{2,1,0:T(8,128)(2,1)}), bf16[16,16,512]{2,1,0:T(8,128)(2,1)S(1)}, u32[]{:S(2)}, u32[]{:S(2)}) async-start(bf16[16,16,512]{2,1,0:T(8,128)(2,1)} %get-tuple-element.33), calls=%async_computation.2 | async-start | bytes 524288 | tf_op jit(solution)/shard_map/all_to_all | solution.py:451

commit v2 on v1

v2 whole, which is shorter than its diff:
```python
import math

import jax
import jax.numpy as jnp
from jax import lax
from jax.experimental import pallas as pl
from jax.experimental.pallas import tpu as pltpu
from jax.sharding import PartitionSpec as P

MIG = 2
LANES = 128
SUB = 8
F32 = jnp.float32
BF16 = jnp.bfloat16


def _smem():
    return pl.BlockSpec(memory_space=pltpu.SMEM)


def _vmem():
    return pl.BlockSpec(memory_space=pltpu.VMEM)


def _any():
    return pl.BlockSpec(memory_space=pl.ANY)


def _hbm():
    return pl.BlockSpec(memory_space=pltpu.HBM)


def _shape(shape, dtype):
    return jax.ShapeDtypeStruct(shape, dtype)


def _call(body, name, out_shape, ins, outs, args, scratch=(), us=1.0, room=32):
    return pl.pallas_call(
        body,
        name=name,
        out_shape=out_shape,
        in_specs=ins,
        out_specs=outs,
        scratch_shapes=list(scratch),
        compiler_params=pltpu.CompilerParams(vmem_limit_bytes=room * 1024 * 1024),
        cost_estimate=pl.CostEstimate(flops=0, bytes_accessed=int(us * 3.5e6), transcendentals=0),
    )(*args)


def _present(anchor_ref, base, requests):
    mask = jnp.int32(0)
    for g in range(requests):
        a = anchor_ref[base + g] - base
        inside = (a >= 0) & (a < requests)
        mask = mask | jnp.where(inside, jnp.int32(1) << jnp.clip(a, 0, requests - 1), 0)
    return mask


def _slots(rep_ref, anchor_ref, requests):
    base = rep_ref[0] * requests
    count = jnp.int32(0)
    found = []
    for g in range(requests):
        a = anchor_ref[base + g]
        local = a - base
        arrived = (local < 0) | (local >= requests)
        found.append((a, jnp.clip(local, 0, requests - 1), arrived, jnp.minimum(count, MIG - 1)))
        count = count + jnp.where(arrived, 1, 0)
    return found


def _pack_body(
    requests, rep_ref, anchor_ref, table_ref, pool_ref, window_ref, scan_ref, out_ref,
    scans_ref, pages_ref, win_ref, sems,
):
    pages = table_ref.shape[0]
    taps, _, channels = window_ref.shape
    blocks = channels // LANES
    whole = pltpu.make_async_copy(window_ref, win_ref, sems.at[0])
    whole.start()
    base = rep_ref[0] * requests
    mask = _present(anchor_ref, base, requests)
    first, second = jnp.int32(0), jnp.int32(0)
    for o in reversed(range(requests)):
        leaves = ((mask >> o) & 1) == 0
        second = jnp.where(leaves, first, second)
        first = jnp.where(leaves, o, first)
    leaving = (first, second)
    copies = [whole]
    for j, o in enumerate(leaving):
        copies.append(pltpu.make_async_copy(scan_ref.at[o], scans_ref.at[j], sems.at[len(copies)]))
        copies[-1].start()
        for m in range(pages):
            copies.append(
                pltpu.make_async_copy(pool_ref.at[table_ref[m, o], 0], pages_ref.at[j, m], sems.at[len(copies)])
            )
            copies[-1].start()
    for copy in copies:
        copy.wait()
    row = lax.broadcasted_iota(jnp.int32, (requests, channels), 0)
    for j, o in enumerate(leaving):
        scan = scans_ref[j]
        high = scan.astype(BF16).astype(F32)
        rest = scan - high
        middle = rest.astype(BF16).astype(F32)
        low = rest - middle
        tails = []
        for part in (high, middle, low):
            for b in range(blocks):
                for h in range(scan.shape[0] // SUB):
                    tails.append(part[h * SUB : (h + 1) * SUB, b * LANES : (b + 1) * LANES])
        lines = [
            jnp.sum(jnp.where(row == o, win_ref[t].astype(F32), 0.0), axis=0, keepdims=True) for t in range(taps)
        ]
        win = jnp.concatenate([*lines, jnp.zeros((SUB - taps, channels), F32)], axis=0)
        for b in range(blocks):
            tails.append(win[:, b * LANES : (b + 1) * LANES])
        for m in range(pages):
            page = pages_ref[j, m].astype(F32)
            for c in range(2):
                for h in range(2):
                    i = 4 * m + 2 * c + h
                    tail = tails[i] if i < len(tails) else jnp.zeros((SUB, LANES), F32)
                    head = page[c, h * SUB : (h + 1) * SUB, :]
                    out_ref[i, j] = jnp.concatenate([head, tail], axis=0).astype(BF16)


def _route_body(requests, anchor_ref, dep_ref, out_ref):
    anchors = anchor_ref[...]
    replicas = anchors.shape[0]
    home = lax.broadcasted_iota(jnp.int32, anchors.shape, 0)
    place = lax.broadcasted_iota(jnp.int32, anchors.shape, 1).astype(F32)
    source = anchors // requests
    bit = (jnp.int32(1) << (anchors - source * requests)).astype(F32)
    arrived = source != home
    staying = jnp.sum(jnp.where(arrived, 0.0, bit), axis=1, keepdims=True).astype(jnp.int32)
    first = ((~staying) & (staying + 1)).astype(F32)
    lowest = jnp.zeros(anchors.shape, F32)
    for s in range(replicas):
        lowest = jnp.where(source == s, first[s : s + 1], lowest)
    item = (source * MIG).astype(F32) + jnp.where(lowest != bit, 1.0, 0.0)
    early = jnp.min(jnp.where(arrived, place, 99.0), axis=1, keepdims=True)
    one = jnp.sum(jnp.where(arrived & (place == early), item, 0.0), axis=1, keepdims=True)
    two = jnp.sum(jnp.where(arrived & (place != early), item, 0.0), axis=1, keepdims=True)
    lane = lax.broadcasted_iota(jnp.int32, out_ref.shape, 1)
    out_ref[...] = jnp.where(lane == 0, one, jnp.where(lane == 1, two, 0.0)).astype(jnp.int32)


def _own_bits(r):
    c, x = r % 2, (r // 2) % 4
    return (x // 2) * 4 + ((x // 2) ^ (x % 2)) * 2 + c


def _expert_body(rep_ref, hidden_ref, weight_ref, dep_ref, keep_ref, send_ref):
    width = weight_ref.shape[2] // 8
    own = _own_bits(rep_ref[0])
    hidden = hidden_ref[0]
    for p in (4, 5, 6, 7, 0, 1, 2, 3):
        block = own ^ ((p % 2) * 4 + (p // 2 % 2) * 2 + p // 4)
        columns = pl.ds(pl.multiple_of(block * width, width), width)
        total = jnp.dot(hidden, weight_ref[0, :, columns], preferred_element_type=F32)
        at = slice(p % 4 * width, (p % 4 + 1) * width)
        if p < 4:
            keep_ref[:, at] = total
        else:
            send_ref[:, at] = total.astype(BF16)


def _fold_body(keep_ref, got_ref, next_ref, send_ref):
    half = next_ref.shape[1]
    next_ref[...] = keep_ref[:, :half] + got_ref[:, :half].astype(F32)
    send_ref[...] = (keep_ref[:, half:] + got_ref[:, half:].astype(F32)).astype(BF16)


def _select_body(index_ref, in_ref, keep_ref, got_ref, out_ref):
    replicas = out_ref.shape[0]
    cap = keep_ref.shape[0] // replicas
    blocks = keep_ref.shape[1] // LANES
    for d in range(replicas):
        for j in range(MIG):
            i = index_ref[d, j]
            out_ref[d, j] = in_ref[i // MIG, i % MIG]
    total = keep_ref[...] + got_ref[...].astype(F32)
    for d in range(replicas):
        rows = total[d * cap : (d + 1) * cap]
        out_ref[d, MIG] = jnp.concatenate(
            [rows[:, b * LANES : (b + 1) * LANES] for b in range(blocks)], axis=0
        ).astype(BF16)


def _local_body(
    requests, rep_ref, anchor_ref, window_ref, conv_ref, taps_ref, bias_ref, mix_ref, dep_ref,
    base_ref, which_ref, taps_out_ref, mix_out_ref,
):
    taps = window_ref.shape[0]
    weights = taps_ref[...]
    row = lax.broadcasted_iota(jnp.int32, (requests, requests), 0)
    col = lax.broadcasted_iota(jnp.int32, (requests, requests), 1)
    row_w = lax.broadcasted_iota(jnp.int32, which_ref.shape, 0)
    col_w = lax.broadcasted_iota(jnp.int32, which_ref.shape, 1)
    pick = jnp.zeros((requests, requests), F32)
    which = jnp.zeros(which_ref.shape, F32)
    for g, (_, local, arrived, order) in enumerate(_slots(rep_ref, anchor_ref, requests)):
        pick = jnp.where((row == g) & (col == local) & ~arrived, 1.0, pick)
        which = jnp.where((row_w == g) & (col_w == order) & arrived, 1.0, which)
    pick = pick.astype(BF16)
    mixed = conv_ref[...].astype(F32) * weights[taps : taps + 1] + bias_ref[...]
    for t in range(taps):
        mixed = mixed + jnp.dot(pick, window_ref[t], preferred_element_type=F32) * weights[t : t + 1]
    base_ref[...] = mixed
    which_ref[...] = which
    taps_out_ref[...] = weights
    mix_out_ref[...] = mix_ref[...]


def _act_body(moved_ref, base_ref, which_ref, taps_ref, mix_ref, out_ref, act_ref, win_ref):
    requests, channels = base_ref.shape
    blocks = channels // LANES
    first = 3 * blocks * 2
    weights = taps_ref[...]
    taps = weights.shape[0] - 1
    mixed = base_ref[...]
    for j in range(MIG):
        for b in range(blocks):
            win_ref[:, b * LANES : (b + 1) * LANES] = moved_ref[first + b, j].astype(F32)[SUB : 2 * SUB]
        line = jnp.sum(win_ref[0:taps, :] * weights[0:taps], axis=0, keepdims=True)
        mixed = mixed + which_ref[:, j : j + 1] * line
    act = mixed * (1.0 / (1.0 + jnp.exp(-mixed)))
    act_ref[...] = act
    turn = (((1,), (1,)), ((), ()))
    partial = lax.dot_general(act.astype(BF16), mix_ref[...], turn, preferred_element_type=F32)
    rank = 2 * LANES
    high = partial.astype(BF16).astype(F32)
    low = (partial - high)[:, rank:]
    fill = jnp.zeros((requests, LANES - 2 * low.shape[1]), F32)
    packed = jnp.concatenate([high[:, :rank], high[:, rank:], low, fill], axis=1)
    experts = out_ref.shape[0]
    replicas = moved_ref.shape[0]
    sums = {}
    for r in range(8):
        total = moved_ref[r, MIG].astype(F32)
        for z in range(1, replicas // 8):
            total = total + moved_ref[z * 8 + r, MIG].astype(F32)
        sums[_own_bits(r)] = total
    empty = jnp.zeros((requests - SUB, LANES), F32)
    for e in range(experts):
        block = sums[e // 2][e % 2 * SUB : (e % 2 + 1) * SUB]
        block = jnp.concatenate([block, empty], axis=0)
        out_ref[e] = jnp.concatenate([packed, block], axis=1).astype(BF16)


def _ready_body(
    requests, states, rep_ref, anchor_ref, routes_ref, share_ref, moved_ref, act_ref, gate_ref, scan_ref, step_ref,
    bias_ref, decay_ref, skip_ref, old_ref, rate_ref, gate_out_ref, skip_out_ref, step_out_ref, bias_out_ref,
    share_out_ref, arr_ref, count_ref,
):
    channels = act_ref.shape[1]
    blocks = channels // LANES
    halves = states // SUB
    n = blocks * halves
    for j in range(MIG):
        for b in range(blocks):
            for h in range(halves):
                i = b * halves + h
                high = moved_ref[i, j].astype(F32)[SUB : 2 * SUB]
                middle = moved_ref[n + i, j].astype(F32)[SUB : 2 * SUB]
                lowest = moved_ref[2 * n + i, j].astype(F32)[SUB : 2 * SUB]
                arr_ref[j, h * SUB : (h + 1) * SUB, b * LANES : (b + 1) * LANES] = high + (middle + lowest)
    for g, (_, local, arrived, order) in enumerate(_slots(rep_ref, anchor_ref, requests)):
        old_ref[g] = jnp.where(arrived, arr_ref[order], scan_ref[local])
    rate_ref[...] = -jnp.exp(decay_ref[...])
    gate = gate_ref[...].astype(F32)
    gate_out_ref[...] = gate * (1.0 / (1.0 + jnp.exp(-gate)))
    skip_out_ref[...] = skip_ref[...] * act_ref[...]
    step_out_ref[...] = step_ref[...]
    bias_out_ref[...] = jnp.broadcast_to(bias_ref[...], bias_out_ref.shape)
    for e in range(count_ref.shape[0]):
        count_ref[e] = 0
    row = lax.broadcasted_iota(jnp.int32, (requests, LANES), 0)
    col = lax.broadcasted_iota(jnp.int32, (requests, LANES), 1)
    share = jnp.zeros((requests, LANES), F32)
    for t in range(requests):
        for k in range(routes_ref.shape[0]):
            e = routes_ref[k, t]
            place = count_ref[e]
            count_ref[e] = place + 1
            share = share + jnp.where((row == t) & (col == e * SUB + place), share_ref[k, t], 0.0)
    share_out_ref[...] = share


def _final_body(
    states, sums_ref, act_ref, old_ref, rate_ref, gate_ref, skip_ref, step_ref, bias_ref, share_ref,
    gated_ref, mix_ref, y_ref,
):
    experts, requests, _ = sums_ref.shape
    rank = 2 * LANES
    projected = sums_ref[0, :, 0 : rank + LANES].astype(F32)
    for e in range(1, experts):
        projected = projected + sums_ref[e, :, 0 : rank + LANES].astype(F32)
    step = jnp.dot(projected[:, :rank].astype(BF16), step_ref[...], preferred_element_type=F32) + bias_ref[0:1]
    step = jnp.maximum(step, 0.0) + jnp.log1p(jnp.exp(-jnp.abs(step)))
    tail = projected[:, rank:]
    columns = jnp.transpose(tail + pltpu.roll(tail, LANES - 2 * states, 1))
    rest = share_ref[...]
    parts = []
    for _ in range(3):
        part = rest.astype(BF16).astype(F32)
        parts.append(part)
        rest = rest - part
    outs = sums_ref[:, :, rank + LANES :].astype(F32)[:, 0:SUB].reshape(experts * SUB, LANES).astype(BF16)
    both = jnp.concatenate([*parts, *(pltpu.roll(p, SUB // 2, 1) for p in parts)], axis=0).astype(BF16)
    terms = jnp.dot(both, outs, preferred_element_type=F32)
    halves = [
        sum(terms[(3 * h + i) * requests : (3 * h + i + 1) * requests] for i in reversed(range(3))) for h in range(2)
    ]
    mix_ref[...] = jnp.concatenate(halves, axis=1).astype(BF16)
    rate = rate_ref[...]
    flow = step * act_ref[...]
    for g in range(requests):
        inflow = columns[0:states, g : g + 1]
        readout = columns[states : 2 * states, g : g + 1]
        state = jnp.exp(step[g : g + 1] * rate) * old_ref[g] + inflow * flow[g : g + 1]
        y_ref[g : g + 1, :] = jnp.sum(readout * state, axis=0, keepdims=True)
    gated_ref[...] = ((y_ref[...] + skip_ref[...]) * gate_ref[...]).astype(BF16)


def _attend_body(
    requests, rep_ref, anchor_ref, len_ref, table_ref, query_ref, key_ref, value_ref, pool_ref, moved_ref, dep_ref,
    out_ref, pages_ref, keys_ref, values_ref,
):
    turn = (((1,), (1,)), ((), ()))
    head = key_ref.shape[1]
    heads = query_ref.shape[1] // head
    pool, _, _, page, _ = pool_ref.shape
    table = table_ref[...].astype(F32).astype(BF16)
    pages = table.shape[0]
    span = pages * page
    slots = _slots(rep_ref, anchor_ref, requests)
    row1 = lax.broadcasted_iota(jnp.int32, (requests, 1), 0)
    row = lax.broadcasted_iota(jnp.int32, (requests, requests), 0)
    col = lax.broadcasted_iota(jnp.int32, (requests, requests), 1)
    live = jnp.zeros((requests, 1), jnp.int32)
    order = jnp.full((requests, 1), -1, jnp.int32)
    pick = jnp.zeros((requests, requests), F32)
    live_of = [jnp.int32(0)] * MIG
    for g, (a, local, arrived, place) in enumerate(slots):
        length = len_ref[a]
        live = jnp.where(row1 == g, length, live)
        order = jnp.where((row1 == g) & arrived, place, order)
        pick = jnp.where((row == g) & (col == local), 1.0, pick)
        live_of = [jnp.where(arrived & (place == j), length, live_of[j]) for j in range(MIG)]
    mine = lax.dot_general(pick.astype(BF16), table, turn, preferred_element_type=F32).astype(jnp.int32)
    here = jnp.where(order < 0, live, 0)
    at = lax.broadcasted_iota(jnp.int32, (requests, pool * page), 1)
    which, token = at // page, at % page
    seen = jnp.zeros((requests, pool * page), jnp.bool_)
    for m in range(pages):
        seen = seen | ((mine[:, m : m + 1] == which) & (token + m * page < here))
    at = lax.broadcasted_iota(jnp.int32, (requests, MIG * span), 1)
    seen_moved = (at // span == order) & (at % span < live)
    down = lax.broadcasted_iota(jnp.int32, (span, head), 0)
    for j in range(MIG):
        for m in range(pages):
            for h in range(2):
                for c, ref in ((0, keys_ref), (1, values_ref)):
                    start = j * span + m * page + h * SUB
                    ref[start : start + SUB, :] = moved_ref[4 * m + 2 * c + h, j].astype(F32)[0:SUB]
        for c, ref in ((0, keys_ref), (1, values_ref)):
            block = ref[j * span : (j + 1) * span, :]
            pages_ref[j, 0, c] = jnp.where(down < live_of[j], block, 0.0).astype(BF16)
    moved_keys = keys_ref[...].astype(BF16)
    moved_values = values_ref[...].astype(BF16)
    pool_keys = pool_ref[:, 0, 0].reshape(pool * page, head)
    pool_values = pool_ref[:, 0, 1].reshape(pool * page, head)
    query = query_ref[...]
    queries = jnp.concatenate([query[:, h * head : (h + 1) * head] for h in range(heads)], axis=0)
    scale = 1.0 / math.sqrt(head)
    scores = lax.dot_general(queries, pool_keys, turn, preferred_element_type=F32) * scale
    scores_moved = lax.dot_general(queries, moved_keys, turn, preferred_element_type=F32) * scale
    new_key = jnp.concatenate([key_ref[...].astype(F32)] * heads, axis=0)
    new_value = jnp.concatenate([value_ref[...].astype(F32)] * heads, axis=0)
    own = jnp.sum(queries.astype(F32) * new_key, axis=1, keepdims=True) * scale
    far = F32(-1e30)
    seen = jnp.concatenate([jnp.where(seen, 1.0, 0.0)] * heads, axis=0) > 0.5
    seen_moved = jnp.concatenate([jnp.where(seen_moved, 1.0, 0.0)] * heads, axis=0) > 0.5
    scores = jnp.where(seen, scores, far)
    scores_moved = jnp.where(seen_moved, scores_moved, far)
    highest = jnp.maximum(
        jnp.maximum(jnp.max(scores, axis=1, keepdims=True), jnp.max(scores_moved, axis=1, keepdims=True)), own
    )
    e_pool = jnp.exp(scores - highest)
    e_moved = jnp.exp(scores_moved - highest)
    e_own = jnp.exp(own - highest)
    total = jnp.sum(e_pool, axis=1, keepdims=True) + jnp.sum(e_moved, axis=1, keepdims=True) + e_own
    w_pool = (e_pool / total).astype(BF16)
    w_moved = (e_moved / total).astype(BF16)
    w_own = (e_own / total).astype(BF16).astype(F32)
    context = jnp.dot(w_pool, pool_values, preferred_element_type=F32)
    context = context + jnp.dot(w_moved, moved_values, preferred_element_type=F32) + w_own * new_value
    for h in range(heads):
        out_ref[:, h * head : (h + 1) * head] = context[h * requests : (h + 1) * requests].astype(BF16)


def per_device(
    query,
    new_key,
    new_value,
    page_pool,
    block_table,
    lengths,
    anchor,
    conv_input,
    gate_input,
    window_state,
    scan_state,
    filter_taps,
    filter_bias,
    mix_weight,
    step_weight,
    step_bias,
    log_decay,
    skip_gain,
    routes,
    route_weight,
    expert_hidden,
    down_weight,
):
    requests, channels = query.shape
    replicas = lax.axis_size("rep")
    experts = lax.axis_size("exp")
    rep = lax.axis_index("rep").astype(jnp.int32).reshape(1)
    states = log_decay.shape[0]
    head = new_key.shape[1]
    pages, page = block_table.shape[1], page_pool.shape[3]
    slots = expert_hidden.shape[1]
    features = down_weight.shape[2]
    table = block_table.T
    window = jnp.transpose(window_state, (1, 0, 2))

    def piece(tiles):
        return _shape((replicas, tiles, 2 * SUB, LANES), BF16)

    packed = _call(
        lambda *refs: _pack_body(requests, *refs),
        "pack_leaving",
        piece(MIG),
        [_smem()] * 3 + [_hbm()] * 3,
        _vmem(),
        (rep, anchor, table, page_pool, window, scan_state),
        scratch=[
            pltpu.VMEM((MIG, states, channels), F32),
            pltpu.VMEM((MIG, pages, 2, page, head), BF16),
            pltpu.VMEM(window.shape, BF16),
            pltpu.SemaphoreType.DMA((1 + MIG * (1 + pages),)),
        ],
        us=1.5,
        room=60,
    )
    spread = lax.all_to_all(packed, "rep", split_axis=0, concat_axis=0, tiled=True)

    keep, send = _call(
        _expert_body,
        "expert_terms",
        [_shape((slots, features // 2), F32), _shape((slots, features // 2), BF16)],
        [_smem()] + [_vmem()] * 2 + [_any()],
        [_vmem()] * 2,
        (rep, expert_hidden, down_weight, packed),
        us=2,
    )

    def at(z, x, c):
        return (z * 4 + x) * 2 + c

    every = [(z, x, c) for z in range(4) for x in range(4) for c in range(2)]
    got = lax.ppermute(send, "rep", [(at(z, x, c), at(z, x, 1 - c)) for z, x, c in every])
    for part, partner in ((4, (1, 0, 3, 2)), (8, (3, 2, 1, 0))):
        keep, send = _call(
            _fold_body,
            "fold",
            [_shape((slots, features // part), F32), _shape((slots, features // part), BF16)],
            [_vmem()] * 2,
            [_vmem()] * 2,
            (keep, got),
            us=0.5,
        )
        got = lax.ppermute(send, "rep", [(at(z, x, c), at(z, partner[x], c)) for z, x, c in every])

    index = _call(
        lambda *refs: _route_body(requests, *refs),
        "route_pieces",
        _shape((replicas, LANES), jnp.int32),
        [_vmem(), _any()],
        _vmem(),
        (anchor.reshape(replicas, requests), packed),
        us=1,
    )
    onward = _call(
        _select_body,
        "select_pieces",
        piece(MIG + 1),
        [_smem()] + [_vmem()] * 3,
        _vmem(),
        (index, spread, keep, got),
        us=1,
    )
    moved = lax.all_to_all(onward, "rep", split_axis=0, concat_axis=0, tiled=True)

    base, which, taps, mix = _call(
        lambda *refs: _local_body(requests, *refs),
        "filter_local",
        [
            _shape((requests, channels), F32),
            _shape((requests, LANES), F32),
            _shape(filter_taps.shape, F32),
            _shape(mix_weight.shape[::-1], BF16),
        ],
        [_smem()] * 2 + [_vmem()] * 5 + [_any()],
        [_vmem()] * 4,
        (rep, anchor, window, conv_input, filter_taps, filter_bias.reshape(1, channels), mix_weight.T, onward),
        us=1.5,
    )
    sums, act = _call(
        _act_body,
        "filter_and_project",
        [_shape((experts, requests, 4 * LANES), BF16), _shape((requests, channels), F32)],
        [_vmem()] * 5,
        [_vmem()] * 2,
        (moved, base, which, taps, mix),
        scratch=[pltpu.VMEM((SUB, channels), F32)],
        us=1.5,
    )
    sums_all = lax.all_to_all(sums, "exp", split_axis=0, concat_axis=0, tiled=True)

    attended, pages_out = _call(
        lambda *refs: _attend_body(requests, *refs),
        "attend",
        [_shape((requests, channels), BF16), _shape((MIG, 1, 2, pages * page, head), BF16)],
        [_smem()] * 3 + [_vmem()] * 6 + [_any()],
        [_vmem()] * 2,
        (rep, anchor, lengths, table, query, new_key, new_value, page_pool, moved, act),
        scratch=[pltpu.VMEM((MIG * pages * page, head), F32)] * 2,
        us=2,
    )
    ready = _call(
        lambda *refs: _ready_body(requests, states, *refs),
        "ready_state",
        [
            _shape((requests, states, channels), F32),
            _shape((states, channels), F32),
            _shape((requests, channels), F32),
            _shape((requests, channels), F32),
            _shape(step_weight.shape, BF16),
            _shape((SUB, channels), F32),
            _shape((requests, LANES), F32),
        ],
        [_smem()] * 4 + [_vmem()] * 8,
        [_vmem()] * 7,
        (
            rep, anchor, routes.T, route_weight.T, moved, act, gate_input, scan_state, step_weight,
            step_bias.reshape(1, channels), log_decay, skip_gain.reshape(1, channels),
        ),
        scratch=[pltpu.VMEM((MIG, states, channels), F32), pltpu.SMEM((experts,), jnp.int32)],
        us=2,
    )
    gated, mixed = _call(
        lambda *refs: _final_body(states, *refs),
        "update_state",
        [_shape((requests, channels), BF16), _shape((requests, features // experts), BF16)],
        [_vmem()] * 9,
        [_vmem()] * 2,
        (sums_all, act, *ready),
        scratch=[pltpu.VMEM((requests, channels), F32)],
        us=2,
    )
    return (attended, pages_out, gated, mixed)


def solution(mesh):
    placed = (
        P("rep", "exp"),
        P("rep", "exp"),
        P("rep", "exp"),
        P("rep", "exp", None, None, None),
        P("rep", None),
        P(),
        P(),
        P("rep", "exp"),
        P("rep", "exp"),
        P("rep", None, "exp"),
        P("rep", None, "exp"),
        P(None, "exp"),
        P("exp"),
        P("exp", None),
        P(None, "exp"),
        P("exp"),
        P(None, "exp"),
        P("exp"),
        P("rep", None),
        P("rep", None),
        P("exp", None, "rep"),
        P("exp", "rep", None),
    )
    return jax.shard_map(
        per_device,
        mesh=mesh,
        in_specs=placed,
        out_specs=(
            P("rep", "exp"),
            P("rep", "exp", None, None, None),
            P("rep", "exp"),
            P("rep", "exp"),
        ),
        check_vma=False,
    )
```

time: 123 us -> 114 us (0.927)
  the two profiles are of different devices: /device:TPU:6 before, /device:TPU:1 now
where the time goes in v2:
time: 114 us; the launch traced here: 113 us
  starting transfers between devices  56 us (49%)
  waiting for transfers between devices  40.9 us (36%)
  Pallas kernels  11.4 us (10%)
  local copies, waits for them, and re-layouts  3.95 us (3%)
    all_to_all x1, waiting for transfers between devices, per_device(): lax.all_to_all(onward, 'rep', split_axis=0, concat_axis=0, tiled=True)  22.8 us
    all_to_all x1, starting transfers between devices, per_device(): lax.all_to_all(packed, 'rep', split_axis=0, concat_axis=0, tiled=True)  19.4 us
    all_to_all x1, starting transfers between devices, per_device(): lax.all_to_all(onward, 'rep', split_axis=0, concat_axis=0, tiled=True)  15.6 us
    pallas_call x11, Pallas kernels, _call(): pl.pallas_call(body, name=name, out_shape=out_shape, in_specs=ins, out_sp...  11.4 us
    all_to_all x1, starting transfers between devices, per_device(): lax.all_to_all(sums, 'exp', split_axis=0, concat_axis=0, tiled=True)  10.9 us
    ppermute x2, waiting for transfers between devices, per_device(): lax.ppermute(send, 'rep', [(at(z, x, c), at(z, partner[x], c)) for z, x,...  8.93 us
    ppermute x2, starting transfers between devices, per_device(): lax.ppermute(send, 'rep', [(at(z, x, c), at(z, partner[x], c)) for z, x,...  7.93 us
    all_to_all x1, waiting for transfers between devices, per_device(): lax.all_to_all(sums, 'exp', split_axis=0, concat_axis=0, tiled=True)  7.5 us
  transfers between devices with their start and end apart: 6, of which 5 were waited for; matrix products, arithmetic and copies ran while one was open for 0% of the time, Pallas kernels for 4%

profile of v2, /device:TPU:1, one launch (start us, length us, event | category | flops | bytes accessed | tf_op | source)
XLA Modules:
  0.0 113.2 jit_solution(8024472030311792882)
XLA Ops:
  0.6 2.7 %pack_leaving.1.refs_1_.dep_ref = bf16[32,2,16,128]{3,2,1,0:T(8,128)(2,1)} custom-call(s32[1]{0:T(128)} %bitcast.refs_0_.rep_ref, s32[512]{0:T(512)} %refs_1_.7, s32[8,16]{1,0:T(8,128)} %bitcast.12, bf16[48,1,2,16,128]{4,3,2,1,0:T(8,128)(2,1)} %refs_7_.2, bf16[3,16,512]{2,1,0:T(8,128)(2,1)} %bitcast.10, f32[16,16,512]{2,1,0:T(8,128)} %refs_7_.3), custom_call_target="tpu_custom_call" | custom-call | bytes 5250000 | tf_op jit(solution)/shard_map/pack_leaving/pallas_call | solution.py:38
  3.4 0.0 copy-start.9
  3.4 0.0 copy-start.1
  3.4 19.4 %all-to-all-start = ((bf16[32,2,16,128]{3,2,1,0:T(8,128)(2,1)}), bf16[32,2,16,128]{3,2,1,0:T(8,128)(2,1)S(1)}, u32[]{:S(2)}, u32[]{:S(2)}) async-start(bf16[32,2,16,128]{3,2,1,0:T(8,128)(2,1)} %pack_leaving.1.refs_1_.dep_ref), calls=%async_computation | async-start | bytes 524288 | tf_op jit(solution)/shard_map/all_to_all | solution.py:459
  22.7 0.0 copy-start
  22.8 1.0 copy-done
  23.7 1.9 %copy-done.2 = bf16[1,384,4096]{2,1,0:T(8,128)(2,1)S(1)} copy-done((bf16[1,384,4096]{2,1,0:T(8,128)(2,1)S(1)}, bf16[1,384,4096]{2,1,0:T(8,128)(2,1)}, u32[]{:S(2)}) %copy-start.2) | copy-done | bytes 3145752
  25.6 0.9 copy-done.8
  26.5 0.7 expert_terms.1
  27.2 0.0 copy-start.5
  27.2 0.0 copy-start.7
  27.2 0.0 copy-start.14
  27.3 0.0 copy-start.15
  27.3 0.0 copy-start.18
  27.3 2.3 %collective-permute-start = (bf16[128,2048]{1,0:T(8,128)(2,1)S(1)}, bf16[128,2048]{1,0:T(8,128)(2,1)S(1)}, u32[]{:S(2)}, u32[]{:S(2)}) collective-permute-start(bf16[128,2048]{1,0:T(8,128)(2,1)S(1)} %get-tuple-element.28), channel_id=1, source_target_pairs={{0,16},{16,0},{32,48},{48,32},{64,80},{80,64},{96,112},{112,96},{1... | collective-permute-start | bytes 1572872 | tf_op jit(solution)/shard_map/ppermute | solution.py:475
  29.6 1.7 %collective-permute-done.got_ref = bf16[128,2048]{1,0:T(8,128)(2,1)S(1)} collective-permute-done((bf16[128,2048]{1,0:T(8,128)(2,1)S(1)}, bf16[128,2048]{1,0:T(8,128)(2,1)S(1)}, u32[]{:S(2)}, u32[]{:S(2)}) %collective-permute-start) | collective-permute-done | bytes 524320 | tf_op jit(solution)/shard_map/ppermute | solution.py:475
  31.2 0.0 copy-start.17
  31.2 0.0 copy-start.19
  31.3 0.1 fold.2
  31.4 0.0 copy-start.3
  31.4 0.0 copy-start.6
  31.4 0.0 copy-start.10
  31.4 0.0 copy-start.11
  31.4 0.0 copy-start.20
  31.4 0.0 copy-start.21
  31.4 0.0 copy-start.22
  31.4 0.0 copy-start.23
  31.4 3.4 %collective-permute-start.1 = (bf16[128,1024]{1,0:T(8,128)(2,1)S(1)}, bf16[128,1024]{1,0:T(8,128)(2,1)S(1)}, u32[]{:S(2)}, u32[]{:S(2)}) collective-permute-start(bf16[128,1024]{1,0:T(8,128)(2,1)S(1)} %get-tuple-element.30), channel_id=1, source_target_pairs={{0,32},{16,48},{32,0},{48,16},{64,96},{80,112},{96,64},{112,80},{1... | collective-permute-start | bytes 786440 | tf_op jit(solution)/shard_map/ppermute | solution.py:486
  34.9 6.8 %collective-permute-done.1.got_ref = bf16[128,1024]{1,0:T(8,128)(2,1)S(1)} collective-permute-done((bf16[128,1024]{1,0:T(8,128)(2,1)S(1)}, bf16[128,1024]{1,0:T(8,128)(2,1)S(1)}, u32[]{:S(2)}, u32[]{:S(2)}) %collective-permute-start.1) | collective-permute-done | bytes 262176 | tf_op jit(solution)/shard_map/ppermute | solution.py:486
  41.8 4.5 %collective-permute-start.2 = (bf16[128,512]{1,0:T(8,128)(2,1)S(1)}, bf16[128,512]{1,0:T(8,128)(2,1)S(1)}, u32[]{:S(2)}, u32[]{:S(2)}) collective-permute-start(bf16[128,512]{1,0:T(8,128)(2,1)S(1)} %get-tuple-element.32), channel_id=1, source_target_pairs={{0,96},{16,112},{32,64},{48,80},{64,32},{80,48},{96,0},{112,16},{1... | collective-permute-start | bytes 393224 | tf_op jit(solution)/shard_map/ppermute | solution.py:486
  46.3 0.0 copy-done.9
  46.3 0.1 reshape.24.refs_0_
  46.4 0.0 copy-done.1
  46.4 0.2 route_pieces.1.index_ref
  46.6 2.1 %collective-permute-done.2.got_ref = bf16[128,512]{1,0:T(8,128)(2,1)S(1)} collective-permute-done((bf16[128,512]{1,0:T(8,128)(2,1)S(1)}, bf16[128,512]{1,0:T(8,128)(2,1)S(1)}, u32[]{:S(2)}, u32[]{:S(2)}) %collective-permute-start.2) | collective-permute-done | bytes 131104 | tf_op jit(solution)/shard_map/ppermute | solution.py:486
  48.7 0.0 all-to-all-done.in_ref
  48.7 2.0 %select_pieces.1.refs_7_ = bf16[32,3,16,128]{3,2,1,0:T(8,128)(2,1)} custom-call(s32[32,128]{1,0:T(8,128)S(1)} %route_pieces.1.index_ref, bf16[32,2,16,128]{3,2,1,0:T(8,128)(2,1)S(1)} %all-to-all-done.in_ref, f32[128,512]{1,0:T(8,128)S(1)} %get-tuple-element.31.keep_ref, bf16[128,512]{1,0:T(8,128)(2,1)S(1)} %collective-permute-done.2.got_ref), custom_call_target="tpu_custom_call" | custom-call | bytes 3500000 | tf_op jit(solution)/shard_map/select_pieces/pallas_call | solution.py:38
  50.7 15.6 %all-to-all-start.1 = ((bf16[32,3,16,128]{3,2,1,0:T(8,128)(2,1)}), bf16[32,3,16,128]{3,2,1,0:T(8,128)(2,1)S(1)}, u32[]{:S(2)}, u32[]{:S(2)}) async-start(bf16[32,3,16,128]{3,2,1,0:T(8,128)(2,1)} %select_pieces.1.refs_7_), calls=%async_computation.1 | async-start | bytes 786432 | tf_op jit(solution)/shard_map/all_to_all | solution.py:506
  66.3 0.0 copy-done.5
  66.3 0.0 copy-done.7
  66.3 0.0 copy-done.14
  66.3 0.0 copy-done.15
  66.3 0.0 copy-done.18
  66.3 0.8 filter_local.1
  67.1 22.8 %all-to-all-done.1.moved_ref.refs_8_.refs_4_ = bf16[32,3,16,128]{3,2,1,0:T(8,128)(2,1)S(1)} async-done(((bf16[32,3,16,128]{3,2,1,0:T(8,128)(2,1)}), bf16[32,3,16,128]{3,2,1,0:T(8,128)(2,1)S(1)}, u32[]{:S(2)}, u32[]{:S(2)}) %all-to-all-start.1) | async-done | bytes 393248 | tf_op jit(solution)/shard_map/all_to_all | solution.py:506
  89.9 1.0 filter_and_project.1
  90.9 10.9 %all-to-all-start.2 = ((bf16[16,16,512]{2,1,0:T(8,128)(2,1)}), bf16[16,16,512]{2,1,0:T(8,128)(2,1)S(1)}, u32[]{:S(2)}, u32[]{:S(2)}) async-start(bf16[16,16,512]{2,1,0:T(8,128)(2,1)} %get-tuple-element.40), calls=%async_computation.2 | async-start | bytes 524288 | tf_op jit(solution)/shard_map/all_to_all | solution.py:532
  101.8 0.0 copy-done.4
  101.8 0.0 copy-done.12
  101.8 0.0 copy-done.13
  101.8 0.0 copy-done.16
  101.8 0.0 copy-done.17
  101.8 0.0 copy-done.19
  101.8 1.9 %attend.1 = (bf16[16,512]{1,0:T(8,128)(2,1)}, bf16[2,1,2,128,128]{4,3,2,1,0:T(8,128)(2,1)}) custom-call(s32[1]{0:T(128)} %bitcast.refs_0_.rep_ref, s32[512]{0:T(512)S(1)} %copy-done.9, s32[512]{0:T(512)S(1)} %copy-done.19, s32[8,16]{1,0:T(8,128)S(1)} %bitcast.13, bf16[16,512]{1,0:T(8,128)(2,1)S(1)} %copy-done.13, bf16[16,128]{1,0:T(8,128)(2,1)S(1)} %copy-done.16, ...), custom_call_target="tpu_custom_call" | custom-call | bytes 7000000 | tf_op jit(solution)/shard_map/attend/pallas_call | solution.py:38
  103.8 0.0 copy-done.3
  103.8 0.0 copy-done.6
  103.8 0.0 copy-done.11
  103.8 0.0 copy-done.20
  103.8 0.0 copy-done.21
  103.8 0.0 copy-done.22
  103.8 0.0 copy-done.23
  103.8 0.9 ready_state.1
  104.7 7.5 %all-to-all-done.2.refs_0_ = bf16[16,16,512]{2,1,0:T(8,128)(2,1)S(1)} async-done(((bf16[16,16,512]{2,1,0:T(8,128)(2,1)}), bf16[16,16,512]{2,1,0:T(8,128)(2,1)S(1)}, u32[]{:S(2)}, u32[]{:S(2)}) %all-to-all-start.2) | async-done | bytes 262176 | tf_op jit(solution)/shard_map/all_to_all | solution.py:532
  112.2 1.1 update_state.1
  (8 shorter events, 0.1 us)
Async XLA Ops:
  3.4 42.9 %copy-start.9 = (s32[512]{0:T(512)S(1)}, s32[512]{0:T(512)}, u32[]{:S(2)}) copy-start(s32[512]{0:T(512)} %refs_1_.7) | copy-start | bytes 6148
  3.4 43.0 %copy-start.1 = (bf16[32,2,16,128]{3,2,1,0:T(8,128)(2,1)S(1)}, bf16[32,2,16,128]{3,2,1,0:T(8,128)(2,1)}, u32[]{:S(2)}) copy-start(bf16[32,2,16,128]{3,2,1,0:T(8,128)(2,1)} %pack_leaving.1.refs_1_.dep_ref) | copy-start | bytes 786436
  3.4 45.3 %all-to-all-start = ((bf16[32,2,16,128]{3,2,1,0:T(8,128)(2,1)}), bf16[32,2,16,128]{3,2,1,0:T(8,128)(2,1)S(1)}, u32[]{:S(2)}, u32[]{:S(2)}) async-start(bf16[32,2,16,128]{3,2,1,0:T(8,128)(2,1)} %pack_leaving.1.refs_1_.dep_ref), calls=%async_computation | async-start | bytes 524288 | tf_op jit(solution)/shard_map/all_to_all | solution.py:459
  22.7 1.0 copy-start
  23.7 1.9 %copy-start.2 = (bf16[1,384,4096]{2,1,0:T(8,128)(2,1)S(1)}, bf16[1,384,4096]{2,1,0:T(8,128)(2,1)}, u32[]{:S(2)}) copy-start(bf16[1,384,4096]{2,1,0:T(8,128)(2,1)} %weight_ref.1) | copy-start | bytes 9437188
  25.6 0.9 copy-start.8
  27.2 39.0 %copy-start.5 = (bf16[512,288]{0,1:T(8,128)(2,1)S(1)}, bf16[512,288]{0,1:T(8,128)(2,1)}, u32[]{:S(2)}) copy-start(bf16[512,288]{0,1:T(8,128)(2,1)} %param.35) | copy-start | bytes 884740
  27.2 39.0 %copy-start.7 = (bf16[16,3,512]{2,0,1:T(8,128)(2,1)S(1)}, bf16[16,3,512]{2,0,1:T(8,128)(2,1)}, u32[]{:S(2)}) copy-start(bf16[16,3,512]{2,0,1:T(8,128)(2,1)} %param.31) | copy-start | bytes 147460
  27.2 39.0 %copy-start.14 = (bf16[16,512]{1,0:T(8,128)(2,1)S(1)}, bf16[16,512]{1,0:T(8,128)(2,1)}, u32[]{:S(2)}) copy-start(bf16[16,512]{1,0:T(8,128)(2,1)} %refs_3_.3) | copy-start | bytes 49156
  27.3 39.0 %copy-start.15 = (f32[4,512]{1,0:T(4,128)S(1)}, f32[4,512]{1,0:T(4,128)}, u32[]{:S(2)}) copy-start(f32[4,512]{1,0:T(4,128)} %refs_4_.2) | copy-start | bytes 24580
  27.3 39.0 %copy-start.18 = (f32[512]{0:T(512)S(1)}, f32[512]{0:T(512)}, u32[]{:S(2)}) copy-start(f32[512]{0:T(512)} %param.34) | copy-start | bytes 6148
  27.3 3.9 %collective-permute-start = (bf16[128,2048]{1,0:T(8,128)(2,1)S(1)}, bf16[128,2048]{1,0:T(8,128)(2,1)S(1)}, u32[]{:S(2)}, u32[]{:S(2)}) collective-permute-start(bf16[128,2048]{1,0:T(8,128)(2,1)S(1)} %get-tuple-element.28), channel_id=1, source_target_pairs={{0,16},{16,0},{32,48},{48,32},{64,80},{80,64},{96,112},{112,96},{1... | collective-permute-start | bytes 1572872 | tf_op jit(solution)/shard_map/ppermute | solution.py:475
  31.2 70.5 %copy-start.4 = (bf16[48,1,2,16,128]{4,3,2,1,0:T(8,128)(2,1)S(1)}, bf16[48,1,2,16,128]{4,3,2,1,0:T(8,128)(2,1)}, u32[]{:S(2)}) copy-start(bf16[48,1,2,16,128]{4,3,2,1,0:T(8,128)(2,1)} %refs_7_.2) | copy-start | bytes 1179652
  31.2 70.5 %copy-start.12 = (s32[16,8]{0,1:T(8,128)S(1)}, s32[16,8]{0,1:T(8,128)}, u32[]{:S(2)}) copy-start(s32[16,8]{0,1:T(8,128)} %param.26) | copy-start | bytes 1540
  31.2 70.6 %copy-start.13 = (bf16[16,512]{1,0:T(8,128)(2,1)S(1)}, bf16[16,512]{1,0:T(8,128)(2,1)}, u32[]{:S(2)}) copy-start(bf16[16,512]{1,0:T(8,128)(2,1)} %refs_4_.3) | copy-start | bytes 49156
  31.2 70.6 %copy-start.16 = (bf16[16,128]{1,0:T(8,128)(2,1)S(1)}, bf16[16,128]{1,0:T(8,128)(2,1)}, u32[]{:S(2)}) copy-start(bf16[16,128]{1,0:T(8,128)(2,1)} %refs_5_.3) | copy-start | bytes 12292
  31.2 70.6 %copy-start.17 = (bf16[16,128]{1,0:T(8,128)(2,1)S(1)}, bf16[16,128]{1,0:T(8,128)(2,1)}, u32[]{:S(2)}) copy-start(bf16[16,128]{1,0:T(8,128)(2,1)} %refs_6_.2) | copy-start | bytes 12292
  31.2 70.6 %copy-start.19 = (s32[512]{0:T(512)S(1)}, s32[512]{0:T(512)}, u32[]{:S(2)}) copy-start(s32[512]{0:T(512)} %refs_2_.1) | copy-start | bytes 6148
  31.4 72.4 %copy-start.3 = (f32[16,16,512]{2,1,0:T(8,128)S(1)}, f32[16,16,512]{2,1,0:T(8,128)}, u32[]{:S(2)}) copy-start(f32[16,16,512]{2,1,0:T(8,128)} %refs_7_.3) | copy-start | bytes 1572868
  31.4 72.4 %copy-start.6 = (bf16[256,512]{1,0:T(8,128)(2,1)S(1)}, bf16[256,512]{1,0:T(8,128)(2,1)}, u32[]{:S(2)}) copy-start(bf16[256,512]{1,0:T(8,128)(2,1)} %refs_8_.1) | copy-start | bytes 786436
  31.4 72.4 %copy-start.10 = (f32[16,512]{1,0:T(8,128)S(1)}, f32[16,512]{1,0:T(8,128)}, u32[]{:S(2)}) copy-start(f32[16,512]{1,0:T(8,128)} %refs_10_.1) | copy-start | bytes 98308
  31.4 72.4 %copy-start.11 = (bf16[16,512]{1,0:T(8,128)(2,1)S(1)}, bf16[16,512]{1,0:T(8,128)(2,1)}, u32[]{:S(2)}) copy-start(bf16[16,512]{1,0:T(8,128)(2,1)} %refs_6_.3) | copy-start | bytes 49156
  31.4 72.4 %copy-start.20 = (f32[512]{0:T(512)S(1)}, f32[512]{0:T(512)}, u32[]{:S(2)}) copy-start(f32[512]{0:T(512)} %param.37) | copy-start | bytes 6148
  31.4 72.4 %copy-start.21 = (f32[512]{0:T(512)S(1)}, f32[512]{0:T(512)}, u32[]{:S(2)}) copy-start(f32[512]{0:T(512)} %param.39) | copy-start | bytes 6148
  31.4 72.4 %copy-start.22 = (s32[16,2]{0,1:T(2,128)S(1)}, s32[16,2]{0,1:T(2,128)}, u32[]{:S(2)}) copy-start(s32[16,2]{0,1:T(2,128)} %param.40) | copy-start | bytes 388
  31.4 72.4 %copy-start.23 = (f32[16,2]{0,1:T(2,128)S(1)}, f32[16,2]{0,1:T(2,128)}, u32[]{:S(2)}) copy-start(f32[16,2]{0,1:T(2,128)} %param.41) | copy-start | bytes 388
  31.4 10.3 %collective-permute-start.1 = (bf16[128,1024]{1,0:T(8,128)(2,1)S(1)}, bf16[128,1024]{1,0:T(8,128)(2,1)S(1)}, u32[]{:S(2)}, u32[]{:S(2)}) collective-permute-start(bf16[128,1024]{1,0:T(8,128)(2,1)S(1)} %get-tuple-element.30), channel_id=1, source_target_pairs={{0,32},{16,48},{32,0},{48,16},{64,96},{80,112},{96,64},{112,80},{1... | collective-permute-start | bytes 786440 | tf_op jit(solution)/shard_map/ppermute | solution.py:486
  41.8 6.9 %collective-permute-start.2 = (bf16[128,512]{1,0:T(8,128)(2,1)S(1)}, bf16[128,512]{1,0:T(8,128)(2,1)S(1)}, u32[]{:S(2)}, u32[]{:S(2)}) collective-permute-start(bf16[128,512]{1,0:T(8,128)(2,1)S(1)} %get-tuple-element.32), channel_id=1, source_target_pairs={{0,96},{16,112},{32,64},{48,80},{64,32},{80,48},{96,0},{112,16},{1... | collective-permute-start | bytes 393224 | tf_op jit(solution)/shard_map/ppermute | solution.py:486
  50.7 39.2 %all-to-all-start.1 = ((bf16[32,3,16,128]{3,2,1,0:T(8,128)(2,1)}), bf16[32,3,16,128]{3,2,1,0:T(8,128)(2,1)S(1)}, u32[]{:S(2)}, u32[]{:S(2)}) async-start(bf16[32,3,16,128]{3,2,1,0:T(8,128)(2,1)} %select_pieces.1.refs_7_), calls=%async_computation.1 | async-start | bytes 786432 | tf_op jit(solution)/shard_map/all_to_all | solution.py:506
  90.9 21.3 %all-to-all-start.2 = ((bf16[16,16,512]{2,1,0:T(8,128)(2,1)}), bf16[16,16,512]{2,1,0:T(8,128)(2,1)S(1)}, u32[]{:S(2)}, u32[]{:S(2)}) async-start(bf16[16,16,512]{2,1,0:T(8,128)(2,1)} %get-tuple-element.40), calls=%async_computation.2 | async-start | bytes 524288 | tf_op jit(solution)/shard_map/all_to_all | solution.py:532

commit v3 on v2

--- a/solution.py
+++ b/solution.py
@@ -10,6 +10,8 @@
 MIG = 2
 LANES = 128
 SUB = 8
+ROWS = 16
+PLANE = 8
 F32 = jnp.float32
 BF16 = jnp.bfloat16
 
@@ -69,15 +71,28 @@
     return found
 
 
+def _levels(slots, requests):
+    found = [jnp.int32(0)] * MIG
+    for a, _, arrived, order in slots:
+        found = [jnp.where(arrived & (order == j), a // (requests * PLANE), found[j]) for j in range(MIG)]
+    return found
+
+
 def _pack_body(
-    requests, rep_ref, anchor_ref, table_ref, pool_ref, window_ref, scan_ref, out_ref,
-    scans_ref, pages_ref, win_ref, sems,
+    requests, rep_ref, anchor_ref, table_ref, pool_ref, window_ref, scan_ref, hidden_ref, weight_ref, out_ref, token_ref,
+    scans_ref, pages_ref, win_ref, rows_ref, blocks_ref, sems,
 ):
     pages = table_ref.shape[0]
     taps, _, channels = window_ref.shape
     blocks = channels // LANES
-    whole = pltpu.make_async_copy(window_ref, win_ref, sems.at[0])
-    whole.start()
+    plane = out_ref.shape[0]
+    width = weight_ref.shape[2] // plane
+    copies = [
+        pltpu.make_async_copy(hidden_ref.at[0], rows_ref, sems.at[0]),
+        pltpu.make_async_copy(window_ref, win_ref, sems.at[1]),
+    ]
+    for copy in copies:
+        copy.start()
     base = rep_ref[0] * requests
     mask = _present(anchor_ref, base, requests)
     first, second = jnp.int32(0), jnp.int32(0)
@@ -86,7 +101,6 @@
         second = jnp.where(leaves, first, second)
         first = jnp.where(leaves, o, first)
     leaving = (first, second)
-    copies = [whole]
     for j, o in enumerate(leaving):
         copies.append(pltpu.make_async_copy(scan_ref.at[o], scans_ref.at[j], sems.at[len(copies)]))
         copies[-1].start()
@@ -95,34 +109,40 @@
                 pltpu.make_async_copy(pool_ref.at[table_ref[m, o], 0], pages_ref.at[j, m], sems.at[len(copies)])
             )
             copies[-1].start()
+    weights = []
+    for f in range(plane):
+        weights.append(
+            pltpu.make_async_copy(
+                weight_ref.at[0, :, pl.ds(f * width, width)], blocks_ref.at[f], sems.at[len(copies) + f]
+            )
+        )
+        weights[-1].start()
     for copy in copies:
         copy.wait()
     row = lax.broadcasted_iota(jnp.int32, (requests, channels), 0)
     for j, o in enumerate(leaving):
         scan = scans_ref[j]
-        high = scan.astype(BF16).astype(F32)
-        rest = scan - high
-        middle = rest.astype(BF16).astype(F32)
-        low = rest - middle
-        tails = []
-        for part in (high, middle, low):
-            for b in range(blocks):
-                for h in range(scan.shape[0] // SUB):
-                    tails.append(part[h * SUB : (h + 1) * SUB, b * LANES : (b + 1) * LANES])
         lines = [
             jnp.sum(jnp.where(row == o, win_ref[t].astype(F32), 0.0), axis=0, keepdims=True) for t in range(taps)
         ]
         win = jnp.concatenate([*lines, jnp.zeros((SUB - taps, channels), F32)], axis=0)
-        for b in range(blocks):
-            tails.append(win[:, b * LANES : (b + 1) * LANES])
-        for m in range(pages):
-            page = pages_ref[j, m].astype(F32)
+        for i in range(plane):
+            b, h = i // 2, i % 2
+            head = scan[h * SUB : (h + 1) * SUB, b * LANES : (b + 1) * LANES]
+            tail = win[:, i * LANES : (i + 1) * LANES] if i < blocks else jnp.zeros((SUB, LANES), F32)
             for c in range(2):
-                for h in range(2):
-                    i = 4 * m + 2 * c + h
-                    tail = tails[i] if i < len(tails) else jnp.zeros((SUB, LANES), F32)
-                    head = page[c, h * SUB : (h + 1) * SUB, :]
-                    out_ref[i, j] = jnp.concatenate([head, tail], axis=0).astype(BF16)
+                out_ref[i, 3 * j + c] = pages_ref[j, i, c]
+            out_ref[i, 3 * j + 2] = jnp.concatenate([head, tail], axis=0).astype(BF16)
+    hidden = rows_ref[...]
+    for f in range(plane):
+        weights[f].wait()
+        total = jnp.dot(hidden, blocks_ref[f], preferred_element_type=F32).astype(BF16)
+        for q in range(hidden.shape[0] // ROWS):
+            for b in range(width // LANES):
+                out_ref[f, 3 * MIG + q * (width // LANES) + b] = total[
+                    q * ROWS : (q + 1) * ROWS, b * LANES : (b + 1) * LANES
+                ]
+    token_ref[...] = jnp.zeros_like(token_ref)
 
 
 def _route_body(requests, anchor_ref, dep_ref, out_ref):
@@ -146,46 +166,29 @@
     out_ref[...] = jnp.where(lane == 0, one, jnp.where(lane == 1, two, 0.0)).astype(jnp.int32)
 
 
-def _own_bits(r):
-    c, x = r % 2, (r // 2) % 4
-    return (x // 2) * 4 + ((x // 2) ^ (x % 2)) * 2 + c
-
-
-def _expert_body(rep_ref, hidden_ref, weight_ref, dep_ref, keep_ref, send_ref):
-    width = weight_ref.shape[2] // 8
-    own = _own_bits(rep_ref[0])
-    hidden = hidden_ref[0]
-    for p in (4, 5, 6, 7, 0, 1, 2, 3):
-        block = own ^ ((p % 2) * 4 + (p // 2 % 2) * 2 + p // 4)
-        columns = pl.ds(pl.multiple_of(block * width, width), width)
-        total = jnp.dot(hidden, weight_ref[0, :, columns], preferred_element_type=F32)
-        at = slice(p % 4 * width, (p % 4 + 1) * width)
-        if p < 4:
-            keep_ref[:, at] = total
-        else:
-            send_ref[:, at] = total.astype(BF16)
-
-
-def _fold_body(keep_ref, got_ref, next_ref, send_ref):
-    half = next_ref.shape[1]
-    next_ref[...] = keep_ref[:, :half] + got_ref[:, :half].astype(F32)
-    send_ref[...] = (keep_ref[:, half:] + got_ref[:, half:].astype(F32)).astype(BF16)
-
-
-def _select_body(index_ref, in_ref, keep_ref, got_ref, out_ref):
-    replicas = out_ref.shape[0]
-    cap = keep_ref.shape[0] // replicas
-    blocks = keep_ref.shape[1] // LANES
+def _select_body(index_ref, in_ref, out_ref):
+    replicas, tiles = out_ref.shape[0], out_ref.shape[1]
+    plane = in_ref.shape[0]
+    cap = 4
+    blocks = ROWS // cap
     for d in range(replicas):
         for j in range(MIG):
             i = index_ref[d, j]
-            out_ref[d, j] = in_ref[i // MIG, i % MIG]
-    total = keep_ref[...] + got_ref[...].astype(F32)
-    for d in range(replicas):
-        rows = total[d * cap : (d + 1) * cap]
-        out_ref[d, MIG] = jnp.concatenate(
-            [rows[:, b * LANES : (b + 1) * LANES] for b in range(blocks)], axis=0
-        ).astype(BF16)
+            member = (i // MIG) % plane
+            for k in range(3):
+                out_ref[d, 3 * j + k] = in_ref[member, 3 * (i % MIG) + k]
+    for q in range(replicas // blocks):
+        totals = []
+        for b in range(blocks):
+            at = 3 * MIG + q * blocks + b
+            total = in_ref[0, at].astype(F32)
+            for p in range(1, plane):
+                total = total + in_ref[p, at].astype(F32)
+            totals.append(total)
+        for n in range(blocks):
+            out_ref[q * blocks + n, tiles - 1] = jnp.concatenate(
+                [total[n * cap : (n + 1) * cap] for total in totals], axis=0
+            ).astype(BF16)
 
 
 def _local_body(
@@ -200,9 +203,10 @@
     col_w = lax.broadcasted_iota(jnp.int32, which_ref.shape, 1)
     pick = jnp.zeros((requests, requests), F32)
     which = jnp.zeros(which_ref.shape, F32)
-    for g, (_, local, arrived, order) in enumerate(_slots(rep_ref, anchor_ref, requests)):
+    for g, (a, local, arrived, order) in enumerate(_slots(rep_ref, anchor_ref, requests)):
         pick = jnp.where((row == g) & (col == local) & ~arrived, 1.0, pick)
-        which = jnp.where((row_w == g) & (col_w == order) & arrived, 1.0, which)
+        level = a // (requests * PLANE)
+        which = jnp.where((row_w == g) & (col_w == level * MIG + order) & arrived, 1.0, which)
     pick = pick.astype(BF16)
     mixed = conv_ref[...].astype(F32) * weights[taps : taps + 1] + bias_ref[...]
     for t in range(taps):
@@ -216,15 +220,17 @@
 def _act_body(moved_ref, base_ref, which_ref, taps_ref, mix_ref, out_ref, act_ref, win_ref):
     requests, channels = base_ref.shape
     blocks = channels // LANES
-    first = 3 * blocks * 2
     weights = taps_ref[...]
     taps = weights.shape[0] - 1
     mixed = base_ref[...]
-    for j in range(MIG):
-        for b in range(blocks):
-            win_ref[:, b * LANES : (b + 1) * LANES] = moved_ref[first + b, j].astype(F32)[SUB : 2 * SUB]
-        line = jnp.sum(win_ref[0:taps, :] * weights[0:taps], axis=0, keepdims=True)
-        mixed = mixed + which_ref[:, j : j + 1] * line
+    levels = moved_ref.shape[0] // PLANE
+    for z in range(levels):
+        for j in range(MIG):
+            for b in range(blocks):
+                tile = moved_ref[z * PLANE + b, 3 * j + 2].astype(F32)
+                win_ref[:, b * LANES : (b + 1) * LANES] = tile[SUB : 2 * SUB]
+            line = jnp.sum(win_ref[0:taps, :] * weights[0:taps], axis=0, keepdims=True)
+            mixed = mixed + which_ref[:, z * MIG + j : z * MIG + j + 1] * line
     act = mixed * (1.0 / (1.0 + jnp.exp(-mixed)))
     act_ref[...] = act
     turn = (((1,), (1,)), ((), ()))
@@ -235,13 +241,12 @@
     fill = jnp.zeros((requests, LANES - 2 * low.shape[1]), F32)
     packed = jnp.concatenate([high[:, :rank], high[:, rank:], low, fill], axis=1)
     experts = out_ref.shape[0]
-    replicas = moved_ref.shape[0]
-    sums = {}
-    for r in range(8):
-        total = moved_ref[r, MIG].astype(F32)
-        for z in range(1, replicas // 8):
-            total = total + moved_ref[z * 8 + r, MIG].astype(F32)
-        sums[_own_bits(r)] = total
+    sums = []
+    for r in range(PLANE):
+        total = moved_ref[r, 3 * MIG].astype(F32)
+        for z in range(1, levels):
+            total = total + moved_ref[z * PLANE + r, 3 * MIG].astype(F32)
+        sums.append(total)
     empty = jnp.zeros((requests - SUB, LANES), F32)
     for e in range(experts):
         block = sums[e // 2][e % 2 * SUB : (e % 2 + 1) * SUB]
@@ -254,19 +259,13 @@
     bias_ref, decay_ref, skip_ref, old_ref, rate_ref, gate_out_ref, skip_out_ref, step_out_ref, bias_out_ref,
     share_out_ref, arr_ref, count_ref,
 ):
-    channels = act_ref.shape[1]
-    blocks = channels // LANES
-    halves = states // SUB
-    n = blocks * halves
-    for j in range(MIG):
-        for b in range(blocks):
-            for h in range(halves):
-                i = b * halves + h
-                high = moved_ref[i, j].astype(F32)[SUB : 2 * SUB]
-                middle = moved_ref[n + i, j].astype(F32)[SUB : 2 * SUB]
-                lowest = moved_ref[2 * n + i, j].astype(F32)[SUB : 2 * SUB]
-                arr_ref[j, h * SUB : (h + 1) * SUB, b * LANES : (b + 1) * LANES] = high + (middle + lowest)
-    for g, (_, local, arrived, order) in enumerate(_slots(rep_ref, anchor_ref, requests)):
+    slots = _slots(rep_ref, anchor_ref, requests)
+    for j, level in enumerate(_levels(slots, requests)):
+        for i in range(PLANE):
+            b, h = i // 2, i % 2
+            tile = moved_ref[level * PLANE + i, 3 * j + 2].astype(F32)
+            arr_ref[j, h * SUB : (h + 1) * SUB, b * LANES : (b + 1) * LANES] = tile[0:SUB]
+    for g, (_, local, arrived, order) in enumerate(slots):
         old_ref[g] = jnp.where(arrived, arr_ref[order], scan_ref[local])
     rate_ref[...] = -jnp.exp(decay_ref[...])
     gate = gate_ref[...].astype(F32)
@@ -359,17 +358,15 @@
     at = lax.broadcasted_iota(jnp.int32, (requests, MIG * span), 1)
     seen_moved = (at // span == order) & (at % span < live)
     down = lax.broadcasted_iota(jnp.int32, (span, head), 0)
-    for j in range(MIG):
-        for m in range(pages):
-            for h in range(2):
-                for c, ref in ((0, keys_ref), (1, values_ref)):
-                    start = j * span + m * page + h * SUB
-                    ref[start : start + SUB, :] = moved_ref[4 * m + 2 * c + h, j].astype(F32)[0:SUB]
+    for j, level in enumerate(_levels(slots, requests)):
         for c, ref in ((0, keys_ref), (1, values_ref)):
-            block = ref[j * span : (j + 1) * span, :]
+            for m in range(pages):
+                start = j * span + m * page
+                ref[start : start + page, :] = moved_ref[level * PLANE + m, 3 * j + c]
+            block = ref[j * span : (j + 1) * span, :].astype(F32)
             pages_ref[j, 0, c] = jnp.where(down < live_of[j], block, 0.0).astype(BF16)
-    moved_keys = keys_ref[...].astype(BF16)
-    moved_values = values_ref[...].astype(BF16)
+    moved_keys = keys_ref[...]
+    moved_values = values_ref[...]
     pool_keys = pool_ref[:, 0, 0].reshape(pool * page, head)
     pool_values = pool_ref[:, 0, 1].reshape(pool * page, head)
     query = query_ref[...]
@@ -437,53 +434,27 @@
     table = block_table.T
     window = jnp.transpose(window_state, (1, 0, 2))
 
-    def piece(tiles):
-        return _shape((replicas, tiles, 2 * SUB, LANES), BF16)
-
-    packed = _call(
+    tiles = 3 * MIG + slots * features // (PLANE * ROWS * LANES)
+    packed, token = _call(
         lambda *refs: _pack_body(requests, *refs),
         "pack_leaving",
-        piece(MIG),
-        [_smem()] * 3 + [_hbm()] * 3,
-        _vmem(),
-        (rep, anchor, table, page_pool, window, scan_state),
+        [_shape((PLANE, tiles, ROWS, LANES), BF16), _shape((SUB, LANES), F32)],
+        [_smem()] * 3 + [_hbm()] * 5,
+        [_vmem()] * 2,
+        (rep, anchor, table, page_pool, window, scan_state, expert_hidden, down_weight),
         scratch=[
             pltpu.VMEM((MIG, states, channels), F32),
             pltpu.VMEM((MIG, pages, 2, page, head), BF16),
             pltpu.VMEM(window.shape, BF16),
-            pltpu.SemaphoreType.DMA((1 + MIG * (1 + pages),)),
+            pltpu.VMEM(expert_hidden.shape[1:], BF16),
+            pltpu.VMEM((PLANE, down_weight.shape[1], features // PLANE), BF16),
+            pltpu.SemaphoreType.DMA((2 + MIG * (1 + pages) + PLANE,)),
         ],
-        us=1.5,
+        us=4,
         room=60,
     )
-    spread = lax.all_to_all(packed, "rep", split_axis=0, concat_axis=0, tiled=True)
-
-    keep, send = _call(
-        _expert_body,
-        "expert_terms",
-        [_shape((slots, features // 2), F32), _shape((slots, features // 2), BF16)],
-        [_smem()] + [_vmem()] * 2 + [_any()],
-        [_vmem()] * 2,
-        (rep, expert_hidden, down_weight, packed),
-        us=2,
-    )
-
-    def at(z, x, c):
-        return (z * 4 + x) * 2 + c
-
-    every = [(z, x, c) for z in range(4) for x in range(4) for c in range(2)]
-    got = lax.ppermute(send, "rep", [(at(z, x, c), at(z, x, 1 - c)) for z, x, c in every])
-    for part, partner in ((4, (1, 0, 3, 2)), (8, (3, 2, 1, 0))):
-        keep, send = _call(
-            _fold_body,
-            "fold",
-            [_shape((slots, features // part), F32), _shape((slots, features // part), BF16)],
-            [_vmem()] * 2,
-            [_vmem()] * 2,
-            (keep, got),
-            us=0.5,
-        )
-        got = lax.ppermute(send, "rep", [(at(z, x, c), at(z, partner[x], c)) for z, x, c in every])
+    planes = [[z * PLANE + i for i in range(PLANE)] for z in range(replicas // PLANE)]
+    spread = lax.all_to_all(packed, "rep", split_axis=0, concat_axis=0, tiled=True, axis_index_groups=planes)
 
     index = _call(
         lambda *refs: _route_body(requests, *refs),
@@ -491,17 +462,17 @@
         _shape((replicas, LANES), jnp.int32),
         [_vmem(), _any()],
         _vmem(),
-        (anchor.reshape(replicas, requests), packed),
+        (anchor.reshape(replicas, requests), token),
         us=1,
     )
     onward = _call(
         _select_body,
         "select_pieces",
-        piece(MIG + 1),
-        [_smem()] + [_vmem()] * 3,
+        _shape((replicas, 3 * MIG + 1, ROWS, LANES), BF16),
+        [_smem(), _vmem()],
         _vmem(),
-        (index, spread, keep, got),
-        us=1,
+        (index, spread),
+        us=1.5,
     )
     moved = lax.all_to_all(onward, "rep", split_axis=0, concat_axis=0, tiled=True)
 
@@ -516,7 +487,7 @@
         ],
         [_smem()] * 2 + [_vmem()] * 5 + [_any()],
         [_vmem()] * 4,
-        (rep, anchor, window, conv_input, filter_taps, filter_bias.reshape(1, channels), mix_weight.T, onward),
+        (rep, anchor, window, conv_input, filter_taps, filter_bias.reshape(1, channels), mix_weight.T, index),
         us=1.5,
     )
     sums, act = _call(
@@ -538,7 +509,7 @@
         [_smem()] * 3 + [_vmem()] * 6 + [_any()],
         [_vmem()] * 2,
         (rep, anchor, lengths, table, query, new_key, new_value, page_pool, moved, act),
-        scratch=[pltpu.VMEM((MIG * pages * page, head), F32)] * 2,
+        scratch=[pltpu.VMEM((MIG * pages * page, head), BF16)] * 2,
         us=2,
     )
     ready = _call(

time: 114 us -> 116 us (1.018)
  waiting for transfers between devices: 40.9 us -> 68.8 us
  starting transfers between devices: 56 us -> 31.3 us
  local copies, waits for them, and re-layouts: 3.95 us -> 0.19 us
  Pallas kernels: 11.4 us -> 13.8 us
    all_to_all x1, waiting for transfers between devices: 22.8 us -> 45.5 us  [per_device(): lax.all_to_all(onward, 'rep', split_axis=0, concat_axis=0, tiled=True)]
    all_to_all x1, waiting for transfers between devices: 0.01 us -> 16.9 us  [per_device(): lax.all_to_all(packed, 'rep', split_axis=0, concat_axis=0, tiled=True, ax...]
    ppermute x3 -> x0, waiting for transfers between devices: 10.6 us -> none  [the longest x2 8.93 us: per_device(): lax.ppermute(send, 'rep', [(at(z, x, c), at(z, partner[x], c)) for z, x,...]
    ppermute x3 -> x0, starting transfers between devices: 10.2 us -> none  [the longest x2 7.93 us: per_device(): lax.ppermute(send, 'rep', [(at(z, x, c), at(z, partner[x], c)) for z, x,...]
    all_to_all x1, starting transfers between devices: 19.4 us -> 10.4 us  [per_device(): lax.all_to_all(packed, 'rep', split_axis=0, concat_axis=0, tiled=True, ax...]
    unnamed x48 -> x42, local copies, waits for them, and re-layouts: 3.88 us -> 0.11 us
    all_to_all x1, starting transfers between devices: 15.6 us -> 12.3 us  [per_device(): lax.all_to_all(onward, 'rep', split_axis=0, concat_axis=0, tiled=True)]
    pallas_call x11 -> x8, Pallas kernels: 11.4 us -> 13.8 us  [_call(): pl.pallas_call(body, name=name, out_shape=out_shape, in_specs=ins, out_sp...]
  transfers between devices with their start and end apart: 6 -> 3, of which waited for: 5 -> 3; matrix products, arithmetic and copies ran while one was open for 0% -> 0% of each run, Pallas kernels for 4% -> 4%
where the time goes in v3:
time: 116 us; the launch traced here: 115 us
  waiting for transfers between devices  68.8 us (59%)
  starting transfers between devices  31.3 us (27%)
  Pallas kernels  13.8 us (12%)
    all_to_all x1, waiting for transfers between devices, per_device(): lax.all_to_all(onward, 'rep', split_axis=0, concat_axis=0, tiled=True)  45.5 us
    all_to_all x1, waiting for transfers between devices, per_device(): lax.all_to_all(packed, 'rep', split_axis=0, concat_axis=0, tiled=True, ax...  16.9 us
    pallas_call x8, Pallas kernels, _call(): pl.pallas_call(body, name=name, out_shape=out_shape, in_specs=ins, out_sp...  13.8 us
    all_to_all x1, starting transfers between devices, per_device(): lax.all_to_all(onward, 'rep', split_axis=0, concat_axis=0, tiled=True)  12.3 us
    all_to_all x1, starting transfers between devices, per_device(): lax.all_to_all(packed, 'rep', split_axis=0, concat_axis=0, tiled=True, ax...  10.4 us
    all_to_all x1, starting transfers between devices, per_device(): lax.all_to_all(sums, 'exp', split_axis=0, concat_axis=0, tiled=True)  8.68 us
    all_to_all x1, waiting for transfers between devices, per_device(): lax.all_to_all(sums, 'exp', split_axis=0, concat_axis=0, tiled=True)  6.45 us
  transfers between devices with their start and end apart: 3, of which 3 were waited for; matrix products, arithmetic and copies ran while one was open for 0% of the time, Pallas kernels for 4%

profile of v3, /device:TPU:1, one launch (start us, length us, event | category | flops | bytes accessed | tf_op | source)
XLA Modules:
  0.0 115.1 jit_solution(16275047692800042358)
XLA Ops:
  0.6 5.2 %pack_leaving.1 = (bf16[8,38,16,128]{3,2,1,0:T(8,128)(2,1)}, f32[8,128]{1,0:T(8,128)}) custom-call(s32[1]{0:T(128)} %bitcast.refs_0_, s32[512]{0:T(512)} %refs_1_.7, s32[8,16]{1,0:T(8,128)} %bitcast.12, bf16[48,1,2,16,128]{4,3,2,1,0:T(8,128)(2,1)} %refs_7_.4, bf16[3,16,512]{2,1,0:T(8,128)(2,1)} %bitcast.10, f32[16,16,512]{2,1,0:T(8,128)} %refs_7_.5, ...), custom_call_target="tpu_custom_call" | custom-call | bytes 14000000 | tf_op jit(solution)/shard_map/pack_leaving/pallas_call | solution.py:40
  5.9 0.0 copy-start.5
  5.9 0.0 copy-start.14
  5.9 10.4 %all-to-all-start = ((bf16[8,38,16,128]{3,2,1,0:T(8,128)(2,1)}), bf16[8,38,16,128]{3,2,1,0:T(8,128)(2,1)S(1)}, u32[]{:S(2)}, u32[]{:S(2)}) async-start(bf16[8,38,16,128]{3,2,1,0:T(8,128)(2,1)} %get-tuple-element.24), calls=%async_computation | async-start | bytes 2490368 | tf_op jit(solution)/shard_map/all_to_all | solution.py:457
  16.3 0.0 copy-done.5
  16.3 0.1 reshape.24.refs_0_
  16.3 0.0 copy-done.14
  16.3 0.2 route_pieces.1.index_ref.refs_7_
  16.6 16.9 %all-to-all-done.in_ref = bf16[8,38,16,128]{3,2,1,0:T(8,128)(2,1)S(1)} async-done(((bf16[8,38,16,128]{3,2,1,0:T(8,128)(2,1)}), bf16[8,38,16,128]{3,2,1,0:T(8,128)(2,1)S(1)}, u32[]{:S(2)}, u32[]{:S(2)}) %all-to-all-start) | async-done | bytes 1245216 | tf_op jit(solution)/shard_map/all_to_all | solution.py:457
  33.5 2.4 %select_pieces.1 = bf16[32,7,16,128]{3,2,1,0:T(8,128)(2,1)} custom-call(s32[32,128]{1,0:T(8,128)S(1)} %route_pieces.1.index_ref.refs_7_, bf16[8,38,16,128]{3,2,1,0:T(8,128)(2,1)S(1)} %all-to-all-done.in_ref), custom_call_target="tpu_custom_call" | custom-call | bytes 5250000 | tf_op jit(solution)/shard_map/select_pieces/pallas_call | solution.py:40
  35.9 0.0 copy-start.2
  35.9 0.0 copy-start.4
  35.9 0.0 copy-start.10
  35.9 0.0 copy-start.11
  35.9 0.0 copy-start.15
  35.9 12.3 %all-to-all-start.1 = ((bf16[32,7,16,128]{3,2,1,0:T(8,128)(2,1)}), bf16[32,7,16,128]{3,2,1,0:T(8,128)(2,1)S(1)}, u32[]{:S(2)}, u32[]{:S(2)}) async-start(bf16[32,7,16,128]{3,2,1,0:T(8,128)(2,1)} %select_pieces.1), calls=%async_computation.1 | async-start | bytes 1835008 | tf_op jit(solution)/shard_map/all_to_all | solution.py:477
  48.2 0.0 copy-start.1
  48.2 0.0 copy-start.7
  48.2 0.0 copy-start.9
  48.3 0.0 copy-start.12
  48.3 0.0 copy-start.13
  48.3 0.0 copy-start.16
  48.3 0.0 copy-done.2
  48.3 0.0 copy-done.4
  48.3 0.0 copy-done.10
  48.3 0.0 copy-done.11
  48.3 0.0 copy-done.15
  48.3 0.9 filter_local.1
  49.2 45.5 %all-to-all-done.1.moved_ref.refs_8_.refs_4_ = bf16[32,7,16,128]{3,2,1,0:T(8,128)(2,1)S(1)} async-done(((bf16[32,7,16,128]{3,2,1,0:T(8,128)(2,1)}), bf16[32,7,16,128]{3,2,1,0:T(8,128)(2,1)S(1)}, u32[]{:S(2)}, u32[]{:S(2)}) %all-to-all-start.1) | async-done | bytes 917536 | tf_op jit(solution)/shard_map/all_to_all | solution.py:477
  94.7 1.0 filter_and_project.1
  95.7 0.0 copy-start
  95.7 0.0 copy-start.3
  95.7 0.0 copy-start.6
  95.7 0.0 copy-start.8
  95.7 0.0 copy-start.17
  95.7 0.0 copy-start.18
  95.8 0.0 copy-start.19
  95.8 0.0 copy-start.20
  95.8 8.7 %all-to-all-start.2 = ((bf16[16,16,512]{2,1,0:T(8,128)(2,1)}), bf16[16,16,512]{2,1,0:T(8,128)(2,1)S(1)}, u32[]{:S(2)}, u32[]{:S(2)}) async-start(bf16[16,16,512]{2,1,0:T(8,128)(2,1)} %get-tuple-element.32), calls=%async_computation.2 | async-start | bytes 524288 | tf_op jit(solution)/shard_map/all_to_all | solution.py:503
  104.5 0.0 copy-done.1
  104.5 0.0 copy-done.7
  104.5 0.0 copy-done.9
  104.5 0.0 copy-done.12
  104.5 0.0 copy-done.13
  104.5 0.0 copy-done.16
  104.5 2.0 %attend.1 = (bf16[16,512]{1,0:T(8,128)(2,1)}, bf16[2,1,2,128,128]{4,3,2,1,0:T(8,128)(2,1)}) custom-call(s32[1]{0:T(128)} %bitcast.refs_0_, s32[512]{0:T(512)S(1)} %copy-done.5, s32[512]{0:T(512)S(1)} %copy-done.16, s32[8,16]{1,0:T(8,128)S(1)} %bitcast.13, bf16[16,512]{1,0:T(8,128)(2,1)S(1)} %copy-done.7, bf16[16,128]{1,0:T(8,128)(2,1)S(1)} %copy-done.12, ...), custom_call_target="tpu_custom_call" | custom-call | bytes 7000000 | tf_op jit(solution)/shard_map/attend/pallas_call | solution.py:40
  106.5 0.0 copy-done
  106.5 0.0 copy-done.3
  106.5 0.0 copy-done.6
  106.6 0.0 copy-done.8
  106.6 0.0 copy-done.17
  106.6 0.0 copy-done.18
  106.6 0.0 copy-done.19
  106.6 0.0 copy-done.20
  106.6 1.0 ready_state.1
  107.6 6.5 %all-to-all-done.2.refs_0_ = bf16[16,16,512]{2,1,0:T(8,128)(2,1)S(1)} async-done(((bf16[16,16,512]{2,1,0:T(8,128)(2,1)}), bf16[16,16,512]{2,1,0:T(8,128)(2,1)S(1)}, u32[]{:S(2)}, u32[]{:S(2)}) %all-to-all-start.2) | async-done | bytes 262176 | tf_op jit(solution)/shard_map/all_to_all | solution.py:503
  114.1 1.1 update_state.1
Async XLA Ops:
  5.9 10.4 %copy-start.5 = (s32[512]{0:T(512)S(1)}, s32[512]{0:T(512)}, u32[]{:S(2)}) copy-start(s32[512]{0:T(512)} %refs_1_.7) | copy-start | bytes 6148
  5.9 10.4 %copy-start.14 = (f32[8,128]{1,0:T(8,128)S(1)}, f32[8,128]{1,0:T(8,128)}, u32[]{:S(2)}) copy-start(f32[8,128]{1,0:T(8,128)} %get-tuple-element.23.refs_1_) | copy-start | bytes 12292
  5.9 27.6 %all-to-all-start = ((bf16[8,38,16,128]{3,2,1,0:T(8,128)(2,1)}), bf16[8,38,16,128]{3,2,1,0:T(8,128)(2,1)S(1)}, u32[]{:S(2)}, u32[]{:S(2)}) async-start(bf16[8,38,16,128]{3,2,1,0:T(8,128)(2,1)} %get-tuple-element.24), calls=%async_computation | async-start | bytes 2490368 | tf_op jit(solution)/shard_map/all_to_all | solution.py:457
  35.9 12.4 %copy-start.2 = (bf16[512,288]{0,1:T(8,128)(2,1)S(1)}, bf16[512,288]{0,1:T(8,128)(2,1)}, u32[]{:S(2)}) copy-start(bf16[512,288]{0,1:T(8,128)(2,1)} %param.35) | copy-start | bytes 884740
  35.9 12.4 %copy-start.4 = (bf16[16,3,512]{2,0,1:T(8,128)(2,1)S(1)}, bf16[16,3,512]{2,0,1:T(8,128)(2,1)}, u32[]{:S(2)}) copy-start(bf16[16,3,512]{2,0,1:T(8,128)(2,1)} %param.31) | copy-start | bytes 147460
  35.9 12.4 %copy-start.10 = (bf16[16,512]{1,0:T(8,128)(2,1)S(1)}, bf16[16,512]{1,0:T(8,128)(2,1)}, u32[]{:S(2)}) copy-start(bf16[16,512]{1,0:T(8,128)(2,1)} %refs_3_.3) | copy-start | bytes 49156
  35.9 12.4 %copy-start.11 = (f32[4,512]{1,0:T(4,128)S(1)}, f32[4,512]{1,0:T(4,128)}, u32[]{:S(2)}) copy-start(f32[4,512]{1,0:T(4,128)} %refs_4_.2) | copy-start | bytes 24580
  35.9 12.4 %copy-start.15 = (f32[512]{0:T(512)S(1)}, f32[512]{0:T(512)}, u32[]{:S(2)}) copy-start(f32[512]{0:T(512)} %param.34) | copy-start | bytes 6148
  35.9 58.8 %all-to-all-start.1 = ((bf16[32,7,16,128]{3,2,1,0:T(8,128)(2,1)}), bf16[32,7,16,128]{3,2,1,0:T(8,128)(2,1)S(1)}, u32[]{:S(2)}, u32[]{:S(2)}) async-start(bf16[32,7,16,128]{3,2,1,0:T(8,128)(2,1)} %select_pieces.1), calls=%async_computation.1 | async-start | bytes 1835008 | tf_op jit(solution)/shard_map/all_to_all | solution.py:477
  48.2 56.3 %copy-start.1 = (bf16[48,1,2,16,128]{4,3,2,1,0:T(8,128)(2,1)S(1)}, bf16[48,1,2,16,128]{4,3,2,1,0:T(8,128)(2,1)}, u32[]{:S(2)}) copy-start(bf16[48,1,2,16,128]{4,3,2,1,0:T(8,128)(2,1)} %refs_7_.4) | copy-start | bytes 1179652
  48.2 56.2 %copy-start.7 = (bf16[16,512]{1,0:T(8,128)(2,1)S(1)}, bf16[16,512]{1,0:T(8,128)(2,1)}, u32[]{:S(2)}) copy-start(bf16[16,512]{1,0:T(8,128)(2,1)} %refs_4_.3) | copy-start | bytes 49156
  48.2 56.2 %copy-start.9 = (s32[16,8]{0,1:T(8,128)S(1)}, s32[16,8]{0,1:T(8,128)}, u32[]{:S(2)}) copy-start(s32[16,8]{0,1:T(8,128)} %param.26) | copy-start | bytes 1540
  48.3 56.2 %copy-start.12 = (bf16[16,128]{1,0:T(8,128)(2,1)S(1)}, bf16[16,128]{1,0:T(8,128)(2,1)}, u32[]{:S(2)}) copy-start(bf16[16,128]{1,0:T(8,128)(2,1)} %refs_5_.3) | copy-start | bytes 12292
  48.3 56.2 %copy-start.13 = (bf16[16,128]{1,0:T(8,128)(2,1)S(1)}, bf16[16,128]{1,0:T(8,128)(2,1)}, u32[]{:S(2)}) copy-start(bf16[16,128]{1,0:T(8,128)(2,1)} %refs_6_.4) | copy-start | bytes 12292
  48.3 56.2 %copy-start.16 = (s32[512]{0:T(512)S(1)}, s32[512]{0:T(512)}, u32[]{:S(2)}) copy-start(s32[512]{0:T(512)} %refs_2_.1) | copy-start | bytes 6148
  95.7 10.8 %copy-start = (f32[16,16,512]{2,1,0:T(8,128)S(1)}, f32[16,16,512]{2,1,0:T(8,128)}, u32[]{:S(2)}) copy-start(f32[16,16,512]{2,1,0:T(8,128)} %refs_7_.5) | copy-start | bytes 1572868
  95.7 10.8 %copy-start.3 = (bf16[256,512]{1,0:T(8,128)(2,1)S(1)}, bf16[256,512]{1,0:T(8,128)(2,1)}, u32[]{:S(2)}) copy-start(bf16[256,512]{1,0:T(8,128)(2,1)} %refs_8_.1) | copy-start | bytes 786436
  95.7 10.8 %copy-start.6 = (f32[16,512]{1,0:T(8,128)S(1)}, f32[16,512]{1,0:T(8,128)}, u32[]{:S(2)}) copy-start(f32[16,512]{1,0:T(8,128)} %refs_10_.1) | copy-start | bytes 98308
  95.7 10.8 %copy-start.8 = (bf16[16,512]{1,0:T(8,128)(2,1)S(1)}, bf16[16,512]{1,0:T(8,128)(2,1)}, u32[]{:S(2)}) copy-start(bf16[16,512]{1,0:T(8,128)(2,1)} %refs_6_.5) | copy-start | bytes 49156
  95.7 10.8 %copy-start.17 = (f32[512]{0:T(512)S(1)}, f32[512]{0:T(512)}, u32[]{:S(2)}) copy-start(f32[512]{0:T(512)} %param.37) | copy-start | bytes 6148
  95.7 10.8 %copy-start.18 = (f32[512]{0:T(512)S(1)}, f32[512]{0:T(512)}, u32[]{:S(2)}) copy-start(f32[512]{0:T(512)} %param.39) | copy-start | bytes 6148
  95.8 10.8 %copy-start.19 = (s32[16,2]{0,1:T(2,128)S(1)}, s32[16,2]{0,1:T(2,128)}, u32[]{:S(2)}) copy-start(s32[16,2]{0,1:T(2,128)} %param.40) | copy-start | bytes 388
  95.8 10.8 %copy-start.20 = (f32[16,2]{0,1:T(2,128)S(1)}, f32[16,2]{0,1:T(2,128)}, u32[]{:S(2)}) copy-start(f32[16,2]{0,1:T(2,128)} %param.41) | copy-start | bytes 388
  95.8 18.3 %all-to-all-start.2 = ((bf16[16,16,512]{2,1,0:T(8,128)(2,1)}), bf16[16,16,512]{2,1,0:T(8,128)(2,1)S(1)}, u32[]{:S(2)}, u32[]{:S(2)}) async-start(bf16[16,16,512]{2,1,0:T(8,128)(2,1)} %get-tuple-element.32), calls=%async_computation.2 | async-start | bytes 524288 | tf_op jit(solution)/shard_map/all_to_all | solution.py:503

commit v4 on v3

--- a/solution.py
+++ b/solution.py
@@ -71,22 +71,17 @@
     return found
 
 
-def _levels(slots, requests):
-    found = [jnp.int32(0)] * MIG
-    for a, _, arrived, order in slots:
-        found = [jnp.where(arrived & (order == j), a // (requests * PLANE), found[j]) for j in range(MIG)]
-    return found
-
-
 def _pack_body(
-    requests, rep_ref, anchor_ref, table_ref, pool_ref, window_ref, scan_ref, hidden_ref, weight_ref, out_ref, token_ref,
+    requests, rep_ref, anchor_ref, table_ref, pool_ref, window_ref, scan_ref, hidden_ref, weight_ref, out_ref, keep_ref, send_ref,
     scans_ref, pages_ref, win_ref, rows_ref, blocks_ref, sems,
 ):
     pages = table_ref.shape[0]
     taps, _, channels = window_ref.shape
     blocks = channels // LANES
-    plane = out_ref.shape[0]
+    plane = PLANE
     width = weight_ref.shape[2] // plane
+    r = rep_ref[0]
+    x, core = (r // 2) % 4, r % 2
     copies = [
         pltpu.make_async_copy(hidden_ref.at[0], rows_ref, sems.at[0]),
         pltpu.make_async_copy(window_ref, win_ref, sems.at[1]),
@@ -110,39 +105,45 @@
             )
             copies[-1].start()
     weights = []
-    for f in range(plane):
+    order = (4, 5, 6, 7, 0, 1, 2, 3)
+    for f, p in enumerate(order):
+        block = ((x + p) % 4) * 2 + (core + p // 4) % 2
+        columns = pl.ds(pl.multiple_of(block * width, width), width)
         weights.append(
-            pltpu.make_async_copy(
-                weight_ref.at[0, :, pl.ds(f * width, width)], blocks_ref.at[f], sems.at[len(copies) + f]
-            )
+            pltpu.make_async_copy(weight_ref.at[0, :, columns], blocks_ref.at[f], sems.at[len(copies) + f])
         )
         weights[-1].start()
     for copy in copies:
         copy.wait()
     row = lax.broadcasted_iota(jnp.int32, (requests, channels), 0)
+    wins = []
     for j, o in enumerate(leaving):
-        scan = scans_ref[j]
         lines = [
             jnp.sum(jnp.where(row == o, win_ref[t].astype(F32), 0.0), axis=0, keepdims=True) for t in range(taps)
         ]
-        win = jnp.concatenate([*lines, jnp.zeros((SUB - taps, channels), F32)], axis=0)
-        for i in range(plane):
-            b, h = i // 2, i % 2
-            head = scan[h * SUB : (h + 1) * SUB, b * LANES : (b + 1) * LANES]
-            tail = win[:, i * LANES : (i + 1) * LANES] if i < blocks else jnp.zeros((SUB, LANES), F32)
-            for c in range(2):
-                out_ref[i, 3 * j + c] = pages_ref[j, i, c]
-            out_ref[i, 3 * j + 2] = jnp.concatenate([head, tail], axis=0).astype(BF16)
+        wins.append([line[:, b * LANES : (b + 1) * LANES] for line in lines for b in range(blocks)])
+    rows_each = scans_ref.shape[1] * blocks // out_ref.shape[0]
+    per_block = scans_ref.shape[1] // rows_each
+    blank = jnp.zeros((1, LANES), F32)
+    for i in range(out_ref.shape[0]):
+        b, q = i // per_block, i % per_block
+        tail = []
+        for j in range(MIG):
+            tail.append(scans_ref[j, q * rows_each : (q + 1) * rows_each, b * LANES : (b + 1) * LANES])
+            tail.append(wins[j][i] if i < len(wins[j]) else blank)
+            tail.extend([blank] * (SUB // MIG - rows_each - 1))
+        m, c, h = i // 4, i // 2 % 2, i % 2
+        heads = [pages_ref[j, m, c].astype(F32)[h * SUB : (h + 1) * SUB] for j in range(MIG)]
+        out_ref[i] = jnp.concatenate([*heads, *tail], axis=0).astype(BF16)
     hidden = rows_ref[...]
-    for f in range(plane):
+    for f, p in enumerate(order):
         weights[f].wait()
-        total = jnp.dot(hidden, blocks_ref[f], preferred_element_type=F32).astype(BF16)
-        for q in range(hidden.shape[0] // ROWS):
-            for b in range(width // LANES):
-                out_ref[f, 3 * MIG + q * (width // LANES) + b] = total[
-                    q * ROWS : (q + 1) * ROWS, b * LANES : (b + 1) * LANES
-                ]
-    token_ref[...] = jnp.zeros_like(token_ref)
+        total = jnp.dot(hidden, blocks_ref[f], preferred_element_type=F32)
+        at = slice(p % 4 * width, (p % 4 + 1) * width)
+        if p < 4:
+            keep_ref[:, at] = total
+        else:
+            send_ref[:, at] = total.astype(BF16)
 
 
 def _route_body(requests, anchor_ref, dep_ref, out_ref):
@@ -166,29 +167,33 @@
     out_ref[...] = jnp.where(lane == 0, one, jnp.where(lane == 1, two, 0.0)).astype(jnp.int32)
 
 
-def _select_body(index_ref, in_ref, out_ref):
-    replicas, tiles = out_ref.shape[0], out_ref.shape[1]
-    plane = in_ref.shape[0]
-    cap = 4
-    blocks = ROWS // cap
+def _fold_body(keep_ref, got_ref, o0, o1, o2, o3):
+    width = o0.shape[1]
+    for k, o in enumerate((o0, o1, o2, o3)):
+        at = slice(k * width, (k + 1) * width)
+        o[...] = (keep_ref[:, at] + got_ref[:, at].astype(F32)).astype(o.dtype)
+
+
+def _select_body(index_ref, in_ref, e0, e1, e2, e3, dep_ref, out_ref):
+    replicas = out_ref.shape[0]
+    row = lax.broadcasted_iota(jnp.int32, (SUB, LANES), 0)
+    half = SUB // MIG
+    cap = e0.shape[0] // replicas
+    blocks = e0.shape[1] // LANES
+    total = (e0[...] + e1[...].astype(F32)) + (e2[...].astype(F32) + e3[...].astype(F32))
     for d in range(replicas):
+        heads, tails = [], []
         for j in range(MIG):
             i = index_ref[d, j]
-            member = (i // MIG) % plane
-            for k in range(3):
-                out_ref[d, 3 * j + k] = in_ref[member, 3 * (i % MIG) + k]
-    for q in range(replicas // blocks):
-        totals = []
-        for b in range(blocks):
-            at = 3 * MIG + q * blocks + b
-            total = in_ref[0, at].astype(F32)
-            for p in range(1, plane):
-                total = total + in_ref[p, at].astype(F32)
-            totals.append(total)
-        for n in range(blocks):
-            out_ref[q * blocks + n, tiles - 1] = jnp.concatenate(
-                [total[n * cap : (n + 1) * cap] for total in totals], axis=0
-            ).astype(BF16)
+            rank = i % MIG
+            item = in_ref[i // MIG].astype(F32)
+            heads.append(jnp.where(rank == 0, item[0:SUB], item[SUB : 2 * SUB]))
+            tail = item[2 * SUB : 3 * SUB]
+            tails.append(jnp.where(rank == j, tail, pltpu.roll(tail, half, 0)))
+        tail = jnp.where(row < half, tails[0], tails[1])
+        rows = total[d * cap : (d + 1) * cap]
+        experts = [rows[:, b * LANES : (b + 1) * LANES] for b in range(blocks)]
+        out_ref[d] = jnp.concatenate([*heads, tail, *experts], axis=0).astype(BF16)
 
 
 def _local_body(
@@ -203,10 +208,9 @@
     col_w = lax.broadcasted_iota(jnp.int32, which_ref.shape, 1)
     pick = jnp.zeros((requests, requests), F32)
     which = jnp.zeros(which_ref.shape, F32)
-    for g, (a, local, arrived, order) in enumerate(_slots(rep_ref, anchor_ref, requests)):
+    for g, (_, local, arrived, order) in enumerate(_slots(rep_ref, anchor_ref, requests)):
         pick = jnp.where((row == g) & (col == local) & ~arrived, 1.0, pick)
-        level = a // (requests * PLANE)
-        which = jnp.where((row_w == g) & (col_w == level * MIG + order) & arrived, 1.0, which)
+        which = jnp.where((row_w == g) & (col_w == order) & arrived, 1.0, which)
     pick = pick.astype(BF16)
     mixed = conv_ref[...].astype(F32) * weights[taps : taps + 1] + bias_ref[...]
     for t in range(taps):
@@ -223,14 +227,13 @@
     weights = taps_ref[...]
     taps = weights.shape[0] - 1
     mixed = base_ref[...]
-    levels = moved_ref.shape[0] // PLANE
-    for z in range(levels):
-        for j in range(MIG):
+    for j in range(MIG):
+        for t in range(taps):
             for b in range(blocks):
-                tile = moved_ref[z * PLANE + b, 3 * j + 2].astype(F32)
-                win_ref[:, b * LANES : (b + 1) * LANES] = tile[SUB : 2 * SUB]
-            line = jnp.sum(win_ref[0:taps, :] * weights[0:taps], axis=0, keepdims=True)
-            mixed = mixed + which_ref[:, z * MIG + j : z * MIG + j + 1] * line
+                at = 2 * SUB + j * (SUB // MIG) + 2
+                win_ref[t : t + 1, b * LANES : (b + 1) * LANES] = moved_ref[t * blocks + b].astype(F32)[at : at + 1]
+        line = jnp.sum(win_ref[0:taps, :] * weights[0:taps], axis=0, keepdims=True)
+        mixed = mixed + which_ref[:, j : j + 1] * line
     act = mixed * (1.0 / (1.0 + jnp.exp(-mixed)))
     act_ref[...] = act
     turn = (((1,), (1,)), ((), ()))
@@ -243,9 +246,9 @@
     experts = out_ref.shape[0]
     sums = []
     for r in range(PLANE):
-        total = moved_ref[r, 3 * MIG].astype(F32)
-        for z in range(1, levels):
-            total = total + moved_ref[z * PLANE + r, 3 * MIG].astype(F32)
+        total = moved_ref[r].astype(F32)[3 * SUB :]
+        for z in range(1, moved_ref.shape[0] // PLANE):
+            total = total + moved_ref[z * PLANE + r].astype(F32)[3 * SUB :]
         sums.append(total)
     empty = jnp.zeros((requests - SUB, LANES), F32)
     for e in range(experts):
@@ -260,11 +263,15 @@
     share_out_ref, arr_ref, count_ref,
 ):
     slots = _slots(rep_ref, anchor_ref, requests)
-    for j, level in enumerate(_levels(slots, requests)):
-        for i in range(PLANE):
-            b, h = i // 2, i % 2
-            tile = moved_ref[level * PLANE + i, 3 * j + 2].astype(F32)
-            arr_ref[j, h * SUB : (h + 1) * SUB, b * LANES : (b + 1) * LANES] = tile[0:SUB]
+    blocks = act_ref.shape[1] // LANES
+    rows_each = states * blocks // moved_ref.shape[0]
+    per_block = states // rows_each
+    for i in range(moved_ref.shape[0]):
+        b, q = i // per_block, i % per_block
+        tail = moved_ref[i].astype(F32)[2 * SUB : 3 * SUB]
+        for j in range(MIG):
+            at = j * (SUB // MIG)
+            arr_ref[j, q * rows_each : (q + 1) * rows_each, b * LANES : (b + 1) * LANES] = tail[at : at + rows_each]
     for g, (_, local, arrived, order) in enumerate(slots):
         old_ref[g] = jnp.where(arrived, arr_ref[order], scan_ref[local])
     rate_ref[...] = -jnp.exp(decay_ref[...])
@@ -358,15 +365,19 @@
     at = lax.broadcasted_iota(jnp.int32, (requests, MIG * span), 1)
     seen_moved = (at // span == order) & (at % span < live)
     down = lax.broadcasted_iota(jnp.int32, (span, head), 0)
-    for j, level in enumerate(_levels(slots, requests)):
+    for i in range(moved_ref.shape[0]):
+        m, c, h = i // 4, i // 2 % 2, i % 2
+        item = moved_ref[i].astype(F32)
+        ref = (keys_ref, values_ref)[c]
+        for j in range(MIG):
+            start = j * span + m * page + h * SUB
+            ref[start : start + SUB, :] = item[j * SUB : (j + 1) * SUB]
+    for j in range(MIG):
         for c, ref in ((0, keys_ref), (1, values_ref)):
-            for m in range(pages):
-                start = j * span + m * page
-                ref[start : start + page, :] = moved_ref[level * PLANE + m, 3 * j + c]
-            block = ref[j * span : (j + 1) * span, :].astype(F32)
+            block = ref[j * span : (j + 1) * span, :]
             pages_ref[j, 0, c] = jnp.where(down < live_of[j], block, 0.0).astype(BF16)
-    moved_keys = keys_ref[...]
-    moved_values = values_ref[...]
+    moved_keys = keys_ref[...].astype(BF16)
+    moved_values = values_ref[...].astype(BF16)
     pool_keys = pool_ref[:, 0, 0].reshape(pool * page, head)
     pool_values = pool_ref[:, 0, 1].reshape(pool * page, head)
     query = query_ref[...]
@@ -434,13 +445,16 @@
     table = block_table.T
     window = jnp.transpose(window_state, (1, 0, 2))
 
-    tiles = 3 * MIG + slots * features // (PLANE * ROWS * LANES)
-    packed, token = _call(
+    packed, keep, send = _call(
         lambda *refs: _pack_body(requests, *refs),
         "pack_leaving",
-        [_shape((PLANE, tiles, ROWS, LANES), BF16), _shape((SUB, LANES), F32)],
+        [
+            _shape((replicas, 3 * SUB, LANES), BF16),
+            _shape((slots, features // 2), F32),
+            _shape((slots, features // 2), BF16),
+        ],
         [_smem()] * 3 + [_hbm()] * 5,
-        [_vmem()] * 2,
+        [_vmem()] * 3,
         (rep, anchor, table, page_pool, window, scan_state, expert_hidden, down_weight),
         scratch=[
             pltpu.VMEM((MIG, states, channels), F32),
@@ -453,8 +467,26 @@
         us=4,
         room=60,
     )
-    planes = [[z * PLANE + i for i in range(PLANE)] for z in range(replicas // PLANE)]
-    spread = lax.all_to_all(packed, "rep", split_axis=0, concat_axis=0, tiled=True, axis_index_groups=planes)
+    spread = lax.all_to_all(packed, "rep", split_axis=0, concat_axis=0, tiled=True)
+
+    def at(z, x, c):
+        return (z * 4 + x) * 2 + c
+
+    every = [(z, x, c) for z in range(4) for x in range(4) for c in range(2)]
+    got = lax.ppermute(send, "rep", [(at(z, x, c), at(z, x, 1 - c)) for z, x, c in every])
+    width = features // PLANE
+    by_x = _call(
+        _fold_body,
+        "fold_cores",
+        [_shape((slots, width), F32)] + [_shape((slots, width), BF16)] * 3,
+        [_vmem()] * 2,
+        [_vmem()] * 4,
+        (keep, got),
+        us=0.5,
+    )
+    came = [by_x[0]] + [
+        lax.ppermute(by_x[k], "rep", [(at(z, x, c), at(z, (x + k) % 4, c)) for z, x, c in every]) for k in (2, 1, 3)
+    ]
 
     index = _call(
         lambda *refs: _route_body(requests, *refs),
@@ -462,20 +494,9 @@
         _shape((replicas, LANES), jnp.int32),
         [_vmem(), _any()],
         _vmem(),
-        (anchor.reshape(replicas, requests), token),
+        (anchor.reshape(replicas, requests), by_x[0]),
         us=1,
     )
-    onward = _call(
-        _select_body,
-        "select_pieces",
-        _shape((replicas, 3 * MIG + 1, ROWS, LANES), BF16),
-        [_smem(), _vmem()],
-        _vmem(),
-        (index, spread),
-        us=1.5,
-    )
-    moved = lax.all_to_all(onward, "rep", split_axis=0, concat_axis=0, tiled=True)
-
     base, which, taps, mix = _call(
         lambda *refs: _local_body(requests, *refs),
         "filter_local",
@@ -490,6 +511,17 @@
         (rep, anchor, window, conv_input, filter_taps, filter_bias.reshape(1, channels), mix_weight.T, index),
         us=1.5,
     )
+    onward = _call(
+        _select_body,
+        "select_pieces",
+        _shape((replicas, 3 * SUB + ROWS, LANES), BF16),
+        [_smem()] + [_vmem()] * 5 + [_any()],
+        _vmem(),
+        (index, spread, *came, which),
+        us=1.5,
+    )
+    moved = lax.all_to_all(onward, "rep", split_axis=0, concat_axis=0, tiled=True)
+
     sums, act = _call(
         _act_body,
         "filter_and_project",
@@ -509,7 +541,7 @@
         [_smem()] * 3 + [_vmem()] * 6 + [_any()],
         [_vmem()] * 2,
         (rep, anchor, lengths, table, query, new_key, new_value, page_pool, moved, act),
-        scratch=[pltpu.VMEM((MIG * pages * page, head), BF16)] * 2,
+        scratch=[pltpu.VMEM((MIG * pages * page, head), F32)] * 2,
         us=2,
     )
     ready = _call(

time: 116 us -> 107 us (0.922)
  waiting for transfers between devices: 68.8 us -> 11.1 us
  blocking collectives: 0 us -> 36.7 us
  starting transfers between devices: 31.3 us -> 43.5 us
  local copies, waits for them, and re-layouts: 0.19 us -> 1.39 us
    all_to_all x2 -> x1, waiting for transfers between devices: 62.4 us -> 0.74 us  [per_device(): lax.all_to_all(packed, 'rep', split_axis=0, concat_axis=0, tiled=True)]
    all_to_all x0 -> x1, blocking collectives: none -> 36.7 us  [per_device(): lax.all_to_all(onward, 'rep', split_axis=0, concat_axis=0, tiled=True)]
    ppermute x0 -> x4, starting transfers between devices: none -> 13.6 us  [the longest x3 11.3 us: per_device(): lax.ppermute(by_x[k], 'rep', [(at(z, x, c), at(z, (x + k) % 4, c)) for z,...]
    all_to_all x2 -> x1, starting transfers between devices: 22.7 us -> 19.4 us  [per_device(): lax.all_to_all(packed, 'rep', split_axis=0, concat_axis=0, tiled=True)]
    ppermute x0 -> x4, waiting for transfers between devices: none -> 2.63 us  [the longest x1 1.86 us: per_device(): lax.ppermute(send, 'rep', [(at(z, x, c), at(z, x, 1 - c)) for z, x, c in...]
    all_to_all x1, starting transfers between devices: 8.68 us -> 10.6 us  [per_device(): lax.all_to_all(sums, 'exp', split_axis=0, concat_axis=0, tiled=True)]
    all_to_all x1, waiting for transfers between devices: 6.45 us -> 7.76 us  [per_device(): lax.all_to_all(sums, 'exp', split_axis=0, concat_axis=0, tiled=True)]
    unnamed x42, local copies, waits for them, and re-layouts: 0.11 us -> 1.32 us
  transfers between devices with their start and end apart: 3 -> 6, of which waited for: 3 -> 4; matrix products, arithmetic and copies ran while one was open for 0% -> 0% of each run, Pallas kernels for 4% -> 4%
where the time goes in v4:
time: 107 us; the launch traced here: 106 us
  starting transfers between devices  43.5 us (41%)
  blocking collectives  36.7 us (34%)
  Pallas kernels  12.7 us (12%)
  waiting for transfers between devices  11.1 us (10%)
  local copies, waits for them, and re-layouts  1.39 us (1%)
    all_to_all x1, blocking collectives, per_device(): lax.all_to_all(onward, 'rep', split_axis=0, concat_axis=0, tiled=True)  36.7 us
    all_to_all x1, starting transfers between devices, per_device(): lax.all_to_all(packed, 'rep', split_axis=0, concat_axis=0, tiled=True)  19.4 us
    pallas_call x9, Pallas kernels, _call(): pl.pallas_call(body, name=name, out_shape=out_shape, in_specs=ins, out_sp...  12.7 us
    ppermute x3, starting transfers between devices, per_device(): lax.ppermute(by_x[k], 'rep', [(at(z, x, c), at(z, (x + k) % 4, c)) for z,...  11.3 us
    all_to_all x1, starting transfers between devices, per_device(): lax.all_to_all(sums, 'exp', split_axis=0, concat_axis=0, tiled=True)  10.6 us
    all_to_all x1, waiting for transfers between devices, per_device(): lax.all_to_all(sums, 'exp', split_axis=0, concat_axis=0, tiled=True)  7.76 us
    ppermute x1, starting transfers between devices, per_device(): lax.ppermute(send, 'rep', [(at(z, x, c), at(z, x, 1 - c)) for z, x, c in...  2.28 us
  transfers between devices with their start and end apart: 6, of which 4 were waited for; matrix products, arithmetic and copies ran while one was open for 0% of the time, Pallas kernels for 4%

profile of v4, /device:TPU:1, one launch (start us, length us, event | category | flops | bytes accessed | tf_op | source)
XLA Modules:
  0.0 106.4 jit_solution(9935611170079981003)
XLA Ops:
  0.6 0.0 copy-start.6
  0.7 0.0 copy-start.3
  0.7 0.0 copy-start.5
  0.7 0.0 copy-start.10
  0.7 0.0 copy-start.12
  0.7 0.0 copy-start.15
  0.7 0.0 copy-start.9
  0.7 0.0 copy-start.11
  0.7 0.0 copy-start.13
  0.7 0.0 copy-start.14
  0.7 0.0 copy-start.16
  0.8 0.0 copy-start.4
  0.8 0.0 copy-start.7
  0.8 0.0 copy-start.8
  0.8 0.0 copy-start.17
  0.8 0.0 copy-start.18
  0.8 0.0 copy-start.20
  0.8 5.5 %pack_leaving.1 = (bf16[32,24,128]{2,1,0:T(8,128)(2,1)}, f32[128,2048]{1,0:T(8,128)}, bf16[128,2048]{1,0:T(8,128)(2,1)}) custom-call(s32[1]{0:T(128)} %bitcast.refs_0_, s32[512]{0:T(512)} %refs_1_.7, s32[8,16]{1,0:T(8,128)} %bitcast.12, bf16[48,1,2,16,128]{4,3,2,1,0:T(8,128)(2,1)} %refs_7_.4, bf16[3,16,512]{2,1,0:T(8,128)(2,1)} %bitcast.10, ...), custom_call_target="tpu_custom_call" | custom-call | bytes 14000000 | tf_op jit(solution)/shard_map/pack_leaving/pallas_call | solution.py:40
  6.3 0.0 copy-start.1
  6.3 0.0 copy-start.19
  6.3 19.4 %all-to-all-start = ((bf16[32,24,128]{2,1,0:T(8,128)(2,1)}), bf16[32,24,128]{2,1,0:T(8,128)(2,1)S(1)}, u32[]{:S(2)}, u32[]{:S(2)}) async-start(bf16[32,24,128]{2,1,0:T(8,128)(2,1)} %get-tuple-element.31), calls=%async_computation | async-start | bytes 393216 | tf_op jit(solution)/shard_map/all_to_all | solution.py:470
  25.7 0.0 copy-start
  25.7 2.3 %collective-permute-start = (bf16[128,2048]{1,0:T(8,128)(2,1)}, bf16[128,2048]{1,0:T(8,128)(2,1)S(1)}, u32[]{:S(2)}, u32[]{:S(2)}) collective-permute-start(bf16[128,2048]{1,0:T(8,128)(2,1)} %get-tuple-element.29), channel_id=1, source_target_pairs={{0,16},{16,0},{32,48},{48,32},{64,80},{80,64},{96,112},{112,96},{1... | collective-permute-start | bytes 1572872 | tf_op jit(solution)/shard_map/ppermute | solution.py:476
  28.0 1.9 %collective-permute-done.got_ref = bf16[128,2048]{1,0:T(8,128)(2,1)S(1)} collective-permute-done((bf16[128,2048]{1,0:T(8,128)(2,1)}, bf16[128,2048]{1,0:T(8,128)(2,1)S(1)}, u32[]{:S(2)}, u32[]{:S(2)}) %collective-permute-start) | collective-permute-done | bytes 524320 | tf_op jit(solution)/shard_map/ppermute | solution.py:476
  29.9 1.2 %copy-done.2 = f32[128,2048]{1,0:T(8,128)S(1)} copy-done((f32[128,2048]{1,0:T(8,128)S(1)}, f32[128,2048]{1,0:T(8,128)}, u32[]{:S(2)}) %copy-start.2) | copy-done | bytes 1048600
  31.1 0.1 fold_cores.1
  31.2 4.8 %collective-permute-start.1 = (bf16[128,512]{1,0:T(8,128)(2,1)S(1)}, bf16[128,512]{1,0:T(8,128)(2,1)S(1)}, u32[]{:S(2)}, u32[]{:S(2)}) collective-permute-start(bf16[128,512]{1,0:T(8,128)(2,1)S(1)} %get-tuple-element.32), channel_id=1, source_target_pairs={{0,64},{16,80},{32,96},{48,112},{64,0},{80,16},{96,32},{112,48},{1... | collective-permute-start | bytes 393224 | tf_op jit(solution)/shard_map/ppermute | solution.py:488
  36.0 2.2 %collective-permute-start.2 = (bf16[128,512]{1,0:T(8,128)(2,1)S(1)}, bf16[128,512]{1,0:T(8,128)(2,1)S(1)}, u32[]{:S(2)}, u32[]{:S(2)}) collective-permute-start(bf16[128,512]{1,0:T(8,128)(2,1)S(1)} %get-tuple-element.33), channel_id=1, source_target_pairs={{0,32},{16,48},{32,64},{48,80},{64,96},{80,112},{96,0},{112,16},{1... | collective-permute-start | bytes 393224 | tf_op jit(solution)/shard_map/ppermute | solution.py:488
  38.2 4.3 %collective-permute-start.3 = (bf16[128,512]{1,0:T(8,128)(2,1)S(1)}, bf16[128,512]{1,0:T(8,128)(2,1)S(1)}, u32[]{:S(2)}, u32[]{:S(2)}) collective-permute-start(bf16[128,512]{1,0:T(8,128)(2,1)S(1)} %get-tuple-element.34), channel_id=1, source_target_pairs={{0,96},{16,112},{32,0},{48,16},{64,32},{80,48},{96,64},{112,80},{1... | collective-permute-start | bytes 393224 | tf_op jit(solution)/shard_map/ppermute | solution.py:488
  42.5 0.0 copy-done.6
  42.5 0.1 reshape.24.refs_0_
  42.6 0.2 route_pieces.1.refs_7_.index_ref
  42.8 0.0 copy-done.3
  42.8 0.0 copy-done.5
  42.8 0.0 copy-done.10
  42.8 0.0 copy-done.12
  42.8 0.0 copy-done.15
  42.9 0.8 filter_local.1
  43.7 0.0 collective-permute-done.1.e1
  43.7 0.0 collective-permute-done.2.e2
  43.7 0.8 collective-permute-done.3.e3
  44.4 0.7 all-to-all-done.in_ref
  45.2 1.3 %select_pieces.1 = bf16[32,40,128]{2,1,0:T(8,128)(2,1)S(1)} custom-call(s32[32,128]{1,0:T(8,128)S(1)} %route_pieces.1.refs_7_.index_ref, bf16[32,24,128]{2,1,0:T(8,128)(2,1)S(1)} %all-to-all-done.in_ref, f32[128,512]{1,0:T(8,128)S(1)} %get-tuple-element.30.refs_1_.e0, bf16[128,512]{1,0:T(8,128)(2,1)S(1)} %collective-permute-done.1.e1, ...), custom_call_target="tpu_custom_call" | custom-call | bytes 5250000 | tf_op jit(solution)/shard_map/select_pieces/pallas_call | solution.py:40
  46.4 36.7 %all_to_all.15.moved_ref.refs_8_.refs_4_ = bf16[32,40,128]{2,1,0:T(8,128)(2,1)S(1)} all-to-all(bf16[32,40,128]{2,1,0:T(8,128)(2,1)S(1)} %select_pieces.1), channel_id=1, replica_groups=mesh['rep'=32,'exp'=16] {'rep'}, dimensions={0} | all-to-all | bytes 655360 | tf_op jit(solution)/shard_map/all_to_all | solution.py:523
  83.1 1.0 filter_and_project.1
  84.1 10.6 %all-to-all-start.2 = ((bf16[16,16,512]{2,1,0:T(8,128)(2,1)}), bf16[16,16,512]{2,1,0:T(8,128)(2,1)S(1)}, u32[]{:S(2)}, u32[]{:S(2)}) async-start(bf16[16,16,512]{2,1,0:T(8,128)(2,1)} %get-tuple-element.42), calls=%async_computation.2 | async-start | bytes 524288 | tf_op jit(solution)/shard_map/all_to_all | solution.py:535
  94.7 0.0 copy-done.9
  94.7 0.0 copy-done.11
  94.7 0.0 copy-done.13
  94.7 0.0 copy-done.14
  94.7 0.0 copy-done.16
  94.8 0.0 copy-done.1
  94.8 1.9 %attend.1 = (bf16[16,512]{1,0:T(8,128)(2,1)}, bf16[2,1,2,128,128]{4,3,2,1,0:T(8,128)(2,1)}) custom-call(s32[1]{0:T(128)} %bitcast.refs_0_, s32[512]{0:T(512)S(1)} %copy-done.6, s32[512]{0:T(512)S(1)} %copy-done.16, s32[8,16]{1,0:T(8,128)S(1)} %bitcast.13, bf16[16,512]{1,0:T(8,128)(2,1)S(1)} %copy-done.11, bf16[16,128]{1,0:T(8,128)(2,1)S(1)} %copy-done.13, ...), custom_call_target="tpu_custom_call" | custom-call | bytes 7000000 | tf_op jit(solution)/shard_map/attend/pallas_call | solution.py:40
  96.7 0.0 copy-done.4
  96.7 0.0 copy-done.7
  96.7 0.0 copy-done.8
  96.7 0.0 copy-done.17
  96.7 0.0 copy-done.18
  96.7 0.0 copy-done.20
  96.7 0.0 copy-done.19
  96.7 0.0 copy-done
  96.8 0.9 ready_state.1
  97.6 7.8 %all-to-all-done.2.refs_0_ = bf16[16,16,512]{2,1,0:T(8,128)(2,1)S(1)} async-done(((bf16[16,16,512]{2,1,0:T(8,128)(2,1)}), bf16[16,16,512]{2,1,0:T(8,128)(2,1)S(1)}, u32[]{:S(2)}, u32[]{:S(2)}) %all-to-all-start.2) | async-done | bytes 262176 | tf_op jit(solution)/shard_map/all_to_all | solution.py:535
  105.4 1.1 update_state.1
  (1 shorter events, 0.0 us)
Async XLA Ops:
  0.6 41.9 %copy-start.6 = (s32[512]{0:T(512)S(1)}, s32[512]{0:T(512)}, u32[]{:S(2)}) copy-start(s32[512]{0:T(512)} %refs_1_.7) | copy-start | bytes 6148
  0.7 42.2 %copy-start.3 = (bf16[512,288]{0,1:T(8,128)(2,1)S(1)}, bf16[512,288]{0,1:T(8,128)(2,1)}, u32[]{:S(2)}) copy-start(bf16[512,288]{0,1:T(8,128)(2,1)} %param.35) | copy-start | bytes 884740
  0.7 42.2 %copy-start.5 = (bf16[16,3,512]{2,0,1:T(8,128)(2,1)S(1)}, bf16[16,3,512]{2,0,1:T(8,128)(2,1)}, u32[]{:S(2)}) copy-start(bf16[16,3,512]{2,0,1:T(8,128)(2,1)} %param.31) | copy-start | bytes 147460
  0.7 42.2 %copy-start.10 = (bf16[16,512]{1,0:T(8,128)(2,1)S(1)}, bf16[16,512]{1,0:T(8,128)(2,1)}, u32[]{:S(2)}) copy-start(bf16[16,512]{1,0:T(8,128)(2,1)} %refs_3_.3) | copy-start | bytes 49156
  0.7 42.2 %copy-start.12 = (f32[4,512]{1,0:T(4,128)S(1)}, f32[4,512]{1,0:T(4,128)}, u32[]{:S(2)}) copy-start(f32[4,512]{1,0:T(4,128)} %refs_4_.2) | copy-start | bytes 24580
  0.7 42.2 %copy-start.15 = (f32[512]{0:T(512)S(1)}, f32[512]{0:T(512)}, u32[]{:S(2)}) copy-start(f32[512]{0:T(512)} %param.34) | copy-start | bytes 6148
  0.7 94.0 %copy-start.9 = (s32[16,8]{0,1:T(8,128)S(1)}, s32[16,8]{0,1:T(8,128)}, u32[]{:S(2)}) copy-start(s32[16,8]{0,1:T(8,128)} %param.26) | copy-start | bytes 1540
  0.7 94.0 %copy-start.11 = (bf16[16,512]{1,0:T(8,128)(2,1)S(1)}, bf16[16,512]{1,0:T(8,128)(2,1)}, u32[]{:S(2)}) copy-start(bf16[16,512]{1,0:T(8,128)(2,1)} %refs_4_.3) | copy-start | bytes 49156
  0.7 94.0 %copy-start.13 = (bf16[16,128]{1,0:T(8,128)(2,1)S(1)}, bf16[16,128]{1,0:T(8,128)(2,1)}, u32[]{:S(2)}) copy-start(bf16[16,128]{1,0:T(8,128)(2,1)} %refs_5_.3) | copy-start | bytes 12292
  0.7 94.0 %copy-start.14 = (bf16[16,128]{1,0:T(8,128)(2,1)S(1)}, bf16[16,128]{1,0:T(8,128)(2,1)}, u32[]{:S(2)}) copy-start(bf16[16,128]{1,0:T(8,128)(2,1)} %refs_6_.4) | copy-start | bytes 12292
  0.7 94.0 %copy-start.16 = (s32[512]{0:T(512)S(1)}, s32[512]{0:T(512)}, u32[]{:S(2)}) copy-start(s32[512]{0:T(512)} %refs_2_.1) | copy-start | bytes 6148
  0.8 95.9 %copy-start.4 = (bf16[256,512]{1,0:T(8,128)(2,1)S(1)}, bf16[256,512]{1,0:T(8,128)(2,1)}, u32[]{:S(2)}) copy-start(bf16[256,512]{1,0:T(8,128)(2,1)} %refs_8_.1) | copy-start | bytes 786436
  0.8 95.9 %copy-start.7 = (f32[16,512]{1,0:T(8,128)S(1)}, f32[16,512]{1,0:T(8,128)}, u32[]{:S(2)}) copy-start(f32[16,512]{1,0:T(8,128)} %refs_10_.1) | copy-start | bytes 98308
  0.8 95.9 %copy-start.8 = (bf16[16,512]{1,0:T(8,128)(2,1)S(1)}, bf16[16,512]{1,0:T(8,128)(2,1)}, u32[]{:S(2)}) copy-start(bf16[16,512]{1,0:T(8,128)(2,1)} %refs_6_.5) | copy-start | bytes 49156
  0.8 95.9 %copy-start.17 = (f32[512]{0:T(512)S(1)}, f32[512]{0:T(512)}, u32[]{:S(2)}) copy-start(f32[512]{0:T(512)} %param.37) | copy-start | bytes 6148
  0.8 95.9 %copy-start.18 = (f32[512]{0:T(512)S(1)}, f32[512]{0:T(512)}, u32[]{:S(2)}) copy-start(f32[512]{0:T(512)} %param.39) | copy-start | bytes 6148
  0.8 95.9 %copy-start.20 = (f32[16,2]{0,1:T(2,128)S(1)}, f32[16,2]{0,1:T(2,128)}, u32[]{:S(2)}) copy-start(f32[16,2]{0,1:T(2,128)} %param.41) | copy-start | bytes 388
  6.3 88.4 %copy-start.1 = (bf16[48,1,2,16,128]{4,3,2,1,0:T(8,128)(2,1)S(1)}, bf16[48,1,2,16,128]{4,3,2,1,0:T(8,128)(2,1)}, u32[]{:S(2)}) copy-start(bf16[48,1,2,16,128]{4,3,2,1,0:T(8,128)(2,1)} %refs_7_.4) | copy-start | bytes 1179652
  6.3 90.4 %copy-start.19 = (s32[16,2]{0,1:T(2,128)S(1)}, s32[16,2]{0,1:T(2,128)}, u32[]{:S(2)}) copy-start(s32[16,2]{0,1:T(2,128)} %param.40) | copy-start | bytes 388
  6.3 38.8 %all-to-all-start = ((bf16[32,24,128]{2,1,0:T(8,128)(2,1)}), bf16[32,24,128]{2,1,0:T(8,128)(2,1)S(1)}, u32[]{:S(2)}, u32[]{:S(2)}) async-start(bf16[32,24,128]{2,1,0:T(8,128)(2,1)} %get-tuple-element.31), calls=%async_computation | async-start | bytes 393216 | tf_op jit(solution)/shard_map/all_to_all | solution.py:470
  25.7 71.1 %copy-start = (f32[16,16,512]{2,1,0:T(8,128)S(1)}, f32[16,16,512]{2,1,0:T(8,128)}, u32[]{:S(2)}) copy-start(f32[16,16,512]{2,1,0:T(8,128)} %refs_7_.5) | copy-start | bytes 1572868
  25.7 4.1 %collective-permute-start = (bf16[128,2048]{1,0:T(8,128)(2,1)}, bf16[128,2048]{1,0:T(8,128)(2,1)S(1)}, u32[]{:S(2)}, u32[]{:S(2)}) collective-permute-start(bf16[128,2048]{1,0:T(8,128)(2,1)} %get-tuple-element.29), channel_id=1, source_target_pairs={{0,16},{16,0},{32,48},{48,32},{64,80},{80,64},{96,112},{112,96},{1... | collective-permute-start | bytes 1572872 | tf_op jit(solution)/shard_map/ppermute | solution.py:476
  29.9 1.2 %copy-start.2 = (f32[128,2048]{1,0:T(8,128)S(1)}, f32[128,2048]{1,0:T(8,128)}, u32[]{:S(2)}) copy-start(f32[128,2048]{1,0:T(8,128)} %get-tuple-element.28.keep_ref) | copy-start | bytes 3145732
  31.2 12.5 %collective-permute-start.1 = (bf16[128,512]{1,0:T(8,128)(2,1)S(1)}, bf16[128,512]{1,0:T(8,128)(2,1)S(1)}, u32[]{:S(2)}, u32[]{:S(2)}) collective-permute-start(bf16[128,512]{1,0:T(8,128)(2,1)S(1)} %get-tuple-element.32), channel_id=1, source_target_pairs={{0,64},{16,80},{32,96},{48,112},{64,0},{80,16},{96,32},{112,48},{1... | collective-permute-start | bytes 393224 | tf_op jit(solution)/shard_map/ppermute | solution.py:488
  36.0 7.7 %collective-permute-start.2 = (bf16[128,512]{1,0:T(8,128)(2,1)S(1)}, bf16[128,512]{1,0:T(8,128)(2,1)S(1)}, u32[]{:S(2)}, u32[]{:S(2)}) collective-permute-start(bf16[128,512]{1,0:T(8,128)(2,1)S(1)} %get-tuple-element.33), channel_id=1, source_target_pairs={{0,32},{16,48},{32,64},{48,80},{64,96},{80,112},{96,0},{112,16},{1... | collective-permute-start | bytes 393224 | tf_op jit(solution)/shard_map/ppermute | solution.py:488
  38.2 6.3 %collective-permute-start.3 = (bf16[128,512]{1,0:T(8,128)(2,1)S(1)}, bf16[128,512]{1,0:T(8,128)(2,1)S(1)}, u32[]{:S(2)}, u32[]{:S(2)}) collective-permute-start(bf16[128,512]{1,0:T(8,128)(2,1)S(1)} %get-tuple-element.34), channel_id=1, source_target_pairs={{0,96},{16,112},{32,0},{48,16},{64,32},{80,48},{96,64},{112,80},{1... | collective-permute-start | bytes 393224 | tf_op jit(solution)/shard_map/ppermute | solution.py:488
  84.1 21.3 %all-to-all-start.2 = ((bf16[16,16,512]{2,1,0:T(8,128)(2,1)}), bf16[16,16,512]{2,1,0:T(8,128)(2,1)S(1)}, u32[]{:S(2)}, u32[]{:S(2)}) async-start(bf16[16,16,512]{2,1,0:T(8,128)(2,1)} %get-tuple-element.42), calls=%async_computation.2 | async-start | bytes 524288 | tf_op jit(solution)/shard_map/all_to_all | solution.py:535

commit v5 on v4

--- a/solution.py
+++ b/solution.py
@@ -12,6 +12,7 @@
 SUB = 8
 ROWS = 16
 PLANE = 8
+FIRST = (16, 8, 8)
 F32 = jnp.float32
 BF16 = jnp.bfloat16
 
@@ -49,6 +50,10 @@
     )(*args)
 
 
+def _turned(size, first):
+    return [[(k + first) % size for k in range(size)]]
+
+
 def _present(anchor_ref, base, requests):
     mask = jnp.int32(0)
     for g in range(requests):
@@ -72,8 +77,8 @@
 
 
 def _pack_body(
-    requests, rep_ref, anchor_ref, table_ref, pool_ref, window_ref, scan_ref, hidden_ref, weight_ref, out_ref, keep_ref, send_ref,
-    scans_ref, pages_ref, win_ref, rows_ref, blocks_ref, sems,
+    requests, rep_ref, anchor_ref, table_ref, pool_ref, window_ref, scan_ref, hidden_ref, weight_ref,
+    out_ref, keep_ref, send_ref, scans_ref, pages_ref, win_ref, rows_ref, blocks_ref, sems,
 ):
     pages = table_ref.shape[0]
     taps, _, channels = window_ref.shape
@@ -82,12 +87,19 @@
     width = weight_ref.shape[2] // plane
     r = rep_ref[0]
     x, core = (r // 2) % 4, r % 2
-    copies = [
-        pltpu.make_async_copy(hidden_ref.at[0], rows_ref, sems.at[0]),
-        pltpu.make_async_copy(window_ref, win_ref, sems.at[1]),
-    ]
-    for copy in copies:
-        copy.start()
+    hidden_copy = pltpu.make_async_copy(hidden_ref.at[0], rows_ref, sems.at[plane])
+    hidden_copy.start()
+    weights = []
+    order = (4, 5, 6, 7, 0, 1, 2, 3)
+    for f, p in enumerate(order):
+        block = ((x + p) % 4) * 2 + (core + p // 4) % 2
+        columns = pl.ds(pl.multiple_of(block * width, width), width)
+        weights.append(
+            pltpu.make_async_copy(weight_ref.at[0, :, columns], blocks_ref.at[f], sems.at[f])
+        )
+        weights[-1].start()
+    copies = [pltpu.make_async_copy(window_ref, win_ref, sems.at[plane + 1])]
+    copies[0].start()
     base = rep_ref[0] * requests
     mask = _present(anchor_ref, base, requests)
     first, second = jnp.int32(0), jnp.int32(0)
@@ -97,22 +109,22 @@
         first = jnp.where(leaves, o, first)
     leaving = (first, second)
     for j, o in enumerate(leaving):
-        copies.append(pltpu.make_async_copy(scan_ref.at[o], scans_ref.at[j], sems.at[len(copies)]))
+        copies.append(pltpu.make_async_copy(scan_ref.at[o], scans_ref.at[j], sems.at[plane + 1 + len(copies)]))
         copies[-1].start()
         for m in range(pages):
-            copies.append(
-                pltpu.make_async_copy(pool_ref.at[table_ref[m, o], 0], pages_ref.at[j, m], sems.at[len(copies)])
-            )
+            page = pool_ref.at[table_ref[m, o], 0]
+            copies.append(pltpu.make_async_copy(page, pages_ref.at[j, m], sems.at[plane + 1 + len(copies)]))
             copies[-1].start()
-    weights = []
-    order = (4, 5, 6, 7, 0, 1, 2, 3)
+    hidden_copy.wait()
+    hidden = rows_ref[...]
     for f, p in enumerate(order):
-        block = ((x + p) % 4) * 2 + (core + p // 4) % 2
-        columns = pl.ds(pl.multiple_of(block * width, width), width)
-        weights.append(
-            pltpu.make_async_copy(weight_ref.at[0, :, columns], blocks_ref.at[f], sems.at[len(copies) + f])
-        )
-        weights[-1].start()
+        weights[f].wait()
+        total = jnp.dot(hidden, blocks_ref[f], preferred_element_type=F32)
+        at = slice(p % 4 * width, (p % 4 + 1) * width)
+        if p < 4:
+            keep_ref[:, at] = total.astype(BF16)
+        else:
+            send_ref[:, at] = total.astype(BF16)
     for copy in copies:
         copy.wait()
     row = lax.broadcasted_iota(jnp.int32, (requests, channels), 0)
@@ -134,16 +146,9 @@
             tail.extend([blank] * (SUB // MIG - rows_each - 1))
         m, c, h = i // 4, i // 2 % 2, i % 2
         heads = [pages_ref[j, m, c].astype(F32)[h * SUB : (h + 1) * SUB] for j in range(MIG)]
-        out_ref[i] = jnp.concatenate([*heads, *tail], axis=0).astype(BF16)
-    hidden = rows_ref[...]
-    for f, p in enumerate(order):
-        weights[f].wait()
-        total = jnp.dot(hidden, blocks_ref[f], preferred_element_type=F32)
-        at = slice(p % 4 * width, (p % 4 + 1) * width)
-        if p < 4:
-            keep_ref[:, at] = total
-        else:
-            send_ref[:, at] = total.astype(BF16)
+        for j in range(MIG):
+            out_ref[i, j] = heads[j].astype(BF16)
+        out_ref[i, MIG] = jnp.concatenate(tail, axis=0).astype(BF16)
 
 
 def _route_body(requests, anchor_ref, dep_ref, out_ref):
@@ -159,7 +164,8 @@
     lowest = jnp.zeros(anchors.shape, F32)
     for s in range(replicas):
         lowest = jnp.where(source == s, first[s : s + 1], lowest)
-    item = (source * MIG).astype(F32) + jnp.where(lowest != bit, 1.0, 0.0)
+    place_of = (source + replicas - FIRST[0]) % replicas
+    item = (place_of * MIG).astype(F32) + jnp.where(lowest != bit, 1.0, 0.0)
     early = jnp.min(jnp.where(arrived, place, 99.0), axis=1, keepdims=True)
     one = jnp.sum(jnp.where(arrived & (place == early), item, 0.0), axis=1, keepdims=True)
     two = jnp.sum(jnp.where(arrived & (place != early), item, 0.0), axis=1, keepdims=True)
@@ -171,29 +177,36 @@
     width = o0.shape[1]
     for k, o in enumerate((o0, o1, o2, o3)):
         at = slice(k * width, (k + 1) * width)
-        o[...] = (keep_ref[:, at] + got_ref[:, at].astype(F32)).astype(o.dtype)
-
-
-def _select_body(index_ref, in_ref, e0, e1, e2, e3, dep_ref, out_ref):
+        o[...] = (keep_ref[:, at].astype(F32) + got_ref[:, at].astype(F32)).astype(o.dtype)
+
+
+def _piece(i, replicas):
+    return (i + FIRST[0] - FIRST[1]) % replicas
+
+
+def _select_body(index_ref, in_ref, e0, e1, e2, e3, out_ref):
     replicas = out_ref.shape[0]
     row = lax.broadcasted_iota(jnp.int32, (SUB, LANES), 0)
     half = SUB // MIG
     cap = e0.shape[0] // replicas
     blocks = e0.shape[1] // LANES
     total = (e0[...] + e1[...].astype(F32)) + (e2[...].astype(F32) + e3[...].astype(F32))
-    for d in range(replicas):
-        heads, tails = [], []
+    for t in range(replicas):
+        d = (t + FIRST[1]) % replicas
+        tails = []
         for j in range(MIG):
             i = index_ref[d, j]
             rank = i % MIG
-            item = in_ref[i // MIG].astype(F32)
-            heads.append(jnp.where(rank == 0, item[0:SUB], item[SUB : 2 * SUB]))
-            tail = item[2 * SUB : 3 * SUB]
+            out_ref[t, j] = in_ref[i // MIG, rank]
+            tail = in_ref[i // MIG, MIG].astype(F32)
             tails.append(jnp.where(rank == j, tail, pltpu.roll(tail, half, 0)))
         tail = jnp.where(row < half, tails[0], tails[1])
         rows = total[d * cap : (d + 1) * cap]
         experts = [rows[:, b * LANES : (b + 1) * LANES] for b in range(blocks)]
-        out_ref[d] = jnp.concatenate([*heads, tail, *experts], axis=0).astype(BF16)
+        out_ref[t, MIG] = tail.astype(BF16)
+        for h in range(2):
+            pair = experts[h * blocks // 2 : (h + 1) * blocks // 2]
+            out_ref[t, MIG + 1 + h] = jnp.concatenate(pair, axis=0).astype(BF16)
 
 
 def _local_body(
@@ -230,8 +243,9 @@
     for j in range(MIG):
         for t in range(taps):
             for b in range(blocks):
-                at = 2 * SUB + j * (SUB // MIG) + 2
-                win_ref[t : t + 1, b * LANES : (b + 1) * LANES] = moved_ref[t * blocks + b].astype(F32)[at : at + 1]
+                at = j * (SUB // MIG) + 2
+                tile = moved_ref[_piece(t * blocks + b, moved_ref.shape[0]), MIG].astype(F32)
+                win_ref[t : t + 1, b * LANES : (b + 1) * LANES] = tile[at : at + 1]
         line = jnp.sum(win_ref[0:taps, :] * weights[0:taps], axis=0, keepdims=True)
         mixed = mixed + which_ref[:, j : j + 1] * line
     act = mixed * (1.0 / (1.0 + jnp.exp(-mixed)))
@@ -242,19 +256,23 @@
     high = partial.astype(BF16).astype(F32)
     low = (partial - high)[:, rank:]
     fill = jnp.zeros((requests, LANES - 2 * low.shape[1]), F32)
-    packed = jnp.concatenate([high[:, :rank], high[:, rank:], low, fill], axis=1)
-    experts = out_ref.shape[0]
-    sums = []
-    for r in range(PLANE):
-        total = moved_ref[r].astype(F32)[3 * SUB :]
-        for z in range(1, moved_ref.shape[0] // PLANE):
-            total = total + moved_ref[z * PLANE + r].astype(F32)[3 * SUB :]
-        sums.append(total)
-    empty = jnp.zeros((requests - SUB, LANES), F32)
-    for e in range(experts):
-        block = sums[e // 2][e % 2 * SUB : (e % 2 + 1) * SUB]
-        block = jnp.concatenate([block, empty], axis=0)
-        out_ref[e] = jnp.concatenate([packed, block], axis=1).astype(BF16)
+    tail = jnp.concatenate([high[:, rank:], low, fill], axis=1)
+    experts, replicas = out_ref.shape[0], moved_ref.shape[0]
+    lane = lax.broadcasted_iota(jnp.int32, (SUB, LANES), 1)
+    steps = [
+        high[h * SUB : (h + 1) * SUB, b * LANES : (b + 1) * LANES].astype(BF16) for h in range(2) for b in range(2)
+    ]
+    for f in range(PLANE):
+        for q in range(2):
+            block = moved_ref[(f - FIRST[1]) % replicas, MIG + 1 + q].astype(F32)
+            for z in range(1, replicas // PLANE):
+                block = block + moved_ref[(z * PLANE + f - FIRST[1]) % replicas, MIG + 1 + q].astype(F32)
+            e = (2 * f + q - FIRST[2]) % experts
+            for n, step in enumerate(steps):
+                out_ref[e, n] = step
+            for h, part in enumerate((pltpu.roll(block, LANES // 2, 1), block)):
+                rows = tail[h * SUB : (h + 1) * SUB]
+                out_ref[e, len(steps) + h] = jnp.where(lane < LANES // 2, rows, part).astype(BF16)
 
 
 def _ready_body(
@@ -268,7 +286,7 @@
     per_block = states // rows_each
     for i in range(moved_ref.shape[0]):
         b, q = i // per_block, i % per_block
-        tail = moved_ref[i].astype(F32)[2 * SUB : 3 * SUB]
+        tail = moved_ref[_piece(i, moved_ref.shape[0]), MIG].astype(F32)
         for j in range(MIG):
             at = j * (SUB // MIG)
             arr_ref[j, q * rows_each : (q + 1) * rows_each, b * LANES : (b + 1) * LANES] = tail[at : at + rows_each]
@@ -280,7 +298,8 @@
     skip_out_ref[...] = skip_ref[...] * act_ref[...]
     step_out_ref[...] = step_ref[...]
     bias_out_ref[...] = jnp.broadcast_to(bias_ref[...], bias_out_ref.shape)
-    for e in range(count_ref.shape[0]):
+    experts = count_ref.shape[0]
+    for e in range(experts):
         count_ref[e] = 0
     row = lax.broadcasted_iota(jnp.int32, (requests, LANES), 0)
     col = lax.broadcasted_iota(jnp.int32, (requests, LANES), 1)
@@ -290,7 +309,7 @@
             e = routes_ref[k, t]
             place = count_ref[e]
             count_ref[e] = place + 1
-            share = share + jnp.where((row == t) & (col == e * SUB + place), share_ref[k, t], 0.0)
+            share = share + jnp.where((row == t) & (col == (e + experts - FIRST[2]) % experts * SUB + place), share_ref[k, t], 0.0)
     share_out_ref[...] = share
 
 
@@ -298,14 +317,20 @@
     states, sums_ref, act_ref, old_ref, rate_ref, gate_ref, skip_ref, step_ref, bias_ref, share_ref,
     gated_ref, mix_ref, y_ref,
 ):
-    experts, requests, _ = sums_ref.shape
-    rank = 2 * LANES
-    projected = sums_ref[0, :, 0 : rank + LANES].astype(F32)
-    for e in range(1, experts):
-        projected = projected + sums_ref[e, :, 0 : rank + LANES].astype(F32)
-    step = jnp.dot(projected[:, :rank].astype(BF16), step_ref[...], preferred_element_type=F32) + bias_ref[0:1]
+    experts = sums_ref.shape[0]
+    requests, _ = act_ref.shape
+    totals = []
+    for n in range(sums_ref.shape[1]):
+        total = sums_ref[0, n].astype(F32)
+        for e in range(1, experts):
+            total = total + sums_ref[e, n].astype(F32)
+        totals.append(total)
+    projected = jnp.concatenate(
+        [jnp.concatenate(totals[0:2], axis=1), jnp.concatenate(totals[2:4], axis=1)], axis=0
+    )
+    step = jnp.dot(projected.astype(BF16), step_ref[...], preferred_element_type=F32) + bias_ref[0:1]
     step = jnp.maximum(step, 0.0) + jnp.log1p(jnp.exp(-jnp.abs(step)))
-    tail = projected[:, rank:]
+    tail = jnp.concatenate(totals[4:6], axis=0)
     columns = jnp.transpose(tail + pltpu.roll(tail, LANES - 2 * states, 1))
     rest = share_ref[...]
     parts = []
@@ -313,7 +338,12 @@
         part = rest.astype(BF16).astype(F32)
         parts.append(part)
         rest = rest - part
-    outs = sums_ref[:, :, rank + LANES :].astype(F32)[:, 0:SUB].reshape(experts * SUB, LANES).astype(BF16)
+    lane = lax.broadcasted_iota(jnp.int32, (SUB, LANES), 1)
+    outs = []
+    for e in range(experts):
+        left = pltpu.roll(sums_ref[e, 4].astype(F32), LANES // 2, 1)
+        outs.append(jnp.where(lane < LANES // 2, left, sums_ref[e, 5].astype(F32)))
+    outs = jnp.concatenate(outs, axis=0).astype(BF16)
     both = jnp.concatenate([*parts, *(pltpu.roll(p, SUB // 2, 1) for p in parts)], axis=0).astype(BF16)
     terms = jnp.dot(both, outs, preferred_element_type=F32)
     halves = [
@@ -367,11 +397,10 @@
     down = lax.broadcasted_iota(jnp.int32, (span, head), 0)
     for i in range(moved_ref.shape[0]):
         m, c, h = i // 4, i // 2 % 2, i % 2
-        item = moved_ref[i].astype(F32)
         ref = (keys_ref, values_ref)[c]
         for j in range(MIG):
             start = j * span + m * page + h * SUB
-            ref[start : start + SUB, :] = item[j * SUB : (j + 1) * SUB]
+            ref[start : start + SUB, :] = moved_ref[_piece(i, moved_ref.shape[0]), j].astype(F32)
     for j in range(MIG):
         for c, ref in ((0, keys_ref), (1, values_ref)):
             block = ref[j * span : (j + 1) * span, :]
@@ -449,8 +478,8 @@
         lambda *refs: _pack_body(requests, *refs),
         "pack_leaving",
         [
-            _shape((replicas, 3 * SUB, LANES), BF16),
-            _shape((slots, features // 2), F32),
+            _shape((replicas, MIG + 1, SUB, LANES), BF16),
+            _shape((slots, features // 2), BF16),
             _shape((slots, features // 2), BF16),
         ],
         [_smem()] * 3 + [_hbm()] * 5,
@@ -467,7 +496,8 @@
         us=4,
         room=60,
     )
-    spread = lax.all_to_all(packed, "rep", split_axis=0, concat_axis=0, tiled=True)
+    turned = _turned(replicas, FIRST[0])
+    spread = lax.all_to_all(packed, "rep", split_axis=0, concat_axis=0, tiled=True, axis_index_groups=turned)
 
     def at(z, x, c):
         return (z * 4 + x) * 2 + c
@@ -497,6 +527,18 @@
         (anchor.reshape(replicas, requests), by_x[0]),
         us=1,
     )
+    onward = _call(
+        _select_body,
+        "select_pieces",
+        _shape((replicas, MIG + 3, SUB, LANES), BF16),
+        [_smem()] + [_vmem()] * 5,
+        _vmem(),
+        (index, spread, *came),
+        us=1.5,
+    )
+    turned = _turned(replicas, FIRST[1])
+    moved = lax.all_to_all(onward, "rep", split_axis=0, concat_axis=0, tiled=True, axis_index_groups=turned)
+
     base, which, taps, mix = _call(
         lambda *refs: _local_body(requests, *refs),
         "filter_local",
@@ -508,31 +550,21 @@
         ],
         [_smem()] * 2 + [_vmem()] * 5 + [_any()],
         [_vmem()] * 4,
-        (rep, anchor, window, conv_input, filter_taps, filter_bias.reshape(1, channels), mix_weight.T, index),
+        (rep, anchor, window, conv_input, filter_taps, filter_bias.reshape(1, channels), mix_weight.T, came[3]),
         us=1.5,
     )
-    onward = _call(
-        _select_body,
-        "select_pieces",
-        _shape((replicas, 3 * SUB + ROWS, LANES), BF16),
-        [_smem()] + [_vmem()] * 5 + [_any()],
-        _vmem(),
-        (index, spread, *came, which),
-        us=1.5,
-    )
-    moved = lax.all_to_all(onward, "rep", split_axis=0, concat_axis=0, tiled=True)
-
     sums, act = _call(
         _act_body,
         "filter_and_project",
-        [_shape((experts, requests, 4 * LANES), BF16), _shape((requests, channels), F32)],
+        [_shape((experts, 6, SUB, LANES), BF16), _shape((requests, channels), F32)],
         [_vmem()] * 5,
         [_vmem()] * 2,
         (moved, base, which, taps, mix),
         scratch=[pltpu.VMEM((SUB, channels), F32)],
         us=1.5,
     )
-    sums_all = lax.all_to_all(sums, "exp", split_axis=0, concat_axis=0, tiled=True)
+    turned = _turned(experts, FIRST[2])
+    sums_all = lax.all_to_all(sums, "exp", split_axis=0, concat_axis=0, tiled=True, axis_index_groups=turned)
 
     attended, pages_out = _call(
         lambda *refs: _attend_body(requests, *refs),

time: 107 us -> 95.9 us (0.90)
  blocking collectives: 36.7 us -> 0 us
  waiting for transfers between devices: 11.1 us -> 28 us
  starting transfers between devices: 43.5 us -> 52 us
    all_to_all x1 -> x0, blocking collectives: 36.7 us -> none  [per_device(): lax.all_to_all(onward, 'rep', split_axis=0, concat_axis=0, tiled=True)]
    all_to_all x2 -> x3, waiting for transfers between devices: 8.5 us -> 20.4 us  [the longest x1 15.9 us: per_device(): lax.all_to_all(onward, 'rep', split_axis=0, concat_axis=0, tiled=True, ax...]
    all_to_all x2 -> x3, starting transfers between devices: 29.9 us -> 40.4 us  [the longest x1 21.4 us: per_device(): lax.all_to_all(packed, 'rep', split_axis=0, concat_axis=0, tiled=True, ax...]
    ppermute x3, waiting for transfers between devices: 0.77 us -> 5.82 us  [per_device(): lax.ppermute(by_x[k], 'rep', [(at(z, x, c), at(z, (x + k) % 4, c)) for z,...]
    ppermute x3, starting transfers between devices: 11.3 us -> 9.28 us  [per_device(): lax.ppermute(by_x[k], 'rep', [(at(z, x, c), at(z, (x + k) % 4, c)) for z,...]
  transfers between devices with their start and end apart: 6 -> 7, of which waited for: 4 -> 5; matrix products, arithmetic and copies ran while one was open for 0% -> 0% of each run, Pallas kernels for 4% -> 4%
where the time goes in v5:
time: 95.9 us; the launch traced here: 95.3 us
  starting transfers between devices  52 us (54%)
  waiting for transfers between devices  28 us (29%)
  Pallas kernels  13.1 us (14%)
  local copies, waits for them, and re-layouts  1.21 us (1%)
  between operations  1.03 us (1%)
    all_to_all x1, starting transfers between devices, per_device(): lax.all_to_all(packed, 'rep', split_axis=0, concat_axis=0, tiled=True, ax...  21.4 us
    all_to_all x1, waiting for transfers between devices, per_device(): lax.all_to_all(onward, 'rep', split_axis=0, concat_axis=0, tiled=True, ax...  15.9 us
    pallas_call x9, Pallas kernels, _call(): pl.pallas_call(body, name=name, out_shape=out_shape, in_specs=ins, out_sp...  13.1 us
    all_to_all x1, starting transfers between devices, per_device(): lax.all_to_all(sums, 'exp', split_axis=0, concat_axis=0, tiled=True, axis...  10.5 us
    ppermute x3, starting transfers between devices, per_device(): lax.ppermute(by_x[k], 'rep', [(at(z, x, c), at(z, (x + k) % 4, c)) for z,...  9.28 us
    all_to_all x1, starting transfers between devices, per_device(): lax.all_to_all(onward, 'rep', split_axis=0, concat_axis=0, tiled=True, ax...  8.51 us
    ppermute x3, waiting for transfers between devices, per_device(): lax.ppermute(by_x[k], 'rep', [(at(z, x, c), at(z, (x + k) % 4, c)) for z,...  5.82 us
    all_to_all x1, waiting for transfers between devices, per_device(): lax.all_to_all(sums, 'exp', split_axis=0, concat_axis=0, tiled=True, axis...  4.57 us
  transfers between devices with their start and end apart: 7, of which 5 were waited for; matrix products, arithmetic and copies ran while one was open for 0% of the time, Pallas kernels for 4%

profile of v5, /device:TPU:1, one launch (start us, length us, event | category | flops | bytes accessed | tf_op | source)
XLA Modules:
  0.0 95.3 jit_solution(14076521052027568183)
XLA Ops:
  0.6 0.0 copy-start.6
  0.7 0.0 copy-start.3
  0.7 0.0 copy-start.5
  0.7 0.0 copy-start.10
  0.7 0.0 copy-start.12
  0.7 0.0 copy-start.15
  0.7 0.0 copy-start.9
  0.7 0.0 copy-start.11
  0.7 0.0 copy-start.13
  0.7 0.0 copy-start.14
  0.7 0.0 copy-start.16
  0.8 0.0 copy-start.4
  0.8 0.0 copy-start.7
  0.8 0.0 copy-start.8
  0.8 0.0 copy-start.17
  0.8 0.0 copy-start.18
  0.8 0.0 copy-start.19
  0.8 0.0 copy-start.20
  0.8 5.2 %pack_leaving.1 = (bf16[32,3,8,128]{3,2,1,0:T(8,128)(2,1)}, bf16[128,2048]{1,0:T(8,128)(2,1)}, bf16[128,2048]{1,0:T(8,128)(2,1)}) custom-call(s32[1]{0:T(128)} %bitcast.refs_0_, s32[512]{0:T(512)} %refs_1_.7, s32[8,16]{1,0:T(8,128)} %bitcast.12, bf16[48,1,2,16,128]{4,3,2,1,0:T(8,128)(2,1)} %refs_7_.4, bf16[3,16,512]{2,1,0:T(8,128)(2,1)} %bitcast.10, ...), custom_call_target="tpu_custom_call" | custom-call | bytes 14000000 | tf_op jit(solution)/shard_map/pack_leaving/pallas_call | solution.py:41
  6.0 0.0 copy-start.1
  6.0 0.0 copy-start
  6.0 21.4 %all-to-all-start = ((bf16[32,3,8,128]{3,2,1,0:T(8,128)(2,1)}), bf16[32,3,8,128]{3,2,1,0:T(8,128)(2,1)S(1)}, u32[]{:S(2)}, u32[]{:S(2)}) async-start(bf16[32,3,8,128]{3,2,1,0:T(8,128)(2,1)} %get-tuple-element.31), calls=%async_computation | async-start | bytes 393216 | tf_op jit(solution)/shard_map/all_to_all | solution.py:500
  27.4 2.3 %collective-permute-start = (bf16[128,2048]{1,0:T(8,128)(2,1)}, bf16[128,2048]{1,0:T(8,128)(2,1)S(1)}, u32[]{:S(2)}, u32[]{:S(2)}) collective-permute-start(bf16[128,2048]{1,0:T(8,128)(2,1)} %get-tuple-element.29), channel_id=1, source_target_pairs={{0,16},{16,0},{32,48},{48,32},{64,80},{80,64},{96,112},{112,96},{1... | collective-permute-start | bytes 1572872 | tf_op jit(solution)/shard_map/ppermute | solution.py:506
  29.7 1.7 %collective-permute-done.got_ref = bf16[128,2048]{1,0:T(8,128)(2,1)S(1)} collective-permute-done((bf16[128,2048]{1,0:T(8,128)(2,1)}, bf16[128,2048]{1,0:T(8,128)(2,1)S(1)}, u32[]{:S(2)}, u32[]{:S(2)}) %collective-permute-start) | collective-permute-done | bytes 524320 | tf_op jit(solution)/shard_map/ppermute | solution.py:506
  31.4 1.0 %copy-done.2 = bf16[128,2048]{1,0:T(8,128)(2,1)S(1)} copy-done((bf16[128,2048]{1,0:T(8,128)(2,1)S(1)}, bf16[128,2048]{1,0:T(8,128)(2,1)}, u32[]{:S(2)}) %copy-start.2) | copy-done | bytes 524312
  32.5 0.1 fold_cores.1
  32.6 4.3 %collective-permute-start.3 = (bf16[128,512]{1,0:T(8,128)(2,1)S(1)}, bf16[128,512]{1,0:T(8,128)(2,1)S(1)}, u32[]{:S(2)}, u32[]{:S(2)}) collective-permute-start(bf16[128,512]{1,0:T(8,128)(2,1)S(1)} %get-tuple-element.34), channel_id=1, source_target_pairs={{0,96},{16,112},{32,0},{48,16},{64,32},{80,48},{96,64},{112,80},{1... | collective-permute-start | bytes 393224 | tf_op jit(solution)/shard_map/ppermute | solution.py:518
  36.9 2.5 %collective-permute-start.1 = (bf16[128,512]{1,0:T(8,128)(2,1)S(1)}, bf16[128,512]{1,0:T(8,128)(2,1)S(1)}, u32[]{:S(2)}, u32[]{:S(2)}) collective-permute-start(bf16[128,512]{1,0:T(8,128)(2,1)S(1)} %get-tuple-element.32), channel_id=1, source_target_pairs={{0,64},{16,80},{32,96},{48,112},{64,0},{80,16},{96,32},{112,48},{1... | collective-permute-start | bytes 393224 | tf_op jit(solution)/shard_map/ppermute | solution.py:518
  39.4 2.5 %collective-permute-start.2 = (bf16[128,512]{1,0:T(8,128)(2,1)S(1)}, bf16[128,512]{1,0:T(8,128)(2,1)S(1)}, u32[]{:S(2)}, u32[]{:S(2)}) collective-permute-start(bf16[128,512]{1,0:T(8,128)(2,1)S(1)} %get-tuple-element.33), channel_id=1, source_target_pairs={{0,32},{16,48},{32,64},{48,80},{64,96},{80,112},{96,0},{112,16},{1... | collective-permute-start | bytes 393224 | tf_op jit(solution)/shard_map/ppermute | solution.py:518
  41.9 0.0 copy-done.6
  41.9 0.1 reshape.24.refs_0_
  42.0 0.2 route_pieces.1.index_ref
  42.2 0.0 collective-permute-done.3.e3.refs_7_
  42.2 2.5 %collective-permute-done.1.e1 = bf16[128,512]{1,0:T(8,128)(2,1)S(1)} collective-permute-done((bf16[128,512]{1,0:T(8,128)(2,1)S(1)}, bf16[128,512]{1,0:T(8,128)(2,1)S(1)}, u32[]{:S(2)}, u32[]{:S(2)}) %collective-permute-start.1) | collective-permute-done | bytes 131104 | tf_op jit(solution)/shard_map/ppermute | solution.py:518
  44.7 3.3 %collective-permute-done.2.e2 = bf16[128,512]{1,0:T(8,128)(2,1)S(1)} collective-permute-done((bf16[128,512]{1,0:T(8,128)(2,1)S(1)}, bf16[128,512]{1,0:T(8,128)(2,1)S(1)}, u32[]{:S(2)}, u32[]{:S(2)}) %collective-permute-start.2) | collective-permute-done | bytes 131104 | tf_op jit(solution)/shard_map/ppermute | solution.py:518
  48.0 0.0 all-to-all-done.in_ref
  48.0 2.0 %select_pieces.1 = bf16[32,5,8,128]{3,2,1,0:T(8,128)(2,1)} custom-call(s32[32,128]{1,0:T(8,128)S(1)} %route_pieces.1.index_ref, bf16[32,3,8,128]{3,2,1,0:T(8,128)(2,1)S(1)} %all-to-all-done.in_ref, f32[128,512]{1,0:T(8,128)S(1)} %get-tuple-element.30.refs_1_.e0, bf16[128,512]{1,0:T(8,128)(2,1)S(1)} %collective-permute-done.1.e1, ...), custom_call_target="tpu_custom_call" | custom-call | bytes 5250000 | tf_op jit(solution)/shard_map/select_pieces/pallas_call | solution.py:41
  50.1 8.5 %all-to-all-start.1 = ((bf16[32,5,8,128]{3,2,1,0:T(8,128)(2,1)}), bf16[32,5,8,128]{3,2,1,0:T(8,128)(2,1)S(1)}, u32[]{:S(2)}, u32[]{:S(2)}) async-start(bf16[32,5,8,128]{3,2,1,0:T(8,128)(2,1)} %select_pieces.1), calls=%async_computation.1 | async-start | bytes 655360 | tf_op jit(solution)/shard_map/all_to_all | solution.py:540
  58.6 0.0 copy-done.3
  58.6 0.0 copy-done.5
  58.6 0.0 copy-done.10
  58.6 0.0 copy-done.12
  58.6 0.0 copy-done.15
  58.6 0.8 filter_local.1
  59.4 15.9 %all-to-all-done.1.moved_ref.refs_8_.refs_4_ = bf16[32,5,8,128]{3,2,1,0:T(8,128)(2,1)S(1)} async-done(((bf16[32,5,8,128]{3,2,1,0:T(8,128)(2,1)}), bf16[32,5,8,128]{3,2,1,0:T(8,128)(2,1)S(1)}, u32[]{:S(2)}, u32[]{:S(2)}) %all-to-all-start.1) | async-done | bytes 327712 | tf_op jit(solution)/shard_map/all_to_all | solution.py:540
  75.3 1.0 %filter_and_project.1 = (bf16[16,6,8,128]{3,2,1,0:T(8,128)(2,1)}, f32[16,512]{1,0:T(8,128)S(1)}) custom-call(bf16[32,5,8,128]{3,2,1,0:T(8,128)(2,1)S(1)} %all-to-all-done.1.moved_ref.refs_8_.refs_4_, f32[16,512]{1,0:T(8,128)S(1)} %get-tuple-element.35.base_ref, f32[16,128]{1,0:T(8,128)S(1)} %get-tuple-element.36.which_ref, ...), custom_call_target="tpu_custom_call" | custom-call | bytes 5250000 | tf_op jit(solution)/shard_map/filter_and_project/pallas_call | solution.py:41
  76.3 10.5 %all-to-all-start.2 = ((bf16[16,6,8,128]{3,2,1,0:T(8,128)(2,1)}), bf16[16,6,8,128]{3,2,1,0:T(8,128)(2,1)S(1)}, u32[]{:S(2)}, u32[]{:S(2)}) async-start(bf16[16,6,8,128]{3,2,1,0:T(8,128)(2,1)} %get-tuple-element.42), calls=%async_computation.2 | async-start | bytes 393216 | tf_op jit(solution)/shard_map/all_to_all | solution.py:567
  86.8 0.0 copy-done.9
  86.8 0.0 copy-done.11
  86.8 0.0 copy-done.13
  86.8 0.0 copy-done.14
  86.8 0.0 copy-done.16
  86.8 0.0 copy-done.1
  86.8 1.9 %attend.1 = (bf16[16,512]{1,0:T(8,128)(2,1)}, bf16[2,1,2,128,128]{4,3,2,1,0:T(8,128)(2,1)}) custom-call(s32[1]{0:T(128)} %bitcast.refs_0_, s32[512]{0:T(512)S(1)} %copy-done.6, s32[512]{0:T(512)S(1)} %copy-done.16, s32[8,16]{1,0:T(8,128)S(1)} %bitcast.13, bf16[16,512]{1,0:T(8,128)(2,1)S(1)} %copy-done.11, bf16[16,128]{1,0:T(8,128)(2,1)S(1)} %copy-done.13, ...), custom_call_target="tpu_custom_call" | custom-call | bytes 7000000 | tf_op jit(solution)/shard_map/attend/pallas_call | solution.py:41
  88.8 0.0 copy-done.4
  88.8 0.0 copy-done.7
  88.8 0.0 copy-done.8
  88.8 0.0 copy-done.17
  88.8 0.0 copy-done.18
  88.8 0.0 copy-done.19
  88.8 0.0 copy-done.20
  88.8 0.9 ready_state.1
  89.7 4.6 %all-to-all-done.2.refs_0_ = bf16[16,6,8,128]{3,2,1,0:T(8,128)(2,1)S(1)} async-done(((bf16[16,6,8,128]{3,2,1,0:T(8,128)(2,1)}), bf16[16,6,8,128]{3,2,1,0:T(8,128)(2,1)S(1)}, u32[]{:S(2)}, u32[]{:S(2)}) %all-to-all-start.2) | async-done | bytes 196640 | tf_op jit(solution)/shard_map/all_to_all | solution.py:567
  94.3 1.1 %update_state.1 = (bf16[16,512]{1,0:T(8,128)(2,1)}, bf16[16,256]{1,0:T(8,128)(2,1)}) custom-call(bf16[16,6,8,128]{3,2,1,0:T(8,128)(2,1)S(1)} %all-to-all-done.2.refs_0_, f32[16,512]{1,0:T(8,128)S(1)} %get-tuple-element.39.refs_9_.refs_5_.refs_1_, f32[16,16,512]{2,1,0:T(8,128)S(1)} %get-tuple-element.43.refs_2_, f32[16,512]{1,0:T(8,128)S(1)} %get-tuple-element.44.refs_3_, ...), custom_call_target="tpu_custom_call" | custom-call | bytes 7000000 | tf_op jit(solution)/shard_map/update_state/pallas_call | solution.py:41
  (2 shorter events, 0.0 us)
Async XLA Ops:
  0.6 41.3 %copy-start.6 = (s32[512]{0:T(512)S(1)}, s32[512]{0:T(512)}, u32[]{:S(2)}) copy-start(s32[512]{0:T(512)} %refs_1_.7) | copy-start | bytes 6148
  0.7 57.9 %copy-start.3 = (bf16[512,288]{0,1:T(8,128)(2,1)S(1)}, bf16[512,288]{0,1:T(8,128)(2,1)}, u32[]{:S(2)}) copy-start(bf16[512,288]{0,1:T(8,128)(2,1)} %param.35) | copy-start | bytes 884740
  0.7 57.9 %copy-start.5 = (bf16[16,3,512]{2,0,1:T(8,128)(2,1)S(1)}, bf16[16,3,512]{2,0,1:T(8,128)(2,1)}, u32[]{:S(2)}) copy-start(bf16[16,3,512]{2,0,1:T(8,128)(2,1)} %param.31) | copy-start | bytes 147460
  0.7 57.9 %copy-start.10 = (bf16[16,512]{1,0:T(8,128)(2,1)S(1)}, bf16[16,512]{1,0:T(8,128)(2,1)}, u32[]{:S(2)}) copy-start(bf16[16,512]{1,0:T(8,128)(2,1)} %refs_3_.3) | copy-start | bytes 49156
  0.7 57.9 %copy-start.12 = (f32[4,512]{1,0:T(4,128)S(1)}, f32[4,512]{1,0:T(4,128)}, u32[]{:S(2)}) copy-start(f32[4,512]{1,0:T(4,128)} %refs_4_.2) | copy-start | bytes 24580
  0.7 57.9 %copy-start.15 = (f32[512]{0:T(512)S(1)}, f32[512]{0:T(512)}, u32[]{:S(2)}) copy-start(f32[512]{0:T(512)} %param.34) | copy-start | bytes 6148
  0.7 86.1 %copy-start.9 = (s32[16,8]{0,1:T(8,128)S(1)}, s32[16,8]{0,1:T(8,128)}, u32[]{:S(2)}) copy-start(s32[16,8]{0,1:T(8,128)} %param.26) | copy-start | bytes 1540
  0.7 86.1 %copy-start.11 = (bf16[16,512]{1,0:T(8,128)(2,1)S(1)}, bf16[16,512]{1,0:T(8,128)(2,1)}, u32[]{:S(2)}) copy-start(bf16[16,512]{1,0:T(8,128)(2,1)} %refs_4_.3) | copy-start | bytes 49156
  0.7 86.1 %copy-start.13 = (bf16[16,128]{1,0:T(8,128)(2,1)S(1)}, bf16[16,128]{1,0:T(8,128)(2,1)}, u32[]{:S(2)}) copy-start(bf16[16,128]{1,0:T(8,128)(2,1)} %refs_5_.3) | copy-start | bytes 12292
  0.7 86.1 %copy-start.14 = (bf16[16,128]{1,0:T(8,128)(2,1)S(1)}, bf16[16,128]{1,0:T(8,128)(2,1)}, u32[]{:S(2)}) copy-start(bf16[16,128]{1,0:T(8,128)(2,1)} %refs_6_.4) | copy-start | bytes 12292
  0.7 86.1 %copy-start.16 = (s32[512]{0:T(512)S(1)}, s32[512]{0:T(512)}, u32[]{:S(2)}) copy-start(s32[512]{0:T(512)} %refs_2_.1) | copy-start | bytes 6148
  0.8 88.0 %copy-start.4 = (bf16[256,512]{1,0:T(8,128)(2,1)S(1)}, bf16[256,512]{1,0:T(8,128)(2,1)}, u32[]{:S(2)}) copy-start(bf16[256,512]{1,0:T(8,128)(2,1)} %refs_8_.1) | copy-start | bytes 786436
  0.8 88.0 %copy-start.7 = (f32[16,512]{1,0:T(8,128)S(1)}, f32[16,512]{1,0:T(8,128)}, u32[]{:S(2)}) copy-start(f32[16,512]{1,0:T(8,128)} %refs_10_.1) | copy-start | bytes 98308
  0.8 88.0 %copy-start.8 = (bf16[16,512]{1,0:T(8,128)(2,1)S(1)}, bf16[16,512]{1,0:T(8,128)(2,1)}, u32[]{:S(2)}) copy-start(bf16[16,512]{1,0:T(8,128)(2,1)} %refs_6_.5) | copy-start | bytes 49156
  0.8 88.0 %copy-start.17 = (f32[512]{0:T(512)S(1)}, f32[512]{0:T(512)}, u32[]{:S(2)}) copy-start(f32[512]{0:T(512)} %param.37) | copy-start | bytes 6148
  0.8 88.0 %copy-start.18 = (f32[512]{0:T(512)S(1)}, f32[512]{0:T(512)}, u32[]{:S(2)}) copy-start(f32[512]{0:T(512)} %param.39) | copy-start | bytes 6148
  0.8 88.0 %copy-start.19 = (s32[16,2]{0,1:T(2,128)S(1)}, s32[16,2]{0,1:T(2,128)}, u32[]{:S(2)}) copy-start(s32[16,2]{0,1:T(2,128)} %param.40) | copy-start | bytes 388
  0.8 88.0 %copy-start.20 = (f32[16,2]{0,1:T(2,128)S(1)}, f32[16,2]{0,1:T(2,128)}, u32[]{:S(2)}) copy-start(f32[16,2]{0,1:T(2,128)} %param.41) | copy-start | bytes 388
  6.0 80.8 %copy-start.1 = (bf16[48,1,2,16,128]{4,3,2,1,0:T(8,128)(2,1)S(1)}, bf16[48,1,2,16,128]{4,3,2,1,0:T(8,128)(2,1)}, u32[]{:S(2)}) copy-start(bf16[48,1,2,16,128]{4,3,2,1,0:T(8,128)(2,1)} %refs_7_.4) | copy-start | bytes 1179652
  6.0 82.8 %copy-start = (f32[16,16,512]{2,1,0:T(8,128)S(1)}, f32[16,16,512]{2,1,0:T(8,128)}, u32[]{:S(2)}) copy-start(f32[16,16,512]{2,1,0:T(8,128)} %refs_7_.5) | copy-start | bytes 1572868
  6.0 42.0 %all-to-all-start = ((bf16[32,3,8,128]{3,2,1,0:T(8,128)(2,1)}), bf16[32,3,8,128]{3,2,1,0:T(8,128)(2,1)S(1)}, u32[]{:S(2)}, u32[]{:S(2)}) async-start(bf16[32,3,8,128]{3,2,1,0:T(8,128)(2,1)} %get-tuple-element.31), calls=%async_computation | async-start | bytes 393216 | tf_op jit(solution)/shard_map/all_to_all | solution.py:500
  27.4 4.0 %collective-permute-start = (bf16[128,2048]{1,0:T(8,128)(2,1)}, bf16[128,2048]{1,0:T(8,128)(2,1)S(1)}, u32[]{:S(2)}, u32[]{:S(2)}) collective-permute-start(bf16[128,2048]{1,0:T(8,128)(2,1)} %get-tuple-element.29), channel_id=1, source_target_pairs={{0,16},{16,0},{32,48},{48,32},{64,80},{80,64},{96,112},{112,96},{1... | collective-permute-start | bytes 1572872 | tf_op jit(solution)/shard_map/ppermute | solution.py:506
  31.4 1.0 %copy-start.2 = (bf16[128,2048]{1,0:T(8,128)(2,1)S(1)}, bf16[128,2048]{1,0:T(8,128)(2,1)}, u32[]{:S(2)}) copy-start(bf16[128,2048]{1,0:T(8,128)(2,1)} %get-tuple-element.28.keep_ref) | copy-start | bytes 1572868
  32.6 9.6 %collective-permute-start.3 = (bf16[128,512]{1,0:T(8,128)(2,1)S(1)}, bf16[128,512]{1,0:T(8,128)(2,1)S(1)}, u32[]{:S(2)}, u32[]{:S(2)}) collective-permute-start(bf16[128,512]{1,0:T(8,128)(2,1)S(1)} %get-tuple-element.34), channel_id=1, source_target_pairs={{0,96},{16,112},{32,0},{48,16},{64,32},{80,48},{96,64},{112,80},{1... | collective-permute-start | bytes 393224 | tf_op jit(solution)/shard_map/ppermute | solution.py:518
  36.9 7.8 %collective-permute-start.1 = (bf16[128,512]{1,0:T(8,128)(2,1)S(1)}, bf16[128,512]{1,0:T(8,128)(2,1)S(1)}, u32[]{:S(2)}, u32[]{:S(2)}) collective-permute-start(bf16[128,512]{1,0:T(8,128)(2,1)S(1)} %get-tuple-element.32), channel_id=1, source_target_pairs={{0,64},{16,80},{32,96},{48,112},{64,0},{80,16},{96,32},{112,48},{1... | collective-permute-start | bytes 393224 | tf_op jit(solution)/shard_map/ppermute | solution.py:518
  39.4 8.7 %collective-permute-start.2 = (bf16[128,512]{1,0:T(8,128)(2,1)S(1)}, bf16[128,512]{1,0:T(8,128)(2,1)S(1)}, u32[]{:S(2)}, u32[]{:S(2)}) collective-permute-start(bf16[128,512]{1,0:T(8,128)(2,1)S(1)} %get-tuple-element.33), channel_id=1, source_target_pairs={{0,32},{16,48},{32,64},{48,80},{64,96},{80,112},{96,0},{112,16},{1... | collective-permute-start | bytes 393224 | tf_op jit(solution)/shard_map/ppermute | solution.py:518
  50.1 25.2 %all-to-all-start.1 = ((bf16[32,5,8,128]{3,2,1,0:T(8,128)(2,1)}), bf16[32,5,8,128]{3,2,1,0:T(8,128)(2,1)S(1)}, u32[]{:S(2)}, u32[]{:S(2)}) async-start(bf16[32,5,8,128]{3,2,1,0:T(8,128)(2,1)} %select_pieces.1), calls=%async_computation.1 | async-start | bytes 655360 | tf_op jit(solution)/shard_map/all_to_all | solution.py:540
  76.3 18.0 %all-to-all-start.2 = ((bf16[16,6,8,128]{3,2,1,0:T(8,128)(2,1)}), bf16[16,6,8,128]{3,2,1,0:T(8,128)(2,1)S(1)}, u32[]{:S(2)}, u32[]{:S(2)}) async-start(bf16[16,6,8,128]{3,2,1,0:T(8,128)(2,1)} %get-tuple-element.42), calls=%async_computation.2 | async-start | bytes 393216 | tf_op jit(solution)/shard_map/all_to_all | solution.py:567

commit v6 on v5

--- a/solution.py
+++ b/solution.py
@@ -12,7 +12,7 @@
 SUB = 8
 ROWS = 16
 PLANE = 8
-FIRST = (16, 8, 8)
+FIRST = (20, 4, 8)
 F32 = jnp.float32
 BF16 = jnp.bfloat16
 
@@ -184,7 +184,7 @@
     return (i + FIRST[0] - FIRST[1]) % replicas
 
 
-def _select_body(index_ref, in_ref, e0, e1, e2, e3, out_ref):
+def _select_body(index_ref, in_ref, e0, e1, e2, e3, dep_ref, out_ref):
     replicas = out_ref.shape[0]
     row = lax.broadcasted_iota(jnp.int32, (SUB, LANES), 0)
     half = SUB // MIG
@@ -527,18 +527,6 @@
         (anchor.reshape(replicas, requests), by_x[0]),
         us=1,
     )
-    onward = _call(
-        _select_body,
-        "select_pieces",
-        _shape((replicas, MIG + 3, SUB, LANES), BF16),
-        [_smem()] + [_vmem()] * 5,
-        _vmem(),
-        (index, spread, *came),
-        us=1.5,
-    )
-    turned = _turned(replicas, FIRST[1])
-    moved = lax.all_to_all(onward, "rep", split_axis=0, concat_axis=0, tiled=True, axis_index_groups=turned)
-
     base, which, taps, mix = _call(
         lambda *refs: _local_body(requests, *refs),
         "filter_local",
@@ -550,9 +538,21 @@
         ],
         [_smem()] * 2 + [_vmem()] * 5 + [_any()],
         [_vmem()] * 4,
-        (rep, anchor, window, conv_input, filter_taps, filter_bias.reshape(1, channels), mix_weight.T, came[3]),
+        (rep, anchor, window, conv_input, filter_taps, filter_bias.reshape(1, channels), mix_weight.T, index),
         us=1.5,
     )
+    onward = _call(
+        _select_body,
+        "select_pieces",
+        _shape((replicas, MIG + 3, SUB, LANES), BF16),
+        [_smem()] + [_vmem()] * 5 + [_any()],
+        _vmem(),
+        (index, spread, *came, which),
+        us=1.5,
+    )
+    turned = _turned(replicas, FIRST[1])
+    moved = lax.all_to_all(onward, "rep", split_axis=0, concat_axis=0, tiled=True, axis_index_groups=turned)
+
     sums, act = _call(
         _act_body,
         "filter_and_project",

time: 95.9 us -> 92.5 us (0.965)
  blocking collectives: 0 us -> 26.3 us
  waiting for transfers between devices: 28 us -> 6.74 us
  starting transfers between devices: 52 us -> 43.4 us
    all_to_all x0 -> x1, blocking collectives: none -> 26.3 us  [per_device(): lax.all_to_all(onward, 'rep', split_axis=0, concat_axis=0, tiled=True, ax...]
    all_to_all x1 -> x0, waiting for transfers between devices: 15.9 us -> none  [per_device(): lax.all_to_all(onward, 'rep', split_axis=0, concat_axis=0, tiled=True, ax...]
    all_to_all x1 -> x0, starting transfers between devices: 8.51 us -> none  [per_device(): lax.all_to_all(onward, 'rep', split_axis=0, concat_axis=0, tiled=True, ax...]
    ppermute x3, waiting for transfers between devices: 5.82 us -> 1.46 us  [per_device(): lax.ppermute(by_x[k], 'rep', [(at(z, x, c), at(z, (x + k) % 4, c)) for z,...]
    all_to_all x1, waiting for transfers between devices: 4.57 us -> 3.54 us  [per_device(): lax.all_to_all(sums, 'exp', split_axis=0, concat_axis=0, tiled=True, axis...]
  transfers between devices with their start and end apart: 7 -> 6, of which waited for: 5 -> 3; matrix products, arithmetic and copies ran while one was open for 0% -> 0% of each run, Pallas kernels for 4% -> 4%
where the time goes in v6:
time: 92.5 us; the launch traced here: 91.1 us
  starting transfers between devices  43.4 us (47%)
  blocking collectives  26.3 us (28%)
  Pallas kernels  12.4 us (13%)
  waiting for transfers between devices  6.74 us (7%)
  local copies, waits for them, and re-layouts  1.21 us (1%)
  between operations  1.03 us (1%)
    all_to_all x1, blocking collectives, per_device(): lax.all_to_all(onward, 'rep', split_axis=0, concat_axis=0, tiled=True, ax...  26.3 us
    all_to_all x1, starting transfers between devices, per_device(): lax.all_to_all(packed, 'rep', split_axis=0, concat_axis=0, tiled=True, ax...  22 us
    pallas_call x9, Pallas kernels, _call(): pl.pallas_call(body, name=name, out_shape=out_shape, in_specs=ins, out_sp...  12.4 us
    all_to_all x1, starting transfers between devices, per_device(): lax.all_to_all(sums, 'exp', split_axis=0, concat_axis=0, tiled=True, axis...  10.4 us
    ppermute x3, starting transfers between devices, per_device(): lax.ppermute(by_x[k], 'rep', [(at(z, x, c), at(z, (x + k) % 4, c)) for z,...  8.69 us
    all_to_all x1, waiting for transfers between devices, per_device(): lax.all_to_all(sums, 'exp', split_axis=0, concat_axis=0, tiled=True, axis...  3.54 us
    ppermute x1, starting transfers between devices, per_device(): lax.ppermute(send, 'rep', [(at(z, x, c), at(z, x, 1 - c)) for z, x, c in...  2.27 us
  transfers between devices with their start and end apart: 6, of which 3 were waited for; matrix products, arithmetic and copies ran while one was open for 0% of the time, Pallas kernels for 4%

profile of v6, /device:TPU:1, one launch (start us, length us, event | category | flops | bytes accessed | tf_op | source)
XLA Modules:
  0.0 91.1 jit_solution(8596508773735468073)
XLA Ops:
  0.6 0.0 copy-start.5
  0.6 0.0 copy-start.6
  0.7 0.0 copy-start.15
  0.7 0.0 copy-start.3
  0.7 0.0 copy-start.10
  0.7 0.0 copy-start.12
  0.7 0.0 copy-start.9
  0.7 0.0 copy-start.11
  0.7 0.0 copy-start.13
  0.7 0.0 copy-start.14
  0.7 0.0 copy-start.16
  0.8 0.0 copy-start.4
  0.8 0.0 copy-start.7
  0.8 0.0 copy-start.8
  0.8 0.0 copy-start.17
  0.8 0.0 copy-start.18
  0.8 0.0 copy-start.19
  0.8 0.0 copy-start.20
  0.8 5.2 %pack_leaving.1 = (bf16[32,3,8,128]{3,2,1,0:T(8,128)(2,1)}, bf16[128,2048]{1,0:T(8,128)(2,1)}, bf16[128,2048]{1,0:T(8,128)(2,1)}) custom-call(s32[1]{0:T(128)} %bitcast.refs_0_, s32[512]{0:T(512)} %refs_1_.7, s32[8,16]{1,0:T(8,128)} %bitcast.12, bf16[48,1,2,16,128]{4,3,2,1,0:T(8,128)(2,1)} %refs_7_.4, bf16[3,16,512]{2,1,0:T(8,128)(2,1)} %bitcast.10, ...), custom_call_target="tpu_custom_call" | custom-call | bytes 14000000 | tf_op jit(solution)/shard_map/pack_leaving/pallas_call | solution.py:41
  6.0 0.0 copy-start.1
  6.0 0.0 copy-start
  6.0 22.0 %all-to-all-start = ((bf16[32,3,8,128]{3,2,1,0:T(8,128)(2,1)}), bf16[32,3,8,128]{3,2,1,0:T(8,128)(2,1)S(1)}, u32[]{:S(2)}, u32[]{:S(2)}) async-start(bf16[32,3,8,128]{3,2,1,0:T(8,128)(2,1)} %get-tuple-element.31), calls=%async_computation | async-start | bytes 393216 | tf_op jit(solution)/shard_map/all_to_all | solution.py:500
  28.1 2.3 %collective-permute-start = (bf16[128,2048]{1,0:T(8,128)(2,1)}, bf16[128,2048]{1,0:T(8,128)(2,1)S(1)}, u32[]{:S(2)}, u32[]{:S(2)}) collective-permute-start(bf16[128,2048]{1,0:T(8,128)(2,1)} %get-tuple-element.29), channel_id=1, source_target_pairs={{0,16},{16,0},{32,48},{48,32},{64,80},{80,64},{96,112},{112,96},{1... | collective-permute-start | bytes 1572872 | tf_op jit(solution)/shard_map/ppermute | solution.py:506
  30.3 1.7 %collective-permute-done.got_ref = bf16[128,2048]{1,0:T(8,128)(2,1)S(1)} collective-permute-done((bf16[128,2048]{1,0:T(8,128)(2,1)}, bf16[128,2048]{1,0:T(8,128)(2,1)S(1)}, u32[]{:S(2)}, u32[]{:S(2)}) %collective-permute-start) | collective-permute-done | bytes 524320 | tf_op jit(solution)/shard_map/ppermute | solution.py:506
  32.1 1.0 %copy-done.2 = bf16[128,2048]{1,0:T(8,128)(2,1)S(1)} copy-done((bf16[128,2048]{1,0:T(8,128)(2,1)S(1)}, bf16[128,2048]{1,0:T(8,128)(2,1)}, u32[]{:S(2)}) %copy-start.2) | copy-done | bytes 524312
  33.1 0.1 fold_cores.1
  33.2 2.2 %collective-permute-start.1 = (bf16[128,512]{1,0:T(8,128)(2,1)S(1)}, bf16[128,512]{1,0:T(8,128)(2,1)S(1)}, u32[]{:S(2)}, u32[]{:S(2)}) collective-permute-start(bf16[128,512]{1,0:T(8,128)(2,1)S(1)} %get-tuple-element.32), channel_id=1, source_target_pairs={{0,64},{16,80},{32,96},{48,112},{64,0},{80,16},{96,32},{112,48},{1... | collective-permute-start | bytes 393224 | tf_op jit(solution)/shard_map/ppermute | solution.py:518
  35.4 2.5 %collective-permute-start.2 = (bf16[128,512]{1,0:T(8,128)(2,1)S(1)}, bf16[128,512]{1,0:T(8,128)(2,1)S(1)}, u32[]{:S(2)}, u32[]{:S(2)}) collective-permute-start(bf16[128,512]{1,0:T(8,128)(2,1)S(1)} %get-tuple-element.33), channel_id=1, source_target_pairs={{0,32},{16,48},{32,64},{48,80},{64,96},{80,112},{96,0},{112,16},{1... | collective-permute-start | bytes 393224 | tf_op jit(solution)/shard_map/ppermute | solution.py:518
  37.9 4.0 %collective-permute-start.3 = (bf16[128,512]{1,0:T(8,128)(2,1)S(1)}, bf16[128,512]{1,0:T(8,128)(2,1)S(1)}, u32[]{:S(2)}, u32[]{:S(2)}) collective-permute-start(bf16[128,512]{1,0:T(8,128)(2,1)S(1)} %get-tuple-element.34), channel_id=1, source_target_pairs={{0,96},{16,112},{32,0},{48,16},{64,32},{80,48},{96,64},{112,80},{1... | collective-permute-start | bytes 393224 | tf_op jit(solution)/shard_map/ppermute | solution.py:518
  41.9 0.0 copy-done.6
  41.9 0.1 reshape.24.refs_0_
  42.0 0.2 route_pieces.1.refs_7_.index_ref
  42.3 0.0 copy-done.5
  42.3 0.0 copy-done.15
  42.3 0.0 copy-done.3
  42.3 0.0 copy-done.10
  42.3 0.0 copy-done.12
  42.3 0.8 filter_local.1
  43.1 0.0 collective-permute-done.1.e1
  43.1 1.5 %collective-permute-done.2.e2 = bf16[128,512]{1,0:T(8,128)(2,1)S(1)} collective-permute-done((bf16[128,512]{1,0:T(8,128)(2,1)S(1)}, bf16[128,512]{1,0:T(8,128)(2,1)S(1)}, u32[]{:S(2)}, u32[]{:S(2)}) %collective-permute-start.2) | collective-permute-done | bytes 131104 | tf_op jit(solution)/shard_map/ppermute | solution.py:518
  44.6 0.0 collective-permute-done.3.e3
  44.6 0.0 all-to-all-done.in_ref
  44.6 1.3 %select_pieces.1 = bf16[32,5,8,128]{3,2,1,0:T(8,128)(2,1)S(1)} custom-call(s32[32,128]{1,0:T(8,128)S(1)} %route_pieces.1.refs_7_.index_ref, bf16[32,3,8,128]{3,2,1,0:T(8,128)(2,1)S(1)} %all-to-all-done.in_ref, f32[128,512]{1,0:T(8,128)S(1)} %get-tuple-element.30.refs_1_.e0, bf16[128,512]{1,0:T(8,128)(2,1)S(1)} %collective-permute-done.1.e1, ...), custom_call_target="tpu_custom_call" | custom-call | bytes 5250000 | tf_op jit(solution)/shard_map/select_pieces/pallas_call | solution.py:41
  45.9 26.3 %all_to_all.15.moved_ref.refs_8_.refs_4_ = bf16[32,5,8,128]{3,2,1,0:T(8,128)(2,1)S(1)} all-to-all(bf16[32,5,8,128]{3,2,1,0:T(8,128)(2,1)S(1)} %select_pieces.1), channel_id=1, replica_groups={{64,80,96,112,128,144,160,176,192,208,224,240,256,272,288,304,320,336,3..., dimensions={0} | all-to-all | bytes 655360 | tf_op jit(solution)/shard_map/all_to_all | solution.py:554
  72.2 1.0 %filter_and_project.1 = (bf16[16,6,8,128]{3,2,1,0:T(8,128)(2,1)}, f32[16,512]{1,0:T(8,128)S(1)}) custom-call(bf16[32,5,8,128]{3,2,1,0:T(8,128)(2,1)S(1)} %all_to_all.15.moved_ref.refs_8_.refs_4_, f32[16,512]{1,0:T(8,128)S(1)} %get-tuple-element.36.base_ref, f32[16,128]{1,0:T(8,128)S(1)} %get-tuple-element.35.dep_ref.which_ref, ...), custom_call_target="tpu_custom_call" | custom-call | bytes 5250000 | tf_op jit(solution)/shard_map/filter_and_project/pallas_call | solution.py:41
  73.2 10.4 %all-to-all-start.2 = ((bf16[16,6,8,128]{3,2,1,0:T(8,128)(2,1)}), bf16[16,6,8,128]{3,2,1,0:T(8,128)(2,1)S(1)}, u32[]{:S(2)}, u32[]{:S(2)}) async-start(bf16[16,6,8,128]{3,2,1,0:T(8,128)(2,1)} %get-tuple-element.42), calls=%async_computation.2 | async-start | bytes 393216 | tf_op jit(solution)/shard_map/all_to_all | solution.py:567
  83.6 0.0 copy-done.9
  83.6 0.0 copy-done.11
  83.6 0.0 copy-done.13
  83.6 0.0 copy-done.14
  83.6 0.0 copy-done.16
  83.6 0.0 copy-done.1
  83.6 1.9 %attend.1 = (bf16[16,512]{1,0:T(8,128)(2,1)}, bf16[2,1,2,128,128]{4,3,2,1,0:T(8,128)(2,1)}) custom-call(s32[1]{0:T(128)} %bitcast.refs_0_, s32[512]{0:T(512)S(1)} %copy-done.6, s32[512]{0:T(512)S(1)} %copy-done.16, s32[8,16]{1,0:T(8,128)S(1)} %bitcast.13, bf16[16,512]{1,0:T(8,128)(2,1)S(1)} %copy-done.11, bf16[16,128]{1,0:T(8,128)(2,1)S(1)} %copy-done.13, ...), custom_call_target="tpu_custom_call" | custom-call | bytes 7000000 | tf_op jit(solution)/shard_map/attend/pallas_call | solution.py:41
  85.5 0.0 copy-done.4
  85.5 0.0 copy-done.7
  85.5 0.0 copy-done.8
  85.6 0.0 copy-done.17
  85.6 0.0 copy-done.18
  85.6 0.0 copy-done.19
  85.6 0.0 copy-done.20
  85.6 0.0 copy-done
  85.6 0.9 ready_state.1
  86.5 3.5 %all-to-all-done.2.refs_0_ = bf16[16,6,8,128]{3,2,1,0:T(8,128)(2,1)S(1)} async-done(((bf16[16,6,8,128]{3,2,1,0:T(8,128)(2,1)}), bf16[16,6,8,128]{3,2,1,0:T(8,128)(2,1)S(1)}, u32[]{:S(2)}, u32[]{:S(2)}) %all-to-all-start.2) | async-done | bytes 196640 | tf_op jit(solution)/shard_map/all_to_all | solution.py:567
  90.0 1.1 %update_state.1 = (bf16[16,512]{1,0:T(8,128)(2,1)}, bf16[16,256]{1,0:T(8,128)(2,1)}) custom-call(bf16[16,6,8,128]{3,2,1,0:T(8,128)(2,1)S(1)} %all-to-all-done.2.refs_0_, f32[16,512]{1,0:T(8,128)S(1)} %get-tuple-element.39.refs_9_.refs_5_.refs_1_, f32[16,16,512]{2,1,0:T(8,128)S(1)} %get-tuple-element.43.refs_2_, f32[16,512]{1,0:T(8,128)S(1)} %get-tuple-element.44.refs_3_, ...), custom_call_target="tpu_custom_call" | custom-call | bytes 7000000 | tf_op jit(solution)/shard_map/update_state/pallas_call | solution.py:41
  (1 shorter events, 0.0 us)
Async XLA Ops:
  0.6 41.6 %copy-start.5 = (bf16[16,3,512]{2,0,1:T(8,128)(2,1)S(1)}, bf16[16,3,512]{2,0,1:T(8,128)(2,1)}, u32[]{:S(2)}) copy-start(bf16[16,3,512]{2,0,1:T(8,128)(2,1)} %param.31) | copy-start | bytes 147460
  0.6 41.3 %copy-start.6 = (s32[512]{0:T(512)S(1)}, s32[512]{0:T(512)}, u32[]{:S(2)}) copy-start(s32[512]{0:T(512)} %refs_1_.7) | copy-start | bytes 6148
  0.7 41.6 %copy-start.15 = (f32[512]{0:T(512)S(1)}, f32[512]{0:T(512)}, u32[]{:S(2)}) copy-start(f32[512]{0:T(512)} %param.34) | copy-start | bytes 6148
  0.7 41.6 %copy-start.3 = (bf16[512,288]{0,1:T(8,128)(2,1)S(1)}, bf16[512,288]{0,1:T(8,128)(2,1)}, u32[]{:S(2)}) copy-start(bf16[512,288]{0,1:T(8,128)(2,1)} %param.35) | copy-start | bytes 884740
  0.7 41.6 %copy-start.10 = (bf16[16,512]{1,0:T(8,128)(2,1)S(1)}, bf16[16,512]{1,0:T(8,128)(2,1)}, u32[]{:S(2)}) copy-start(bf16[16,512]{1,0:T(8,128)(2,1)} %refs_3_.3) | copy-start | bytes 49156
  0.7 41.6 %copy-start.12 = (f32[4,512]{1,0:T(4,128)S(1)}, f32[4,512]{1,0:T(4,128)}, u32[]{:S(2)}) copy-start(f32[4,512]{1,0:T(4,128)} %refs_4_.2) | copy-start | bytes 24580
  0.7 82.9 %copy-start.9 = (s32[16,8]{0,1:T(8,128)S(1)}, s32[16,8]{0,1:T(8,128)}, u32[]{:S(2)}) copy-start(s32[16,8]{0,1:T(8,128)} %param.26) | copy-start | bytes 1540
  0.7 82.8 %copy-start.11 = (bf16[16,512]{1,0:T(8,128)(2,1)S(1)}, bf16[16,512]{1,0:T(8,128)(2,1)}, u32[]{:S(2)}) copy-start(bf16[16,512]{1,0:T(8,128)(2,1)} %refs_4_.3) | copy-start | bytes 49156
  0.7 82.8 %copy-start.13 = (bf16[16,128]{1,0:T(8,128)(2,1)S(1)}, bf16[16,128]{1,0:T(8,128)(2,1)}, u32[]{:S(2)}) copy-start(bf16[16,128]{1,0:T(8,128)(2,1)} %refs_5_.3) | copy-start | bytes 12292
  0.7 82.8 %copy-start.14 = (bf16[16,128]{1,0:T(8,128)(2,1)S(1)}, bf16[16,128]{1,0:T(8,128)(2,1)}, u32[]{:S(2)}) copy-start(bf16[16,128]{1,0:T(8,128)(2,1)} %refs_6_.4) | copy-start | bytes 12292
  0.7 82.8 %copy-start.16 = (s32[512]{0:T(512)S(1)}, s32[512]{0:T(512)}, u32[]{:S(2)}) copy-start(s32[512]{0:T(512)} %refs_2_.1) | copy-start | bytes 6148
  0.8 84.8 %copy-start.4 = (bf16[256,512]{1,0:T(8,128)(2,1)S(1)}, bf16[256,512]{1,0:T(8,128)(2,1)}, u32[]{:S(2)}) copy-start(bf16[256,512]{1,0:T(8,128)(2,1)} %refs_8_.1) | copy-start | bytes 786436
  0.8 84.8 %copy-start.7 = (f32[16,512]{1,0:T(8,128)S(1)}, f32[16,512]{1,0:T(8,128)}, u32[]{:S(2)}) copy-start(f32[16,512]{1,0:T(8,128)} %refs_10_.1) | copy-start | bytes 98308
  0.8 84.8 %copy-start.8 = (bf16[16,512]{1,0:T(8,128)(2,1)S(1)}, bf16[16,512]{1,0:T(8,128)(2,1)}, u32[]{:S(2)}) copy-start(bf16[16,512]{1,0:T(8,128)(2,1)} %refs_6_.5) | copy-start | bytes 49156
  0.8 84.8 %copy-start.17 = (f32[512]{0:T(512)S(1)}, f32[512]{0:T(512)}, u32[]{:S(2)}) copy-start(f32[512]{0:T(512)} %param.37) | copy-start | bytes 6148
  0.8 84.8 %copy-start.18 = (f32[512]{0:T(512)S(1)}, f32[512]{0:T(512)}, u32[]{:S(2)}) copy-start(f32[512]{0:T(512)} %param.39) | copy-start | bytes 6148
  0.8 84.8 %copy-start.19 = (s32[16,2]{0,1:T(2,128)S(1)}, s32[16,2]{0,1:T(2,128)}, u32[]{:S(2)}) copy-start(s32[16,2]{0,1:T(2,128)} %param.40) | copy-start | bytes 388
  0.8 84.8 %copy-start.20 = (f32[16,2]{0,1:T(2,128)S(1)}, f32[16,2]{0,1:T(2,128)}, u32[]{:S(2)}) copy-start(f32[16,2]{0,1:T(2,128)} %param.41) | copy-start | bytes 388
  6.0 77.6 %copy-start.1 = (bf16[48,1,2,16,128]{4,3,2,1,0:T(8,128)(2,1)S(1)}, bf16[48,1,2,16,128]{4,3,2,1,0:T(8,128)(2,1)}, u32[]{:S(2)}) copy-start(bf16[48,1,2,16,128]{4,3,2,1,0:T(8,128)(2,1)} %refs_7_.4) | copy-start | bytes 1179652
  6.0 79.6 %copy-start = (f32[16,16,512]{2,1,0:T(8,128)S(1)}, f32[16,16,512]{2,1,0:T(8,128)}, u32[]{:S(2)}) copy-start(f32[16,16,512]{2,1,0:T(8,128)} %refs_7_.5) | copy-start | bytes 1572868
  6.0 38.5 %all-to-all-start = ((bf16[32,3,8,128]{3,2,1,0:T(8,128)(2,1)}), bf16[32,3,8,128]{3,2,1,0:T(8,128)(2,1)S(1)}, u32[]{:S(2)}, u32[]{:S(2)}) async-start(bf16[32,3,8,128]{3,2,1,0:T(8,128)(2,1)} %get-tuple-element.31), calls=%async_computation | async-start | bytes 393216 | tf_op jit(solution)/shard_map/all_to_all | solution.py:500
  28.1 4.0 %collective-permute-start = (bf16[128,2048]{1,0:T(8,128)(2,1)}, bf16[128,2048]{1,0:T(8,128)(2,1)S(1)}, u32[]{:S(2)}, u32[]{:S(2)}) collective-permute-start(bf16[128,2048]{1,0:T(8,128)(2,1)} %get-tuple-element.29), channel_id=1, source_target_pairs={{0,16},{16,0},{32,48},{48,32},{64,80},{80,64},{96,112},{112,96},{1... | collective-permute-start | bytes 1572872 | tf_op jit(solution)/shard_map/ppermute | solution.py:506
  32.1 1.0 %copy-start.2 = (bf16[128,2048]{1,0:T(8,128)(2,1)S(1)}, bf16[128,2048]{1,0:T(8,128)(2,1)}, u32[]{:S(2)}) copy-start(bf16[128,2048]{1,0:T(8,128)(2,1)} %get-tuple-element.28.keep_ref) | copy-start | bytes 1572868
  33.2 9.9 %collective-permute-start.1 = (bf16[128,512]{1,0:T(8,128)(2,1)S(1)}, bf16[128,512]{1,0:T(8,128)(2,1)S(1)}, u32[]{:S(2)}, u32[]{:S(2)}) collective-permute-start(bf16[128,512]{1,0:T(8,128)(2,1)S(1)} %get-tuple-element.32), channel_id=1, source_target_pairs={{0,64},{16,80},{32,96},{48,112},{64,0},{80,16},{96,32},{112,48},{1... | collective-permute-start | bytes 393224 | tf_op jit(solution)/shard_map/ppermute | solution.py:518
  35.4 9.1 %collective-permute-start.2 = (bf16[128,512]{1,0:T(8,128)(2,1)S(1)}, bf16[128,512]{1,0:T(8,128)(2,1)S(1)}, u32[]{:S(2)}, u32[]{:S(2)}) collective-permute-start(bf16[128,512]{1,0:T(8,128)(2,1)S(1)} %get-tuple-element.33), channel_id=1, source_target_pairs={{0,32},{16,48},{32,64},{48,80},{64,96},{80,112},{96,0},{112,16},{1... | collective-permute-start | bytes 393224 | tf_op jit(solution)/shard_map/ppermute | solution.py:518
  37.9 6.6 %collective-permute-start.3 = (bf16[128,512]{1,0:T(8,128)(2,1)S(1)}, bf16[128,512]{1,0:T(8,128)(2,1)S(1)}, u32[]{:S(2)}, u32[]{:S(2)}) collective-permute-start(bf16[128,512]{1,0:T(8,128)(2,1)S(1)} %get-tuple-element.34), channel_id=1, source_target_pairs={{0,96},{16,112},{32,0},{48,16},{64,32},{80,48},{96,64},{112,80},{1... | collective-permute-start | bytes 393224 | tf_op jit(solution)/shard_map/ppermute | solution.py:518
  73.2 16.9 %all-to-all-start.2 = ((bf16[16,6,8,128]{3,2,1,0:T(8,128)(2,1)}), bf16[16,6,8,128]{3,2,1,0:T(8,128)(2,1)S(1)}, u32[]{:S(2)}, u32[]{:S(2)}) async-start(bf16[16,6,8,128]{3,2,1,0:T(8,128)(2,1)} %get-tuple-element.42), calls=%async_computation.2 | async-start | bytes 393216 | tf_op jit(solution)/shard_map/all_to_all | solution.py:567

commit v7 on v6

--- a/solution.py
+++ b/solution.py
@@ -12,7 +12,7 @@
 SUB = 8
 ROWS = 16
 PLANE = 8
-FIRST = (20, 4, 8)
+FIRST = (20, 4, 10)
 F32 = jnp.float32
 BF16 = jnp.bfloat16
 

time: 92.5 us -> 90.9 us (0.983)
  waiting for transfers between devices: 6.74 us -> 4.16 us
  starting transfers between devices: 43.4 us -> 44.7 us
    all_to_all x1, waiting for transfers between devices: 3.54 us -> 0.96 us  [per_device(): lax.all_to_all(sums, 'exp', split_axis=0, concat_axis=0, tiled=True, axis...]
    all_to_all x1, starting transfers between devices: 10.4 us -> 11.8 us  [per_device(): lax.all_to_all(sums, 'exp', split_axis=0, concat_axis=0, tiled=True, axis...]
where the time goes in v7:
time: 90.9 us; the launch traced here: 89.9 us
  starting transfers between devices  44.7 us (49%)
  blocking collectives  26.3 us (29%)
  Pallas kernels  12.4 us (14%)
  waiting for transfers between devices  4.16 us (5%)
  local copies, waits for them, and re-layouts  1.21 us (1%)
  between operations  1.03 us (1%)
    all_to_all x1, blocking collectives, per_device(): lax.all_to_all(onward, 'rep', split_axis=0, concat_axis=0, tiled=True, ax...  26.3 us
    all_to_all x1, starting transfers between devices, per_device(): lax.all_to_all(packed, 'rep', split_axis=0, concat_axis=0, tiled=True, ax...  22 us
    pallas_call x9, Pallas kernels, _call(): pl.pallas_call(body, name=name, out_shape=out_shape, in_specs=ins, out_sp...  12.4 us
    all_to_all x1, starting transfers between devices, per_device(): lax.all_to_all(sums, 'exp', split_axis=0, concat_axis=0, tiled=True, axis...  11.8 us
    ppermute x3, starting transfers between devices, per_device(): lax.ppermute(by_x[k], 'rep', [(at(z, x, c), at(z, (x + k) % 4, c)) for z,...  8.69 us
    ppermute x1, starting transfers between devices, per_device(): lax.ppermute(send, 'rep', [(at(z, x, c), at(z, x, 1 - c)) for z, x, c in...  2.27 us
  transfers between devices with their start and end apart: 6, of which 3 were waited for; matrix products, arithmetic and copies ran while one was open for 0% of the time, Pallas kernels for 4%

profile of v7, /device:TPU:1, one launch (start us, length us, event | category | flops | bytes accessed | tf_op | source)
XLA Modules:
  0.0 89.9 jit_solution(3448193460632903098)
XLA Ops:
  0.6 0.0 copy-start.5
  0.6 0.0 copy-start.6
  0.7 0.0 copy-start.15
  0.7 0.0 copy-start.3
  0.7 0.0 copy-start.10
  0.7 0.0 copy-start.12
  0.7 0.0 copy-start.9
  0.7 0.0 copy-start.11
  0.7 0.0 copy-start.13
  0.7 0.0 copy-start.14
  0.7 0.0 copy-start.16
  0.8 0.0 copy-start.4
  0.8 0.0 copy-start.7
  0.8 0.0 copy-start.8
  0.8 0.0 copy-start.17
  0.8 0.0 copy-start.18
  0.8 0.0 copy-start.19
  0.8 0.0 copy-start.20
  0.8 5.2 %pack_leaving.1 = (bf16[32,3,8,128]{3,2,1,0:T(8,128)(2,1)}, bf16[128,2048]{1,0:T(8,128)(2,1)}, bf16[128,2048]{1,0:T(8,128)(2,1)}) custom-call(s32[1]{0:T(128)} %bitcast.refs_0_, s32[512]{0:T(512)} %refs_1_.7, s32[8,16]{1,0:T(8,128)} %bitcast.12, bf16[48,1,2,16,128]{4,3,2,1,0:T(8,128)(2,1)} %refs_7_.4, bf16[3,16,512]{2,1,0:T(8,128)(2,1)} %bitcast.10, ...), custom_call_target="tpu_custom_call" | custom-call | bytes 14000000 | tf_op jit(solution)/shard_map/pack_leaving/pallas_call | solution.py:41
  6.0 0.0 copy-start.1
  6.0 0.0 copy-start
  6.0 22.0 %all-to-all-start = ((bf16[32,3,8,128]{3,2,1,0:T(8,128)(2,1)}), bf16[32,3,8,128]{3,2,1,0:T(8,128)(2,1)S(1)}, u32[]{:S(2)}, u32[]{:S(2)}) async-start(bf16[32,3,8,128]{3,2,1,0:T(8,128)(2,1)} %get-tuple-element.31), calls=%async_computation | async-start | bytes 393216 | tf_op jit(solution)/shard_map/all_to_all | solution.py:500
  28.1 2.3 %collective-permute-start = (bf16[128,2048]{1,0:T(8,128)(2,1)}, bf16[128,2048]{1,0:T(8,128)(2,1)S(1)}, u32[]{:S(2)}, u32[]{:S(2)}) collective-permute-start(bf16[128,2048]{1,0:T(8,128)(2,1)} %get-tuple-element.29), channel_id=1, source_target_pairs={{0,16},{16,0},{32,48},{48,32},{64,80},{80,64},{96,112},{112,96},{1... | collective-permute-start | bytes 1572872 | tf_op jit(solution)/shard_map/ppermute | solution.py:506
  30.3 1.7 %collective-permute-done.got_ref = bf16[128,2048]{1,0:T(8,128)(2,1)S(1)} collective-permute-done((bf16[128,2048]{1,0:T(8,128)(2,1)}, bf16[128,2048]{1,0:T(8,128)(2,1)S(1)}, u32[]{:S(2)}, u32[]{:S(2)}) %collective-permute-start) | collective-permute-done | bytes 524320 | tf_op jit(solution)/shard_map/ppermute | solution.py:506
  32.1 1.0 %copy-done.2 = bf16[128,2048]{1,0:T(8,128)(2,1)S(1)} copy-done((bf16[128,2048]{1,0:T(8,128)(2,1)S(1)}, bf16[128,2048]{1,0:T(8,128)(2,1)}, u32[]{:S(2)}) %copy-start.2) | copy-done | bytes 524312
  33.1 0.1 fold_cores.1
  33.2 2.2 %collective-permute-start.1 = (bf16[128,512]{1,0:T(8,128)(2,1)S(1)}, bf16[128,512]{1,0:T(8,128)(2,1)S(1)}, u32[]{:S(2)}, u32[]{:S(2)}) collective-permute-start(bf16[128,512]{1,0:T(8,128)(2,1)S(1)} %get-tuple-element.32), channel_id=1, source_target_pairs={{0,64},{16,80},{32,96},{48,112},{64,0},{80,16},{96,32},{112,48},{1... | collective-permute-start | bytes 393224 | tf_op jit(solution)/shard_map/ppermute | solution.py:518
  35.4 2.5 %collective-permute-start.2 = (bf16[128,512]{1,0:T(8,128)(2,1)S(1)}, bf16[128,512]{1,0:T(8,128)(2,1)S(1)}, u32[]{:S(2)}, u32[]{:S(2)}) collective-permute-start(bf16[128,512]{1,0:T(8,128)(2,1)S(1)} %get-tuple-element.33), channel_id=1, source_target_pairs={{0,32},{16,48},{32,64},{48,80},{64,96},{80,112},{96,0},{112,16},{1... | collective-permute-start | bytes 393224 | tf_op jit(solution)/shard_map/ppermute | solution.py:518
  37.9 4.0 %collective-permute-start.3 = (bf16[128,512]{1,0:T(8,128)(2,1)S(1)}, bf16[128,512]{1,0:T(8,128)(2,1)S(1)}, u32[]{:S(2)}, u32[]{:S(2)}) collective-permute-start(bf16[128,512]{1,0:T(8,128)(2,1)S(1)} %get-tuple-element.34), channel_id=1, source_target_pairs={{0,96},{16,112},{32,0},{48,16},{64,32},{80,48},{96,64},{112,80},{1... | collective-permute-start | bytes 393224 | tf_op jit(solution)/shard_map/ppermute | solution.py:518
  41.9 0.0 copy-done.6
  41.9 0.1 reshape.24.refs_0_
  42.0 0.2 route_pieces.1.refs_7_.index_ref
  42.3 0.0 copy-done.5
  42.3 0.0 copy-done.15
  42.3 0.0 copy-done.3
  42.3 0.0 copy-done.10
  42.3 0.0 copy-done.12
  42.3 0.8 filter_local.1
  43.1 0.0 collective-permute-done.1.e1
  43.1 1.5 %collective-permute-done.2.e2 = bf16[128,512]{1,0:T(8,128)(2,1)S(1)} collective-permute-done((bf16[128,512]{1,0:T(8,128)(2,1)S(1)}, bf16[128,512]{1,0:T(8,128)(2,1)S(1)}, u32[]{:S(2)}, u32[]{:S(2)}) %collective-permute-start.2) | collective-permute-done | bytes 131104 | tf_op jit(solution)/shard_map/ppermute | solution.py:518
  44.6 0.0 collective-permute-done.3.e3
  44.6 0.0 all-to-all-done.in_ref
  44.6 1.3 %select_pieces.1 = bf16[32,5,8,128]{3,2,1,0:T(8,128)(2,1)S(1)} custom-call(s32[32,128]{1,0:T(8,128)S(1)} %route_pieces.1.refs_7_.index_ref, bf16[32,3,8,128]{3,2,1,0:T(8,128)(2,1)S(1)} %all-to-all-done.in_ref, f32[128,512]{1,0:T(8,128)S(1)} %get-tuple-element.30.refs_1_.e0, bf16[128,512]{1,0:T(8,128)(2,1)S(1)} %collective-permute-done.1.e1, ...), custom_call_target="tpu_custom_call" | custom-call | bytes 5250000 | tf_op jit(solution)/shard_map/select_pieces/pallas_call | solution.py:41
  45.9 26.3 %all_to_all.15.moved_ref.refs_8_.refs_4_ = bf16[32,5,8,128]{3,2,1,0:T(8,128)(2,1)S(1)} all-to-all(bf16[32,5,8,128]{3,2,1,0:T(8,128)(2,1)S(1)} %select_pieces.1), channel_id=1, replica_groups={{64,80,96,112,128,144,160,176,192,208,224,240,256,272,288,304,320,336,3..., dimensions={0} | all-to-all | bytes 655360 | tf_op jit(solution)/shard_map/all_to_all | solution.py:554
  72.2 1.0 %filter_and_project.1 = (bf16[16,6,8,128]{3,2,1,0:T(8,128)(2,1)}, f32[16,512]{1,0:T(8,128)S(1)}) custom-call(bf16[32,5,8,128]{3,2,1,0:T(8,128)(2,1)S(1)} %all_to_all.15.moved_ref.refs_8_.refs_4_, f32[16,512]{1,0:T(8,128)S(1)} %get-tuple-element.36.base_ref, f32[16,128]{1,0:T(8,128)S(1)} %get-tuple-element.35.dep_ref.which_ref, ...), custom_call_target="tpu_custom_call" | custom-call | bytes 5250000 | tf_op jit(solution)/shard_map/filter_and_project/pallas_call | solution.py:41
  73.2 11.8 %all-to-all-start.2 = ((bf16[16,6,8,128]{3,2,1,0:T(8,128)(2,1)}), bf16[16,6,8,128]{3,2,1,0:T(8,128)(2,1)S(1)}, u32[]{:S(2)}, u32[]{:S(2)}) async-start(bf16[16,6,8,128]{3,2,1,0:T(8,128)(2,1)} %get-tuple-element.42), calls=%async_computation.2 | async-start | bytes 393216 | tf_op jit(solution)/shard_map/all_to_all | solution.py:567
  84.9 0.0 copy-done.9
  84.9 0.0 copy-done.11
  85.0 0.0 copy-done.13
  85.0 0.0 copy-done.14
  85.0 0.0 copy-done.16
  85.0 0.0 copy-done.1
  85.0 1.9 %attend.1 = (bf16[16,512]{1,0:T(8,128)(2,1)}, bf16[2,1,2,128,128]{4,3,2,1,0:T(8,128)(2,1)}) custom-call(s32[1]{0:T(128)} %bitcast.refs_0_, s32[512]{0:T(512)S(1)} %copy-done.6, s32[512]{0:T(512)S(1)} %copy-done.16, s32[8,16]{1,0:T(8,128)S(1)} %bitcast.13, bf16[16,512]{1,0:T(8,128)(2,1)S(1)} %copy-done.11, bf16[16,128]{1,0:T(8,128)(2,1)S(1)} %copy-done.13, ...), custom_call_target="tpu_custom_call" | custom-call | bytes 7000000 | tf_op jit(solution)/shard_map/attend/pallas_call | solution.py:41
  86.9 0.0 copy-done.4
  86.9 0.0 copy-done.7
  86.9 0.0 copy-done.8
  86.9 0.0 copy-done.17
  86.9 0.0 copy-done.18
  87.0 0.0 copy-done.19
  87.0 0.0 copy-done.20
  87.0 0.0 copy-done
  87.0 0.9 ready_state.1
  87.9 1.0 %all-to-all-done.2.refs_0_ = bf16[16,6,8,128]{3,2,1,0:T(8,128)(2,1)S(1)} async-done(((bf16[16,6,8,128]{3,2,1,0:T(8,128)(2,1)}), bf16[16,6,8,128]{3,2,1,0:T(8,128)(2,1)S(1)}, u32[]{:S(2)}, u32[]{:S(2)}) %all-to-all-start.2) | async-done | bytes 196640 | tf_op jit(solution)/shard_map/all_to_all | solution.py:567
  88.8 1.1 %update_state.1 = (bf16[16,512]{1,0:T(8,128)(2,1)}, bf16[16,256]{1,0:T(8,128)(2,1)}) custom-call(bf16[16,6,8,128]{3,2,1,0:T(8,128)(2,1)S(1)} %all-to-all-done.2.refs_0_, f32[16,512]{1,0:T(8,128)S(1)} %get-tuple-element.39.refs_9_.refs_5_.refs_1_, f32[16,16,512]{2,1,0:T(8,128)S(1)} %get-tuple-element.43.refs_2_, f32[16,512]{1,0:T(8,128)S(1)} %get-tuple-element.44.refs_3_, ...), custom_call_target="tpu_custom_call" | custom-call | bytes 7000000 | tf_op jit(solution)/shard_map/update_state/pallas_call | solution.py:41
  (1 shorter events, 0.0 us)
Async XLA Ops:
  0.6 41.6 %copy-start.5 = (bf16[16,3,512]{2,0,1:T(8,128)(2,1)S(1)}, bf16[16,3,512]{2,0,1:T(8,128)(2,1)}, u32[]{:S(2)}) copy-start(bf16[16,3,512]{2,0,1:T(8,128)(2,1)} %param.31) | copy-start | bytes 147460
  0.6 41.3 %copy-start.6 = (s32[512]{0:T(512)S(1)}, s32[512]{0:T(512)}, u32[]{:S(2)}) copy-start(s32[512]{0:T(512)} %refs_1_.7) | copy-start | bytes 6148
  0.7 41.6 %copy-start.15 = (f32[512]{0:T(512)S(1)}, f32[512]{0:T(512)}, u32[]{:S(2)}) copy-start(f32[512]{0:T(512)} %param.34) | copy-start | bytes 6148
  0.7 41.6 %copy-start.3 = (bf16[512,288]{0,1:T(8,128)(2,1)S(1)}, bf16[512,288]{0,1:T(8,128)(2,1)}, u32[]{:S(2)}) copy-start(bf16[512,288]{0,1:T(8,128)(2,1)} %param.35) | copy-start | bytes 884740
  0.7 41.6 %copy-start.10 = (bf16[16,512]{1,0:T(8,128)(2,1)S(1)}, bf16[16,512]{1,0:T(8,128)(2,1)}, u32[]{:S(2)}) copy-start(bf16[16,512]{1,0:T(8,128)(2,1)} %refs_3_.3) | copy-start | bytes 49156
  0.7 41.6 %copy-start.12 = (f32[4,512]{1,0:T(4,128)S(1)}, f32[4,512]{1,0:T(4,128)}, u32[]{:S(2)}) copy-start(f32[4,512]{1,0:T(4,128)} %refs_4_.2) | copy-start | bytes 24580
  0.7 84.2 %copy-start.9 = (s32[16,8]{0,1:T(8,128)S(1)}, s32[16,8]{0,1:T(8,128)}, u32[]{:S(2)}) copy-start(s32[16,8]{0,1:T(8,128)} %param.26) | copy-start | bytes 1540
  0.7 84.2 %copy-start.11 = (bf16[16,512]{1,0:T(8,128)(2,1)S(1)}, bf16[16,512]{1,0:T(8,128)(2,1)}, u32[]{:S(2)}) copy-start(bf16[16,512]{1,0:T(8,128)(2,1)} %refs_4_.3) | copy-start | bytes 49156
  0.7 84.2 %copy-start.13 = (bf16[16,128]{1,0:T(8,128)(2,1)S(1)}, bf16[16,128]{1,0:T(8,128)(2,1)}, u32[]{:S(2)}) copy-start(bf16[16,128]{1,0:T(8,128)(2,1)} %refs_5_.3) | copy-start | bytes 12292
  0.7 84.2 %copy-start.14 = (bf16[16,128]{1,0:T(8,128)(2,1)S(1)}, bf16[16,128]{1,0:T(8,128)(2,1)}, u32[]{:S(2)}) copy-start(bf16[16,128]{1,0:T(8,128)(2,1)} %refs_6_.4) | copy-start | bytes 12292
  0.7 84.2 %copy-start.16 = (s32[512]{0:T(512)S(1)}, s32[512]{0:T(512)}, u32[]{:S(2)}) copy-start(s32[512]{0:T(512)} %refs_2_.1) | copy-start | bytes 6148
  0.8 86.2 %copy-start.4 = (bf16[256,512]{1,0:T(8,128)(2,1)S(1)}, bf16[256,512]{1,0:T(8,128)(2,1)}, u32[]{:S(2)}) copy-start(bf16[256,512]{1,0:T(8,128)(2,1)} %refs_8_.1) | copy-start | bytes 786436
  0.8 86.2 %copy-start.7 = (f32[16,512]{1,0:T(8,128)S(1)}, f32[16,512]{1,0:T(8,128)}, u32[]{:S(2)}) copy-start(f32[16,512]{1,0:T(8,128)} %refs_10_.1) | copy-start | bytes 98308
  0.8 86.2 %copy-start.8 = (bf16[16,512]{1,0:T(8,128)(2,1)S(1)}, bf16[16,512]{1,0:T(8,128)(2,1)}, u32[]{:S(2)}) copy-start(bf16[16,512]{1,0:T(8,128)(2,1)} %refs_6_.5) | copy-start | bytes 49156
  0.8 86.1 %copy-start.17 = (f32[512]{0:T(512)S(1)}, f32[512]{0:T(512)}, u32[]{:S(2)}) copy-start(f32[512]{0:T(512)} %param.37) | copy-start | bytes 6148
  0.8 86.1 %copy-start.18 = (f32[512]{0:T(512)S(1)}, f32[512]{0:T(512)}, u32[]{:S(2)}) copy-start(f32[512]{0:T(512)} %param.39) | copy-start | bytes 6148
  0.8 86.1 %copy-start.19 = (s32[16,2]{0,1:T(2,128)S(1)}, s32[16,2]{0,1:T(2,128)}, u32[]{:S(2)}) copy-start(s32[16,2]{0,1:T(2,128)} %param.40) | copy-start | bytes 388
  0.8 86.1 %copy-start.20 = (f32[16,2]{0,1:T(2,128)S(1)}, f32[16,2]{0,1:T(2,128)}, u32[]{:S(2)}) copy-start(f32[16,2]{0,1:T(2,128)} %param.41) | copy-start | bytes 388
  6.0 79.0 %copy-start.1 = (bf16[48,1,2,16,128]{4,3,2,1,0:T(8,128)(2,1)S(1)}, bf16[48,1,2,16,128]{4,3,2,1,0:T(8,128)(2,1)}, u32[]{:S(2)}) copy-start(bf16[48,1,2,16,128]{4,3,2,1,0:T(8,128)(2,1)} %refs_7_.4) | copy-start | bytes 1179652
  6.0 81.0 %copy-start = (f32[16,16,512]{2,1,0:T(8,128)S(1)}, f32[16,16,512]{2,1,0:T(8,128)}, u32[]{:S(2)}) copy-start(f32[16,16,512]{2,1,0:T(8,128)} %refs_7_.5) | copy-start | bytes 1572868
  6.0 38.5 %all-to-all-start = ((bf16[32,3,8,128]{3,2,1,0:T(8,128)(2,1)}), bf16[32,3,8,128]{3,2,1,0:T(8,128)(2,1)S(1)}, u32[]{:S(2)}, u32[]{:S(2)}) async-start(bf16[32,3,8,128]{3,2,1,0:T(8,128)(2,1)} %get-tuple-element.31), calls=%async_computation | async-start | bytes 393216 | tf_op jit(solution)/shard_map/all_to_all | solution.py:500
  28.1 4.0 %collective-permute-start = (bf16[128,2048]{1,0:T(8,128)(2,1)}, bf16[128,2048]{1,0:T(8,128)(2,1)S(1)}, u32[]{:S(2)}, u32[]{:S(2)}) collective-permute-start(bf16[128,2048]{1,0:T(8,128)(2,1)} %get-tuple-element.29), channel_id=1, source_target_pairs={{0,16},{16,0},{32,48},{48,32},{64,80},{80,64},{96,112},{112,96},{1... | collective-permute-start | bytes 1572872 | tf_op jit(solution)/shard_map/ppermute | solution.py:506
  32.1 1.0 %copy-start.2 = (bf16[128,2048]{1,0:T(8,128)(2,1)S(1)}, bf16[128,2048]{1,0:T(8,128)(2,1)}, u32[]{:S(2)}) copy-start(bf16[128,2048]{1,0:T(8,128)(2,1)} %get-tuple-element.28.keep_ref) | copy-start | bytes 1572868
  33.2 9.9 %collective-permute-start.1 = (bf16[128,512]{1,0:T(8,128)(2,1)S(1)}, bf16[128,512]{1,0:T(8,128)(2,1)S(1)}, u32[]{:S(2)}, u32[]{:S(2)}) collective-permute-start(bf16[128,512]{1,0:T(8,128)(2,1)S(1)} %get-tuple-element.32), channel_id=1, source_target_pairs={{0,64},{16,80},{32,96},{48,112},{64,0},{80,16},{96,32},{112,48},{1... | collective-permute-start | bytes 393224 | tf_op jit(solution)/shard_map/ppermute | solution.py:518
  35.4 9.1 %collective-permute-start.2 = (bf16[128,512]{1,0:T(8,128)(2,1)S(1)}, bf16[128,512]{1,0:T(8,128)(2,1)S(1)}, u32[]{:S(2)}, u32[]{:S(2)}) collective-permute-start(bf16[128,512]{1,0:T(8,128)(2,1)S(1)} %get-tuple-element.33), channel_id=1, source_target_pairs={{0,32},{16,48},{32,64},{48,80},{64,96},{80,112},{96,0},{112,16},{1... | collective-permute-start | bytes 393224 | tf_op jit(solution)/shard_map/ppermute | solution.py:518
  37.9 6.6 %collective-permute-start.3 = (bf16[128,512]{1,0:T(8,128)(2,1)S(1)}, bf16[128,512]{1,0:T(8,128)(2,1)S(1)}, u32[]{:S(2)}, u32[]{:S(2)}) collective-permute-start(bf16[128,512]{1,0:T(8,128)(2,1)S(1)} %get-tuple-element.34), channel_id=1, source_target_pairs={{0,96},{16,112},{32,0},{48,16},{64,32},{80,48},{96,64},{112,80},{1... | collective-permute-start | bytes 393224 | tf_op jit(solution)/shard_map/ppermute | solution.py:518
  73.2 15.7 %all-to-all-start.2 = ((bf16[16,6,8,128]{3,2,1,0:T(8,128)(2,1)}), bf16[16,6,8,128]{3,2,1,0:T(8,128)(2,1)S(1)}, u32[]{:S(2)}, u32[]{:S(2)}) async-start(bf16[16,6,8,128]{3,2,1,0:T(8,128)(2,1)} %get-tuple-element.42), calls=%async_computation.2 | async-start | bytes 393216 | tf_op jit(solution)/shard_map/all_to_all | solution.py:567

commit v8 on v7

--- a/solution.py
+++ b/solution.py
@@ -78,7 +78,7 @@
 
 def _pack_body(
     requests, rep_ref, anchor_ref, table_ref, pool_ref, window_ref, scan_ref, hidden_ref, weight_ref,
-    out_ref, keep_ref, send_ref, scans_ref, pages_ref, win_ref, rows_ref, blocks_ref, sems,
+    out_ref, mine_ref, keep_ref, send_ref, scans_ref, pages_ref, win_ref, rows_ref, blocks_ref, sems,
 ):
     pages = table_ref.shape[0]
     taps, _, channels = window_ref.shape
@@ -121,8 +121,10 @@
         weights[f].wait()
         total = jnp.dot(hidden, blocks_ref[f], preferred_element_type=F32)
         at = slice(p % 4 * width, (p % 4 + 1) * width)
-        if p < 4:
-            keep_ref[:, at] = total.astype(BF16)
+        if p == 0:
+            mine_ref[...] = total.astype(BF16)
+        elif p < 4:
+            keep_ref[:, (p - 1) * width : p * width] = total.astype(BF16)
         else:
             send_ref[:, at] = total.astype(BF16)
     for copy in copies:
@@ -173,24 +175,26 @@
     out_ref[...] = jnp.where(lane == 0, one, jnp.where(lane == 1, two, 0.0)).astype(jnp.int32)
 
 
-def _fold_body(keep_ref, got_ref, o0, o1, o2, o3):
-    width = o0.shape[1]
-    for k, o in enumerate((o0, o1, o2, o3)):
-        at = slice(k * width, (k + 1) * width)
-        o[...] = (keep_ref[:, at].astype(F32) + got_ref[:, at].astype(F32)).astype(o.dtype)
+def _fold_body(keep_ref, got_ref, o1, o2, o3):
+    width = o1.shape[1]
+    for k, o in enumerate((o1, o2, o3)):
+        mine = keep_ref[:, k * width : (k + 1) * width].astype(F32)
+        o[...] = (mine + got_ref[:, (k + 1) * width : (k + 2) * width].astype(F32)).astype(o.dtype)
 
 
 def _piece(i, replicas):
     return (i + FIRST[0] - FIRST[1]) % replicas
 
 
-def _select_body(index_ref, in_ref, e0, e1, e2, e3, dep_ref, out_ref):
+def _select_body(index_ref, in_ref, mine_ref, got_ref, e1, e2, e3, dep_ref, out_ref):
     replicas = out_ref.shape[0]
     row = lax.broadcasted_iota(jnp.int32, (SUB, LANES), 0)
     half = SUB // MIG
-    cap = e0.shape[0] // replicas
-    blocks = e0.shape[1] // LANES
-    total = (e0[...] + e1[...].astype(F32)) + (e2[...].astype(F32) + e3[...].astype(F32))
+    cap = e1.shape[0] // replicas
+    width = e1.shape[1]
+    blocks = width // LANES
+    total = mine_ref[...].astype(F32) + got_ref[:, :width].astype(F32)
+    total = (total + e1[...].astype(F32)) + (e2[...].astype(F32) + e3[...].astype(F32))
     for t in range(replicas):
         d = (t + FIRST[1]) % replicas
         tails = []
@@ -474,16 +478,17 @@
     table = block_table.T
     window = jnp.transpose(window_state, (1, 0, 2))
 
-    packed, keep, send = _call(
+    packed, mine, keep, send = _call(
         lambda *refs: _pack_body(requests, *refs),
         "pack_leaving",
         [
             _shape((replicas, MIG + 1, SUB, LANES), BF16),
-            _shape((slots, features // 2), BF16),
+            _shape((slots, features // PLANE), BF16),
+            _shape((slots, 3 * features // PLANE), BF16),
             _shape((slots, features // 2), BF16),
         ],
         [_smem()] * 3 + [_hbm()] * 5,
-        [_vmem()] * 3,
+        [_vmem()] * 4,
         (rep, anchor, table, page_pool, window, scan_state, expert_hidden, down_weight),
         scratch=[
             pltpu.VMEM((MIG, states, channels), F32),
@@ -508,14 +513,14 @@
     by_x = _call(
         _fold_body,
         "fold_cores",
-        [_shape((slots, width), F32)] + [_shape((slots, width), BF16)] * 3,
+        [_shape((slots, width), BF16)] * 3,
         [_vmem()] * 2,
-        [_vmem()] * 4,
+        [_vmem()] * 3,
         (keep, got),
         us=0.5,
     )
-    came = [by_x[0]] + [
-        lax.ppermute(by_x[k], "rep", [(at(z, x, c), at(z, (x + k) % 4, c)) for z, x, c in every]) for k in (2, 1, 3)
+    came = [
+        lax.ppermute(by_x[k - 1], "rep", [(at(z, x, c), at(z, (x + k) % 4, c)) for z, x, c in every]) for k in (2, 1, 3)
     ]
 
     index = _call(
@@ -545,9 +550,9 @@
         _select_body,
         "select_pieces",
         _shape((replicas, MIG + 3, SUB, LANES), BF16),
-        [_smem()] + [_vmem()] * 5 + [_any()],
+        [_smem()] + [_vmem()] * 6 + [_any()],
         _vmem(),
-        (index, spread, *came, which),
+        (index, spread, mine, got, *came, which),
         us=1.5,
     )
     turned = _turned(replicas, FIRST[1])

time: 90.9 us -> 92.7 us (1.020)
  waiting for transfers between devices: 4.16 us -> 6.52 us
    ppermute x3, waiting for transfers between devices: 1.46 us -> 3.82 us  [per_device(): lax.ppermute(by_x[k - 1], 'rep', [(at(z, x, c), at(z, (x + k) % 4, c)) fo...]
    unnamed x42 -> x44, local copies, waits for them, and re-layouts: 1.13 us -> 1.99 us
where the time goes in v8:
time: 92.7 us; the launch traced here: 91.7 us
  starting transfers between devices  43.9 us (47%)
  blocking collectives  25.8 us (28%)
  Pallas kernels  12.4 us (13%)
  waiting for transfers between devices  6.52 us (7%)
  local copies, waits for them, and re-layouts  2.07 us (2%)
  between operations  1.04 us (1%)
    all_to_all x1, blocking collectives, per_device(): lax.all_to_all(onward, 'rep', split_axis=0, concat_axis=0, tiled=True, ax...  25.8 us
    all_to_all x1, starting transfers between devices, per_device(): lax.all_to_all(packed, 'rep', split_axis=0, concat_axis=0, tiled=True, ax...  22 us
    pallas_call x9, Pallas kernels, _call(): pl.pallas_call(body, name=name, out_shape=out_shape, in_specs=ins, out_sp...  12.4 us
    all_to_all x1, starting transfers between devices, per_device(): lax.all_to_all(sums, 'exp', split_axis=0, concat_axis=0, tiled=True, axis...  11.8 us
    ppermute x3, starting transfers between devices, per_device(): lax.ppermute(by_x[k - 1], 'rep', [(at(z, x, c), at(z, (x + k) % 4, c)) fo...  7.81 us
    ppermute x3, waiting for transfers between devices, per_device(): lax.ppermute(by_x[k - 1], 'rep', [(at(z, x, c), at(z, (x + k) % 4, c)) fo...  3.82 us
    ppermute x1, starting transfers between devices, per_device(): lax.ppermute(send, 'rep', [(at(z, x, c), at(z, x, 1 - c)) for z, x, c in...  2.27 us
    unnamed x44, local copies, waits for them, and re-layouts  1.99 us
  transfers between devices with their start and end apart: 6, of which 3 were waited for; matrix products, arithmetic and copies ran while one was open for 0% of the time, Pallas kernels for 4%

profile of v8, /device:TPU:1, one launch (start us, length us, event | category | flops | bytes accessed | tf_op | source)
XLA Modules:
  0.0 91.7 jit_solution(13666794813682311947)
XLA Ops:
  0.6 0.0 copy-start.7
  0.6 0.0 copy-start.5
  0.7 0.0 copy-start.3
  0.7 0.0 copy-start.16
  0.7 0.0 copy-start.13
  0.7 0.0 copy-start.11
  0.7 0.0 copy-start.10
  0.7 0.0 copy-start.12
  0.7 0.0 copy-start.14
  0.7 0.0 copy-start.15
  0.7 0.0 copy-start.17
  0.8 0.0 copy-start.4
  0.8 0.0 copy-start.8
  0.8 0.0 copy-start.9
  0.8 0.0 copy-start.18
  0.8 0.0 copy-start.19
  0.8 0.0 copy-start.20
  0.8 0.0 copy-start.21
  0.8 5.1 %pack_leaving.1 = (bf16[32,3,8,128]{3,2,1,0:T(8,128)(2,1)}, bf16[128,512]{1,0:T(8,128)(2,1)}, bf16[128,1536]{1,0:T(8,128)(2,1)}, bf16[128,2048]{1,0:T(8,128)(2,1)}) custom-call(s32[1]{0:T(128)} %bitcast.refs_0_, s32[512]{0:T(512)} %refs_1_.7, s32[8,16]{1,0:T(8,128)} %bitcast.12, bf16[48,1,2,16,128]{4,3,2,1,0:T(8,128)(2,1)} %refs_7_.4, ...), custom_call_target="tpu_custom_call" | custom-call | bytes 14000000 | tf_op jit(solution)/shard_map/pack_leaving/pallas_call | solution.py:41
  6.0 0.0 copy-start.1
  6.0 0.0 copy-start
  6.0 22.0 %all-to-all-start = ((bf16[32,3,8,128]{3,2,1,0:T(8,128)(2,1)}), bf16[32,3,8,128]{3,2,1,0:T(8,128)(2,1)S(1)}, u32[]{:S(2)}, u32[]{:S(2)}) async-start(bf16[32,3,8,128]{3,2,1,0:T(8,128)(2,1)} %get-tuple-element.31), calls=%async_computation | async-start | bytes 393216 | tf_op jit(solution)/shard_map/all_to_all | solution.py:505
  28.0 2.3 %collective-permute-start = (bf16[128,2048]{1,0:T(8,128)(2,1)}, bf16[128,2048]{1,0:T(8,128)(2,1)S(1)}, u32[]{:S(2)}, u32[]{:S(2)}) collective-permute-start(bf16[128,2048]{1,0:T(8,128)(2,1)} %get-tuple-element.29), channel_id=1, source_target_pairs={{0,16},{16,0},{32,48},{48,32},{64,80},{80,64},{96,112},{112,96},{1... | collective-permute-start | bytes 1572872 | tf_op jit(solution)/shard_map/ppermute | solution.py:511
  30.3 1.7 %collective-permute-done.got_ref = bf16[128,2048]{1,0:T(8,128)(2,1)S(1)} collective-permute-done((bf16[128,2048]{1,0:T(8,128)(2,1)}, bf16[128,2048]{1,0:T(8,128)(2,1)S(1)}, u32[]{:S(2)}, u32[]{:S(2)}) %collective-permute-start) | collective-permute-done | bytes 524320 | tf_op jit(solution)/shard_map/ppermute | solution.py:511
  32.0 1.0 %copy-done.2 = bf16[128,1536]{1,0:T(8,128)(2,1)S(1)} copy-done((bf16[128,1536]{1,0:T(8,128)(2,1)S(1)}, bf16[128,1536]{1,0:T(8,128)(2,1)}, u32[]{:S(2)}) %copy-start.2) | copy-done | bytes 393240
  33.0 0.1 fold_cores.1
  33.1 2.2 %collective-permute-start.1 = (bf16[128,512]{1,0:T(8,128)(2,1)S(1)}, bf16[128,512]{1,0:T(8,128)(2,1)S(1)}, u32[]{:S(2)}, u32[]{:S(2)}) collective-permute-start(bf16[128,512]{1,0:T(8,128)(2,1)S(1)} %get-tuple-element.33), channel_id=1, source_target_pairs={{0,64},{16,80},{32,96},{48,112},{64,0},{80,16},{96,32},{112,48},{1... | collective-permute-start | bytes 393224 | tf_op jit(solution)/shard_map/ppermute | solution.py:523
  35.3 3.7 %collective-permute-start.3 = (bf16[128,512]{1,0:T(8,128)(2,1)S(1)}, bf16[128,512]{1,0:T(8,128)(2,1)S(1)}, u32[]{:S(2)}, u32[]{:S(2)}) collective-permute-start(bf16[128,512]{1,0:T(8,128)(2,1)S(1)} %get-tuple-element.34), channel_id=1, source_target_pairs={{0,96},{16,112},{32,0},{48,16},{64,32},{80,48},{96,64},{112,80},{1... | collective-permute-start | bytes 393224 | tf_op jit(solution)/shard_map/ppermute | solution.py:523
  39.0 1.9 %collective-permute-start.2 = (bf16[128,512]{1,0:T(8,128)(2,1)S(1)}, bf16[128,512]{1,0:T(8,128)(2,1)S(1)}, u32[]{:S(2)}, u32[]{:S(2)}) collective-permute-start(bf16[128,512]{1,0:T(8,128)(2,1)S(1)} %get-tuple-element.30.refs_1_), channel_id=1, source_target_pairs={{0,32},{16,48},{32,64},{48,80},{64,96},{80,112},{96,0},{112,16},{1... | collective-permute-start | bytes 393224 | tf_op jit(solution)/shard_map/ppermute | solution.py:523
  41.0 0.0 copy-done.7
  41.0 0.1 reshape.24.refs_0_
  41.0 0.2 route_pieces.1.refs_7_.index_ref
  41.3 0.0 copy-done.5
  41.3 0.0 copy-done.3
  41.3 0.0 copy-done.16
  41.3 0.0 copy-done.13
  41.3 0.0 copy-done.11
  41.3 0.8 filter_local.1
  42.1 0.0 collective-permute-done.1.e1
  42.1 0.0 collective-permute-done.3.e3
  42.1 3.8 %collective-permute-done.2.e2 = bf16[128,512]{1,0:T(8,128)(2,1)S(1)} collective-permute-done((bf16[128,512]{1,0:T(8,128)(2,1)S(1)}, bf16[128,512]{1,0:T(8,128)(2,1)S(1)}, u32[]{:S(2)}, u32[]{:S(2)}) %collective-permute-start.2) | collective-permute-done | bytes 131104 | tf_op jit(solution)/shard_map/ppermute | solution.py:523
  45.9 0.0 all-to-all-done.in_ref
  46.0 0.9 copy-done.6
  46.9 1.3 %select_pieces.1 = bf16[32,5,8,128]{3,2,1,0:T(8,128)(2,1)S(1)} custom-call(s32[32,128]{1,0:T(8,128)S(1)} %route_pieces.1.refs_7_.index_ref, bf16[32,3,8,128]{3,2,1,0:T(8,128)(2,1)S(1)} %all-to-all-done.in_ref, bf16[128,512]{1,0:T(8,128)(2,1)S(1)} %copy-done.6, bf16[128,2048]{1,0:T(8,128)(2,1)S(1)} %collective-permute-done.got_ref, ...), custom_call_target="tpu_custom_call" | custom-call | bytes 5250000 | tf_op jit(solution)/shard_map/select_pieces/pallas_call | solution.py:41
  48.2 25.8 %all_to_all.15.moved_ref.refs_8_.refs_4_ = bf16[32,5,8,128]{3,2,1,0:T(8,128)(2,1)S(1)} all-to-all(bf16[32,5,8,128]{3,2,1,0:T(8,128)(2,1)S(1)} %select_pieces.1), channel_id=1, replica_groups={{64,80,96,112,128,144,160,176,192,208,224,240,256,272,288,304,320,336,3..., dimensions={0} | all-to-all | bytes 655360 | tf_op jit(solution)/shard_map/all_to_all | solution.py:559
  74.0 1.0 %filter_and_project.1 = (bf16[16,6,8,128]{3,2,1,0:T(8,128)(2,1)}, f32[16,512]{1,0:T(8,128)S(1)}) custom-call(bf16[32,5,8,128]{3,2,1,0:T(8,128)(2,1)S(1)} %all_to_all.15.moved_ref.refs_8_.refs_4_, f32[16,512]{1,0:T(8,128)S(1)} %get-tuple-element.36.base_ref, f32[16,128]{1,0:T(8,128)S(1)} %get-tuple-element.35.dep_ref.which_ref, ...), custom_call_target="tpu_custom_call" | custom-call | bytes 5250000 | tf_op jit(solution)/shard_map/filter_and_project/pallas_call | solution.py:41
  75.0 11.8 %all-to-all-start.2 = ((bf16[16,6,8,128]{3,2,1,0:T(8,128)(2,1)}), bf16[16,6,8,128]{3,2,1,0:T(8,128)(2,1)S(1)}, u32[]{:S(2)}, u32[]{:S(2)}) async-start(bf16[16,6,8,128]{3,2,1,0:T(8,128)(2,1)} %get-tuple-element.42), calls=%async_computation.2 | async-start | bytes 393216 | tf_op jit(solution)/shard_map/all_to_all | solution.py:572
  86.7 0.0 copy-done.10
  86.7 0.0 copy-done.12
  86.8 0.0 copy-done.14
  86.8 0.0 copy-done.15
  86.8 0.0 copy-done.17
  86.8 0.0 copy-done.1
  86.8 1.9 %attend.1 = (bf16[16,512]{1,0:T(8,128)(2,1)}, bf16[2,1,2,128,128]{4,3,2,1,0:T(8,128)(2,1)}) custom-call(s32[1]{0:T(128)} %bitcast.refs_0_, s32[512]{0:T(512)S(1)} %copy-done.7, s32[512]{0:T(512)S(1)} %copy-done.17, s32[8,16]{1,0:T(8,128)S(1)} %bitcast.13, bf16[16,512]{1,0:T(8,128)(2,1)S(1)} %copy-done.12, bf16[16,128]{1,0:T(8,128)(2,1)S(1)} %copy-done.14, ...), custom_call_target="tpu_custom_call" | custom-call | bytes 7000000 | tf_op jit(solution)/shard_map/attend/pallas_call | solution.py:41
  88.7 0.0 copy-done.4
  88.7 0.0 copy-done.8
  88.7 0.0 copy-done.9
  88.7 0.0 copy-done.18
  88.7 0.0 copy-done.19
  88.8 0.0 copy-done.20
  88.8 0.0 copy-done.21
  88.8 0.9 ready_state.1
  89.7 1.0 %all-to-all-done.2.refs_0_ = bf16[16,6,8,128]{3,2,1,0:T(8,128)(2,1)S(1)} async-done(((bf16[16,6,8,128]{3,2,1,0:T(8,128)(2,1)}), bf16[16,6,8,128]{3,2,1,0:T(8,128)(2,1)S(1)}, u32[]{:S(2)}, u32[]{:S(2)}) %all-to-all-start.2) | async-done | bytes 196640 | tf_op jit(solution)/shard_map/all_to_all | solution.py:572
  90.6 1.1 %update_state.1 = (bf16[16,512]{1,0:T(8,128)(2,1)}, bf16[16,256]{1,0:T(8,128)(2,1)}) custom-call(bf16[16,6,8,128]{3,2,1,0:T(8,128)(2,1)S(1)} %all-to-all-done.2.refs_0_, f32[16,512]{1,0:T(8,128)S(1)} %get-tuple-element.39.refs_9_.refs_5_.refs_1_, f32[16,16,512]{2,1,0:T(8,128)S(1)} %get-tuple-element.43.refs_2_, f32[16,512]{1,0:T(8,128)S(1)} %get-tuple-element.44.refs_3_, ...), custom_call_target="tpu_custom_call" | custom-call | bytes 7000000 | tf_op jit(solution)/shard_map/update_state/pallas_call | solution.py:41
  (3 shorter events, 0.0 us)
Async XLA Ops:
  0.6 40.3 %copy-start.7 = (s32[512]{0:T(512)S(1)}, s32[512]{0:T(512)}, u32[]{:S(2)}) copy-start(s32[512]{0:T(512)} %refs_1_.7) | copy-start | bytes 6148
  0.6 40.6 %copy-start.5 = (bf16[16,3,512]{2,0,1:T(8,128)(2,1)S(1)}, bf16[16,3,512]{2,0,1:T(8,128)(2,1)}, u32[]{:S(2)}) copy-start(bf16[16,3,512]{2,0,1:T(8,128)(2,1)} %param.31) | copy-start | bytes 147460
  0.7 40.6 %copy-start.3 = (bf16[512,288]{0,1:T(8,128)(2,1)S(1)}, bf16[512,288]{0,1:T(8,128)(2,1)}, u32[]{:S(2)}) copy-start(bf16[512,288]{0,1:T(8,128)(2,1)} %param.35) | copy-start | bytes 884740
  0.7 40.6 %copy-start.16 = (f32[512]{0:T(512)S(1)}, f32[512]{0:T(512)}, u32[]{:S(2)}) copy-start(f32[512]{0:T(512)} %param.34) | copy-start | bytes 6148
  0.7 40.6 %copy-start.13 = (f32[4,512]{1,0:T(4,128)S(1)}, f32[4,512]{1,0:T(4,128)}, u32[]{:S(2)}) copy-start(f32[4,512]{1,0:T(4,128)} %refs_4_.2) | copy-start | bytes 24580
  0.7 40.6 %copy-start.11 = (bf16[16,512]{1,0:T(8,128)(2,1)S(1)}, bf16[16,512]{1,0:T(8,128)(2,1)}, u32[]{:S(2)}) copy-start(bf16[16,512]{1,0:T(8,128)(2,1)} %refs_3_.3) | copy-start | bytes 49156
  0.7 86.0 %copy-start.10 = (s32[16,8]{0,1:T(8,128)S(1)}, s32[16,8]{0,1:T(8,128)}, u32[]{:S(2)}) copy-start(s32[16,8]{0,1:T(8,128)} %param.26) | copy-start | bytes 1540
  0.7 86.0 %copy-start.12 = (bf16[16,512]{1,0:T(8,128)(2,1)S(1)}, bf16[16,512]{1,0:T(8,128)(2,1)}, u32[]{:S(2)}) copy-start(bf16[16,512]{1,0:T(8,128)(2,1)} %refs_4_.3) | copy-start | bytes 49156
  0.7 86.0 %copy-start.14 = (bf16[16,128]{1,0:T(8,128)(2,1)S(1)}, bf16[16,128]{1,0:T(8,128)(2,1)}, u32[]{:S(2)}) copy-start(bf16[16,128]{1,0:T(8,128)(2,1)} %refs_5_.3) | copy-start | bytes 12292
  0.7 86.0 %copy-start.15 = (bf16[16,128]{1,0:T(8,128)(2,1)S(1)}, bf16[16,128]{1,0:T(8,128)(2,1)}, u32[]{:S(2)}) copy-start(bf16[16,128]{1,0:T(8,128)(2,1)} %refs_6_.4) | copy-start | bytes 12292
  0.7 86.0 %copy-start.17 = (s32[512]{0:T(512)S(1)}, s32[512]{0:T(512)}, u32[]{:S(2)}) copy-start(s32[512]{0:T(512)} %refs_2_.1) | copy-start | bytes 6148
  0.8 88.0 %copy-start.4 = (bf16[256,512]{1,0:T(8,128)(2,1)S(1)}, bf16[256,512]{1,0:T(8,128)(2,1)}, u32[]{:S(2)}) copy-start(bf16[256,512]{1,0:T(8,128)(2,1)} %refs_8_.1) | copy-start | bytes 786436
  0.8 88.0 %copy-start.8 = (f32[16,512]{1,0:T(8,128)S(1)}, f32[16,512]{1,0:T(8,128)}, u32[]{:S(2)}) copy-start(f32[16,512]{1,0:T(8,128)} %refs_10_.1) | copy-start | bytes 98308
  0.8 88.0 %copy-start.9 = (bf16[16,512]{1,0:T(8,128)(2,1)S(1)}, bf16[16,512]{1,0:T(8,128)(2,1)}, u32[]{:S(2)}) copy-start(bf16[16,512]{1,0:T(8,128)(2,1)} %refs_6_.5) | copy-start | bytes 49156
  0.8 87.9 %copy-start.18 = (f32[512]{0:T(512)S(1)}, f32[512]{0:T(512)}, u32[]{:S(2)}) copy-start(f32[512]{0:T(512)} %param.37) | copy-start | bytes 6148
  0.8 87.9 %copy-start.19 = (f32[512]{0:T(512)S(1)}, f32[512]{0:T(512)}, u32[]{:S(2)}) copy-start(f32[512]{0:T(512)} %param.39) | copy-start | bytes 6148
  0.8 87.9 %copy-start.20 = (s32[16,2]{0,1:T(2,128)S(1)}, s32[16,2]{0,1:T(2,128)}, u32[]{:S(2)}) copy-start(s32[16,2]{0,1:T(2,128)} %param.40) | copy-start | bytes 388
  0.8 87.9 %copy-start.21 = (f32[16,2]{0,1:T(2,128)S(1)}, f32[16,2]{0,1:T(2,128)}, u32[]{:S(2)}) copy-start(f32[16,2]{0,1:T(2,128)} %param.41) | copy-start | bytes 388
  6.0 80.8 %copy-start.1 = (bf16[48,1,2,16,128]{4,3,2,1,0:T(8,128)(2,1)S(1)}, bf16[48,1,2,16,128]{4,3,2,1,0:T(8,128)(2,1)}, u32[]{:S(2)}) copy-start(bf16[48,1,2,16,128]{4,3,2,1,0:T(8,128)(2,1)} %refs_7_.4) | copy-start | bytes 1179652
  6.0 82.8 %copy-start = (f32[16,16,512]{2,1,0:T(8,128)S(1)}, f32[16,16,512]{2,1,0:T(8,128)}, u32[]{:S(2)}) copy-start(f32[16,16,512]{2,1,0:T(8,128)} %refs_7_.5) | copy-start | bytes 1572868
  6.0 40.0 %all-to-all-start = ((bf16[32,3,8,128]{3,2,1,0:T(8,128)(2,1)}), bf16[32,3,8,128]{3,2,1,0:T(8,128)(2,1)S(1)}, u32[]{:S(2)}, u32[]{:S(2)}) async-start(bf16[32,3,8,128]{3,2,1,0:T(8,128)(2,1)} %get-tuple-element.31), calls=%async_computation | async-start | bytes 393216 | tf_op jit(solution)/shard_map/all_to_all | solution.py:505
  28.0 4.0 %collective-permute-start = (bf16[128,2048]{1,0:T(8,128)(2,1)}, bf16[128,2048]{1,0:T(8,128)(2,1)S(1)}, u32[]{:S(2)}, u32[]{:S(2)}) collective-permute-start(bf16[128,2048]{1,0:T(8,128)(2,1)} %get-tuple-element.29), channel_id=1, source_target_pairs={{0,16},{16,0},{32,48},{48,32},{64,80},{80,64},{96,112},{112,96},{1... | collective-permute-start | bytes 1572872 | tf_op jit(solution)/shard_map/ppermute | solution.py:511
  32.0 1.0 %copy-start.2 = (bf16[128,1536]{1,0:T(8,128)(2,1)S(1)}, bf16[128,1536]{1,0:T(8,128)(2,1)}, u32[]{:S(2)}) copy-start(bf16[128,1536]{1,0:T(8,128)(2,1)} %get-tuple-element.28.keep_ref) | copy-start | bytes 1179652
  33.1 9.0 %collective-permute-start.1 = (bf16[128,512]{1,0:T(8,128)(2,1)S(1)}, bf16[128,512]{1,0:T(8,128)(2,1)S(1)}, u32[]{:S(2)}, u32[]{:S(2)}) collective-permute-start(bf16[128,512]{1,0:T(8,128)(2,1)S(1)} %get-tuple-element.33), channel_id=1, source_target_pairs={{0,64},{16,80},{32,96},{48,112},{64,0},{80,16},{96,32},{112,48},{1... | collective-permute-start | bytes 393224 | tf_op jit(solution)/shard_map/ppermute | solution.py:523
  35.3 6.8 %collective-permute-start.3 = (bf16[128,512]{1,0:T(8,128)(2,1)S(1)}, bf16[128,512]{1,0:T(8,128)(2,1)S(1)}, u32[]{:S(2)}, u32[]{:S(2)}) collective-permute-start(bf16[128,512]{1,0:T(8,128)(2,1)S(1)} %get-tuple-element.34), channel_id=1, source_target_pairs={{0,96},{16,112},{32,0},{48,16},{64,32},{80,48},{96,64},{112,80},{1... | collective-permute-start | bytes 393224 | tf_op jit(solution)/shard_map/ppermute | solution.py:523
  39.0 6.9 %collective-permute-start.2 = (bf16[128,512]{1,0:T(8,128)(2,1)S(1)}, bf16[128,512]{1,0:T(8,128)(2,1)S(1)}, u32[]{:S(2)}, u32[]{:S(2)}) collective-permute-start(bf16[128,512]{1,0:T(8,128)(2,1)S(1)} %get-tuple-element.30.refs_1_), channel_id=1, source_target_pairs={{0,32},{16,48},{32,64},{48,80},{64,96},{80,112},{96,0},{112,16},{1... | collective-permute-start | bytes 393224 | tf_op jit(solution)/shard_map/ppermute | solution.py:523
  46.0 0.9 copy-start.6
  75.0 15.7 %all-to-all-start.2 = ((bf16[16,6,8,128]{3,2,1,0:T(8,128)(2,1)}), bf16[16,6,8,128]{3,2,1,0:T(8,128)(2,1)S(1)}, u32[]{:S(2)}, u32[]{:S(2)}) async-start(bf16[16,6,8,128]{3,2,1,0:T(8,128)(2,1)} %get-tuple-element.42), calls=%async_computation.2 | async-start | bytes 393216 | tf_op jit(solution)/shard_map/all_to_all | solution.py:572
